TPU v7x, 32 devices: a whole 2x2x4 slice. The times are simulated.
32 devices in a mesh: dp: 8 (over z, y), expert: 4 (over x, core).
Axes of the slice: x: 2, y: 2, z: 4, core: 2. Of those that a mesh axis runs over, the one named last changes fastest.
Arguments:
- source: bfloat16 [8, 1024, 512], P('dp', 'expert'), may hold values from -6 to 6
- target: bfloat16 [8, 1024, 512], P('dp', 'expert'), may hold values from -6 to 6
- attention_in: bfloat16 [3, 512, 1536], replicated, may hold values from -0.25 to 0.25
- attention_out: bfloat16 [3, 512, 512], replicated, may hold values from -3 to 3
- norm_gains: float32 [6, 512], replicated, may hold values from 0.5 to 1.5
- encoder_up: bfloat16 [16, 2048, 512], P('expert'), may hold values from -0.25 to 0.25
- encoder_down: bfloat16 [16, 2048, 512], P('expert'), may hold values from -0.1875 to 0.1875
- decoder_up: bfloat16 [16, 2048, 512], P('expert'), may hold values from -0.25 to 0.25
- decoder_down: bfloat16 [16, 2048, 512], P('expert'), may hold values from -0.1875 to 0.1875
- encoder_route: int32 [2, 8, 1024], P(None, 'dp', 'expert'), may hold values from 0 to 15, as said below
- encoder_slot: int32 [2, 8, 1024], P(None, 'dp', 'expert'), may hold values from 0 to 31, as said below
- decoder_route: int32 [2, 8, 1024], P(None, 'dp', 'expert'), may hold values from 0 to 15, as said below
- decoder_slot: int32 [2, 8, 1024], P(None, 'dp', 'expert'), may hold values from 0 to 31, as said below
- output_grad: float32 [2, 8, 1024, 512], P(None, 'dp', 'expert'), may hold values from -6 to 6
Outputs:
- decoder_output: bfloat16 [2, 8, 1024, 512], P(None, 'dp', 'expert')
- source_grad: float32 [8, 1024, 512], P('dp', 'expert')
- target_grad: float32 [8, 1024, 512], P('dp', 'expert')
- attention_in_grad: float32 [3, 512, 1536], replicated
- attention_out_grad: float32 [3, 512, 512], replicated
- norm_gains_grad: float32 [6, 512], replicated
- encoder_up_grad: float32 [16, 2048, 512], P('expert', 'dp')
- encoder_down_grad: float32 [16, 2048, 512], P('expert', 'dp')
- decoder_up_grad: float32 [16, 2048, 512], P('expert', 'dp')
- decoder_down_grad: float32 [16, 2048, 512], P('expert', 'dp')
- expert_counts: int32 [2, 2, 16], replicated
Inputs may be any that keep to these rules, and one draw needn't show every extreme that they name: `encoder_route`: in each pass, among the tokens of one device (the 1 pairs of a dp index, the 256 positions of an expert index), no expert is named more than 32 times; in each pass one expert is named exactly 32 times by the tokens of every device. `encoder_slot`: in each pass, tokens of one device that name the same expert in encoder_route carry different slots. `decoder_route`: in each pass, among the tokens of one device (the 1 pairs of a dp index, the 256 positions of an expert index), no expert is named more than 32 times; in each pass one expert is named exactly 32 times by the tokens of every device. `decoder_slot`: in each pass, tokens of one device that name the same expert in decoder_route carry different slots.
All inputs are finite; a program needn't handle non-finite values.
Results may differ from a plain program's by a relative error of at most 0.024.
Values may be sent and summed in bfloat16 or wider, within the bound.
A program may use at most 256 MiB of HBM per device.

v0:
```python
import jax
import jax.numpy as jnp
from jax import lax
from jax.sharding import PartitionSpec as P

HEAD_DIM = 64
EXPERTS = 16


NORM_EPSILON = 1e-05
MASKED = -1e30


def layer_norm(values, gain):
    centered = values - jnp.mean(values, axis=-1, keepdims=True)
    spread = jnp.mean(centered * centered, axis=-1, keepdims=True)
    return centered * lax.rsqrt(spread + NORM_EPSILON) * gain


def activate(values):
    return jax.nn.gelu(values, approximate=True)


def split_heads(values):
    return values.reshape(values.shape[:-1] + (values.shape[-1] // HEAD_DIM, HEAD_DIM))


def join_heads(values):
    return values.reshape(values.shape[:-2] + (values.shape[-2] * values.shape[-1],))


def attention_scores(queries, key_rows, query_place, key_place, causal):
    scores = jnp.einsum(
        "bqhd,bkhd->bhqk", queries, key_rows, preferred_element_type=jnp.float32
    ) * HEAD_DIM ** (-0.5)
    if causal:
        scores = jnp.where(query_place[:, None] >= key_place[None, :], scores, MASKED)
    return scores


def core_forward(queries, key_rows, value_rows, query_place, key_place, causal):
    scores = attention_scores(queries, key_rows, query_place, key_place, causal)
    row_max = jnp.max(scores, axis=-1, keepdims=True)
    lifted = jnp.exp(scores - row_max)
    row_total = jnp.sum(lifted, axis=-1, keepdims=True)
    weights = (lifted / row_total).astype(jnp.bfloat16)
    blended = jnp.einsum("bhqk,bkhd->bqhd", weights, value_rows, preferred_element_type=jnp.float32)
    return (blended.astype(jnp.bfloat16), row_max + jnp.log(row_total))


def core_backward(
    queries, key_rows, value_rows, blended_grad, log_total, query_place, key_place, causal
):
    scores = attention_scores(queries, key_rows, query_place, key_place, causal)
    weights = jnp.exp(scores - log_total)
    values_grad = jnp.einsum(
        "bhqk,bqhd->bkhd",
        weights.astype(jnp.bfloat16),
        blended_grad,
        preferred_element_type=jnp.float32,
    )
    weights_grad = jnp.einsum(
        "bqhd,bkhd->bhqk", blended_grad, value_rows, preferred_element_type=jnp.float32
    )
    centre = jnp.sum(weights * weights_grad, axis=-1, keepdims=True)
    scores_grad = (weights * (weights_grad - centre)).astype(jnp.bfloat16)
    query_grad = jnp.einsum(
        "bhqk,bkhd->bqhd", scores_grad, key_rows, preferred_element_type=jnp.float32
    ) * HEAD_DIM ** (-0.5)
    keys_grad = jnp.einsum(
        "bhqk,bqhd->bkhd", scores_grad, queries, preferred_element_type=jnp.float32
    ) * HEAD_DIM ** (-0.5)
    return (query_grad, keys_grad, values_grad)


def local_places(seq_rows):
    return lax.axis_index("expert") * seq_rows + jnp.arange(seq_rows, dtype=jnp.int32)


def attend(queries, key_rows, value_rows, causal):
    gathered_keys, gathered_values = (
        lax.all_gather(key_rows, "expert", axis=1, tiled=True),
        lax.all_gather(value_rows, "expert", axis=1, tiled=True),
    )
    query_place = local_places(queries.shape[1])
    key_place = jnp.arange(gathered_keys.shape[1], dtype=jnp.int32)
    merged, log_total = core_forward(
        queries, gathered_keys, gathered_values, query_place, key_place, causal
    )
    retained = (queries, gathered_keys, gathered_values, log_total)
    return (merged, retained)


def attend_back(retained, blended_grad, causal):
    queries, gathered_keys, gathered_values, log_total = retained
    query_place = local_places(queries.shape[1])
    key_place = jnp.arange(gathered_keys.shape[1], dtype=jnp.int32)
    query_grad, keys_grad, values_grad = core_backward(
        queries,
        gathered_keys,
        gathered_values,
        blended_grad,
        log_total,
        query_place,
        key_place,
        causal,
    )
    keys_grad, values_grad = (
        lax.psum_scatter(
            keys_grad.astype(jnp.bfloat16), "expert", scatter_dimension=1, tiled=True
        ).astype(jnp.float32),
        lax.psum_scatter(
            values_grad.astype(jnp.bfloat16), "expert", scatter_dimension=1, tiled=True
        ).astype(jnp.float32),
    )
    query_grad = query_grad.astype(jnp.bfloat16)
    keys_grad = keys_grad.astype(jnp.bfloat16)
    values_grad = values_grad.astype(jnp.bfloat16)
    return (query_grad, keys_grad, values_grad)


def self_forward(residual, gain, inward, outward, causal):
    feature = residual.shape[-1]
    normed, norm_back = jax.vjp(layer_norm, residual, gain)
    normed = normed.astype(jnp.bfloat16)
    packed = jnp.einsum("brd,dk->brk", normed, inward, preferred_element_type=jnp.float32).astype(
        jnp.bfloat16
    )
    blended, retained = attend(
        split_heads(packed[..., :feature]),
        split_heads(packed[..., feature : 2 * feature]),
        split_heads(packed[..., 2 * feature :]),
        causal,
    )
    merged = join_heads(blended)
    branch = jnp.einsum("brd,de->bre", merged, outward, preferred_element_type=jnp.float32)
    return (residual + branch, (normed, norm_back, merged, retained))


def self_backward(stored, upstream, inward, outward, causal):
    normed, norm_back, merged, retained = stored
    branch_grad = upstream.astype(jnp.bfloat16)
    outward_grad = jnp.einsum(
        "brd,bre->de", merged, branch_grad, preferred_element_type=jnp.float32
    )
    merged_grad = jnp.einsum(
        "bre,de->brd", branch_grad, outward, preferred_element_type=jnp.float32
    ).astype(jnp.bfloat16)
    query_grad, keys_grad, values_grad = attend_back(retained, split_heads(merged_grad), causal)
    packed_grad = jnp.concatenate(
        [join_heads(query_grad), join_heads(keys_grad), join_heads(values_grad)], axis=-1
    )
    inward_grad = jnp.einsum("brd,brk->dk", normed, packed_grad, preferred_element_type=jnp.float32)
    normed_grad = jnp.einsum("brk,dk->brd", packed_grad, inward, preferred_element_type=jnp.float32)
    residual_grad, gain_grad = norm_back(normed_grad)
    return (upstream + residual_grad, gain_grad, inward_grad, outward_grad)


def cross_forward(decoder_mid, memory, gain, inward, outward):
    feature = decoder_mid.shape[-1]
    normed, norm_back = jax.vjp(layer_norm, decoder_mid, gain)
    normed = normed.astype(jnp.bfloat16)
    queries = jnp.einsum(
        "brd,dk->brk", normed, inward[:, :feature], preferred_element_type=jnp.float32
    ).astype(jnp.bfloat16)
    both_queries = jnp.broadcast_to(queries[None], (2,) + queries.shape).reshape(
        (-1,) + queries.shape[1:]
    )
    key_value = jnp.einsum(
        "pbrd,dk->pbrk", memory, inward[:, feature:], preferred_element_type=jnp.float32
    ).astype(jnp.bfloat16)
    key_value = key_value.reshape((-1,) + key_value.shape[2:])
    blended, retained = attend(
        split_heads(both_queries),
        split_heads(key_value[..., :feature]),
        split_heads(key_value[..., feature:]),
        False,
    )
    merged = join_heads(blended)
    branch = jnp.einsum("brd,de->bre", merged, outward, preferred_element_type=jnp.float32)
    return (
        decoder_mid[None] + branch.reshape((2,) + decoder_mid.shape),
        (normed, norm_back, memory, merged, retained),
    )


def cross_backward(stored, upstream, inward, outward):
    normed, norm_back, memory, merged, retained = stored
    feature = normed.shape[-1]
    branch_grad = upstream.reshape((-1,) + upstream.shape[2:]).astype(jnp.bfloat16)
    outward_grad = jnp.einsum(
        "brd,bre->de", merged, branch_grad, preferred_element_type=jnp.float32
    )
    merged_grad = jnp.einsum(
        "bre,de->brd", branch_grad, outward, preferred_element_type=jnp.float32
    ).astype(jnp.bfloat16)
    query_grad, keys_grad, values_grad = attend_back(retained, split_heads(merged_grad), False)
    query_grad = join_heads(query_grad).reshape(upstream.shape)
    pair_grad = jnp.concatenate([join_heads(keys_grad), join_heads(values_grad)], axis=-1)
    pair_grad = pair_grad.reshape(upstream.shape[:-1] + (2 * feature,))
    query_inward = jnp.einsum(
        "brd,pbrk->dk", normed, query_grad, preferred_element_type=jnp.float32
    )
    pair_inward = jnp.einsum("pbrd,pbrk->dk", memory, pair_grad, preferred_element_type=jnp.float32)
    normed_grad = jnp.einsum(
        "pbrk,dk->brd", query_grad, inward[:, :feature], preferred_element_type=jnp.float32
    )
    memory_grad = jnp.einsum(
        "pbrk,dk->pbrd", pair_grad, inward[:, feature:], preferred_element_type=jnp.float32
    )
    middle_grad, gain_grad = norm_back(normed_grad)
    inward_grad = jnp.concatenate([query_inward, pair_inward], axis=1)
    return (
        jnp.sum(upstream, axis=0) + middle_grad,
        memory_grad,
        gain_grad,
        inward_grad,
        outward_grad,
    )


def moe_forward(moe_rows, routes, slots, weight_up, weight_down):
    token_count, feature = (moe_rows.shape[1], moe_rows.shape[2])
    capacity = 2 * token_count // EXPERTS
    columns = routes * capacity + slots
    dispatch_table = (columns[..., None] == jnp.arange(EXPERTS * capacity, dtype=jnp.int32)).astype(
        jnp.bfloat16
    )
    outgoing = jnp.einsum(
        "pts,ptd->spd", dispatch_table, moe_rows, preferred_element_type=jnp.float32
    )
    outgoing = outgoing.astype(jnp.bfloat16).reshape(EXPERTS, 2 * capacity, feature)
    arrived = lax.all_to_all(outgoing, "expert", split_axis=0, concat_axis=1, tiled=True)
    hidden = jnp.einsum("emd,efd->emf", arrived, weight_up, preferred_element_type=jnp.float32)
    active = activate(hidden).astype(jnp.bfloat16)
    result = jnp.einsum(
        "emf,efd->emd", active, weight_down, preferred_element_type=jnp.float32
    ).astype(jnp.bfloat16)
    returned = lax.all_to_all(result, "expert", split_axis=1, concat_axis=0, tiled=True)
    blended = jnp.einsum(
        "pts,spd->ptd",
        dispatch_table,
        returned.reshape(EXPERTS * capacity, 2, feature),
        preferred_element_type=jnp.float32,
    )
    return (blended, (dispatch_table, arrived, hidden, active))


def moe_backward(retained, upstream, weight_up, weight_down):
    dispatch_table, arrived, hidden, active = retained
    feature = upstream.shape[-1]
    capacity = dispatch_table.shape[-1] // EXPERTS
    outgoing = jnp.einsum(
        "pts,ptd->spd",
        dispatch_table,
        upstream.astype(jnp.bfloat16),
        preferred_element_type=jnp.float32,
    )
    outgoing = outgoing.astype(jnp.bfloat16).reshape(EXPERTS, 2 * capacity, feature)
    result_grad = lax.all_to_all(outgoing, "expert", split_axis=0, concat_axis=1, tiled=True)
    down_grad = jnp.einsum("emf,emd->efd", active, result_grad, preferred_element_type=jnp.float32)
    active_grad = jnp.einsum(
        "emd,efd->emf", result_grad, weight_down, preferred_element_type=jnp.float32
    )
    smooth_back = jax.vjp(activate, hidden)[1]
    (hidden_grad,) = smooth_back(active_grad)
    hidden_grad = hidden_grad.astype(jnp.bfloat16)
    up_grad = jnp.einsum("emf,emd->efd", hidden_grad, arrived, preferred_element_type=jnp.float32)
    arrived_grad = jnp.einsum(
        "emf,efd->emd", hidden_grad, weight_up, preferred_element_type=jnp.float32
    ).astype(jnp.bfloat16)
    returned = lax.all_to_all(arrived_grad, "expert", split_axis=1, concat_axis=0, tiled=True)
    tokens_grad = jnp.einsum(
        "pts,spd->ptd",
        dispatch_table,
        returned.reshape(EXPERTS * capacity, 2, feature),
        preferred_element_type=jnp.float32,
    )
    return (tokens_grad, up_grad, down_grad)


def route_counts(routes):
    hits = (routes[..., None] == jnp.arange(EXPERTS, dtype=jnp.int32)).astype(jnp.float32)
    return jnp.sum(hits, axis=1)


def local(
    source,
    target,
    attention_in,
    attention_out,
    norm_gains,
    encoder_up,
    encoder_down,
    decoder_up,
    decoder_down,
    encoder_route,
    encoder_slot,
    decoder_route,
    decoder_slot,
    output_grad,
):
    pair_count, seq_rows, feature = source.shape
    token_count = pair_count * seq_rows
    encoder_routes = encoder_route.reshape(2, token_count)
    encoder_slots = encoder_slot.reshape(2, token_count)
    decoder_routes = decoder_route.reshape(2, token_count)
    decoder_slots = decoder_slot.reshape(2, token_count)
    encoder_attended, encoder_stored = self_forward(
        source.astype(jnp.float32), norm_gains[0], attention_in[0], attention_out[0], False
    )
    moe_input, input_back = jax.vjp(layer_norm, encoder_attended, norm_gains[1])
    moe_input = moe_input.astype(jnp.bfloat16)
    moe_input = jnp.broadcast_to(moe_input, (2, token_count, feature))
    encoder_mixed, encoder_kept = moe_forward(
        moe_input, encoder_routes, encoder_slots, encoder_up, encoder_down
    )
    encoder_final = encoder_attended + encoder_mixed
    memory, memory_back = jax.vjp(layer_norm, encoder_final, norm_gains[2])
    memory = memory.astype(jnp.bfloat16).reshape(2, pair_count, seq_rows, feature)
    decoder_attended, decoder_stored = self_forward(
        target.astype(jnp.float32), norm_gains[3], attention_in[1], attention_out[1], True
    )
    decoder_crossed, cross_stored = cross_forward(
        decoder_attended, memory, norm_gains[4], attention_in[2], attention_out[2]
    )
    moe_rows, rows_back = jax.vjp(layer_norm, decoder_crossed, norm_gains[5])
    moe_rows = moe_rows.astype(jnp.bfloat16).reshape(2, token_count, feature)
    decoder_mixed, decoder_kept = moe_forward(
        moe_rows, decoder_routes, decoder_slots, decoder_up, decoder_down
    )
    final = decoder_crossed + decoder_mixed.reshape(2, pair_count, seq_rows, feature)
    rows_grad, decoder_up_grad, decoder_down_grad = moe_backward(
        decoder_kept, output_grad.reshape(2, token_count, feature), decoder_up, decoder_down
    )
    crossed_part, gain_five = rows_back(rows_grad.reshape(2, pair_count, seq_rows, feature))
    crossed_grad = output_grad + crossed_part
    attended_grad, memory_grad, gain_four, cross_inward, cross_outward = cross_backward(
        cross_stored, crossed_grad, attention_in[2], attention_out[2]
    )
    target_grad, gain_three, decoder_inward, decoder_outward = self_backward(
        decoder_stored, attended_grad, attention_in[1], attention_out[1], True
    )
    final_grad, gain_two = memory_back(memory_grad.reshape(2, token_count, feature))
    input_grad, encoder_up_grad, encoder_down_grad = moe_backward(
        encoder_kept, final_grad, encoder_up, encoder_down
    )
    input_part, gain_one = input_back(
        jnp.sum(input_grad, axis=0).reshape(pair_count, seq_rows, feature)
    )
    encoder_grad = jnp.sum(final_grad, axis=0).reshape(pair_count, seq_rows, feature) + input_part
    source_grad, gain_zero, encoder_inward, encoder_outward = self_backward(
        encoder_stored, encoder_grad, attention_in[0], attention_out[0], False
    )
    counts = jnp.stack([route_counts(encoder_routes), route_counts(decoder_routes)])
    inward_grads = jnp.stack([encoder_inward, decoder_inward, cross_inward])
    outward_grads = jnp.stack([encoder_outward, decoder_outward, cross_outward])
    gain_grads = jnp.stack([gain_zero, gain_one, gain_two, gain_three, gain_four, gain_five])
    inward_grads, outward_grads, gain_grads, counts = lax.psum(
        (inward_grads, outward_grads, gain_grads, counts), ("dp", "expert")
    )
    encoder_up_grad, encoder_down_grad, decoder_up_grad, decoder_down_grad = (
        lax.psum_scatter(
            encoder_up_grad.astype(jnp.bfloat16), "dp", scatter_dimension=1, tiled=True
        ).astype(jnp.float32),
        lax.psum_scatter(
            encoder_down_grad.astype(jnp.bfloat16), "dp", scatter_dimension=1, tiled=True
        ).astype(jnp.float32),
        lax.psum_scatter(
            decoder_up_grad.astype(jnp.bfloat16), "dp", scatter_dimension=1, tiled=True
        ).astype(jnp.float32),
        lax.psum_scatter(
            decoder_down_grad.astype(jnp.bfloat16), "dp", scatter_dimension=1, tiled=True
        ).astype(jnp.float32),
    )
    return (
        final.astype(jnp.bfloat16),
        source_grad,
        target_grad,
        inward_grads,
        outward_grads,
        gain_grads,
        encoder_up_grad,
        encoder_down_grad,
        decoder_up_grad,
        decoder_down_grad,
        counts.astype(jnp.int32),
    )


def solution(mesh):
    in_specs = (
        P("dp", "expert", None),
        P("dp", "expert", None),
        P(),
        P(),
        P(),
        P("expert", None, None),
        P("expert", None, None),
        P("expert", None, None),
        P("expert", None, None),
        P(None, "dp", "expert"),
        P(None, "dp", "expert"),
        P(None, "dp", "expert"),
        P(None, "dp", "expert"),
        P(None, "dp", "expert", None),
    )
    out_specs = (
        P(None, "dp", "expert", None),
        P("dp", "expert", None),
        P("dp", "expert", None),
        P(),
        P(),
        P(),
        P("expert", "dp", None),
        P("expert", "dp", None),
        P("expert", "dp", None),
        P("expert", "dp", None),
        P(),
    )
    return jax.shard_map(local, mesh=mesh, in_specs=in_specs, out_specs=out_specs, check_vma=False)
```

profile of v0, /device:TPU:0, one launch (start us, length us, event | category | flops | bytes accessed | tf_op | source)
XLA Modules:
  0.0 1351.3 jit_solution(9468084146364427910)
XLA Ops:
  16.6 16.7 %all-gather.13.cloned.1.call-done = bf16[1,1024,8,64]{1,3,2,0:T(8,128)(2,1)} async-done(((bf16[1,256,8,64]{1,3,2,0:T(8,128)(2,1)}), bf16[1,1024,8,64]{1,3,2,0:T(8,128)(2,1)}) %all-gather.13.cloned.1.call-update) | async-done | bytes 1048592 | tf_op jit(solution)/shard_map/all_gather | solution.py:82
  41.1 11.2 all-gather.11.cloned.1.call-done
  70.5 10.4 all-to-all-done
  87.2 8.2 convolution_convert_fusion.9
  104.3 11.9 all-to-all-done.1
  148.1 8.6 all-gather.17.cloned.1.call-done
  170.5 11.0 all-gather.15.cloned.1.call-done
  181.6 8.5 fusion.71
  203.0 9.4 fusion.209
  217.5 12.4 fusion.17
  243.1 14.4 %all-to-all-done.5 = bf16[4,256,512]{2,0,1:T(4,128)(2,1)S(1)} async-done(((bf16[4,256,512]{2,0,1:T(4,128)(2,1)}), bf16[4,256,512]{2,0,1:T(4,128)(2,1)S(1)}, u32[]{:S(2)}, u32[]{:S(2)}) %all-to-all-start.5) | async-done | bytes 1048608 | tf_op jit(solution)/shard_map/all_to_all | solution.py:272
  267.5 9.4 convert_bitcast_fusion
  277.0 9.9 multiply_reduce_fusion
  286.9 8.0 multiply_convert_fusion
  301.2 6.8 fusion.70
  313.7 29.5 %reduce-scatter.11.cloned.1.call-done = bf16[2,256,8,64]{1,3,2,0:T(8,128)(2,1)} async-done(((bf16[2,1024,8,64]{1,3,2,0:T(8,128)(2,1)}), bf16[2,256,8,64]{1,3,2,0:T(8,128)(2,1)}) %reduce-scatter.11.cloned.1.call-update) | async-done | bytes 524304 | tf_op jit(solution)/shard_map/reduce_scatter | solution.py:109
  360.8 7.0 multiply_reduce_fusion.2
  369.0 10.7 fusion.10
  393.6 6.8 multiply_convert_fusion.1
  435.5 7.9 convolution_convert_fusion
  444.6 7.8 convolution_convert_fusion.1
  452.7 7.9 convolution_convert_fusion.2
  461.8 7.9 convolution_convert_fusion.3
  502.4 8.6 convolution_convert_fusion.8
  516.9 14.2 %all-to-all-done.3 = bf16[4,256,512]{2,0,1:T(4,128)(2,1)S(1)} async-done(((bf16[4,256,512]{2,0,1:T(4,128)(2,1)}), bf16[4,256,512]{2,0,1:T(4,128)(2,1)S(1)}, u32[]{:S(2)}, u32[]{:S(2)}) %all-to-all-start.3) | async-done | bytes 1048608 | tf_op jit(solution)/shard_map/all_to_all | solution.py:239
  542.7 41.9 %all-reduce = (f32[6,512]{1,0:T(8,128)}, f32[2,2,16]{2,1,0:T(2,128)S(1)}) all-reduce(f32[6,512]{1,0:T(8,128)S(1)} %stack.68, f32[2,2,16]{2,1,0:T(2,128)S(1)} %pad_maximum_fusion.5), channel_id=1, replica_groups=mesh['dp'=8,'expert'=4] {'dp','expert'}, use_global_device_ids=true, to_apply=%region_50.51 | all-reduce | flops 3136 | bytes 25088 | tf_op jit(solution)/shard_map/psum | solution.py:359
  587.2 53.7 %reduce-scatter.29.cloned.1.call-done = bf16[4,256,512]{2,1,0:T(8,128)(2,1)} async-done(((bf16[4,2048,512]{2,1,0:T(8,128)(2,1)}), bf16[4,256,512]{2,1,0:T(8,128)(2,1)}) %reduce-scatter.29.cloned.1.call-update) | async-done | bytes 1048592 | tf_op jit(solution)/shard_map/reduce_scatter | solution.py:372
  643.8 149.5 %reduce-scatter.27.cloned.1.call-done = bf16[4,256,512]{2,1,0:T(8,128)(2,1)} async-done(((bf16[4,2048,512]{2,1,0:T(8,128)(2,1)}), bf16[4,256,512]{2,1,0:T(8,128)(2,1)}) %reduce-scatter.27.cloned.1.call-update) | async-done | bytes 1048592 | tf_op jit(solution)/shard_map/reduce_scatter | solution.py:369
  796.1 149.1 %reduce-scatter.25.cloned.1.call-done = bf16[4,256,512]{2,1,0:T(8,128)(2,1)} async-done(((bf16[4,2048,512]{2,1,0:T(8,128)(2,1)}), bf16[4,256,512]{2,1,0:T(8,128)(2,1)}) %reduce-scatter.25.cloned.1.call-update) | async-done | bytes 1048592 | tf_op jit(solution)/shard_map/reduce_scatter | solution.py:366
  948.0 149.5 %reduce-scatter.23.cloned.1.call-done = bf16[4,256,512]{2,1,0:T(8,128)(2,1)} async-done(((bf16[4,2048,512]{2,1,0:T(8,128)(2,1)}), bf16[4,256,512]{2,1,0:T(8,128)(2,1)}) %reduce-scatter.23.cloned.1.call-update) | async-done | bytes 1048592 | tf_op jit(solution)/shard_map/reduce_scatter | solution.py:363
  1100.4 233.9 %all-reduce.4.cloned.1.call-done = (f32[3,512,1536]{2,1,0:T(8,128)}, f32[3,512,512]{2,1,0:T(8,128)}) async-done(((f32[3,512,1536]{2,1,0:T(8,128)}, f32[3,512,512]{2,1,0:T(8,128)}), (f32[3,512,1536]{2,1,0:T(8,128)}, f32[3,512,512]{2,1,0:T(8,128)})) %all-reduce.4.cloned.1.call-update) | async-done | bytes 12582928 | tf_op jit(solution)/shard_map/psum | solution.py:359
  1334.3 8.4 copy.243
  (439 shorter events, 283.8 us)
Async XLA Ops:
  7.2 26.1 %all-gather.13.cloned.1.call-start = ((), (), s32[]{:S(2)}) async-start(), calls=%async_computation.21 | async-start | bytes 1310720 | tf_op jit(solution)/shard_map/all_gather | solution.py:82
  10.5 56.5 %copy-start.59 = (f32[1,512]{1,0:T(1,128)}, f32[1,512]{1,0:T(1,128)S(1)}, u32[]{:S(2)}) copy-start(f32[1,512]{1,0:T(1,128)S(1)} %get-tuple-element.93) | copy-start | bytes 6148
  10.5 107.2 %copy-start.83 = (f32[1,512]{1,0:T(1,128)}, f32[1,512]{1,0:T(1,128)S(1)}, u32[]{:S(2)}) copy-start(f32[1,512]{1,0:T(1,128)S(1)} %get-tuple-element.90) | copy-start | bytes 6148
  10.5 136.0 %copy-start.77 = (f32[1,512]{1,0:T(1,128)}, f32[1,512]{1,0:T(1,128)S(1)}, u32[]{:S(2)}) copy-start(f32[1,512]{1,0:T(1,128)S(1)} %get-tuple-element.94) | copy-start | bytes 6148
  13.6 38.7 %all-gather.11.cloned.1.call-start = ((), (), s32[]{:S(2)}) async-start(), calls=%async_computation.20 | async-start | bytes 1310720 | tf_op jit(solution)/shard_map/all_gather | solution.py:83
  16.6 100.3 %copy-start.85 = (s32[2,256]{1,0:T(2,128)}, s32[2,256]{1,0:T(2,128)S(1)}, u32[]{:S(2)}) copy-start(s32[2,256]{1,0:T(2,128)S(1)} %bitcast_add_fusion.4) | copy-start | bytes 6148
  59.6 57.2 %copy-start.19 = (f32[1,256,512]{2,1,0:T(8,128)}, f32[1,256,512]{2,1,0:T(8,128)S(1)}, u32[]{:S(2)}) copy-start(f32[1,256,512]{2,1,0:T(8,128)S(1)} %get-tuple-element.98) | copy-start | bytes 1572868
  62.9 18.0 %all-to-all-start = ((bf16[16,64,512]{2,1,0:T(8,128)(2,1)}), bf16[16,64,512]{2,1,0:T(8,128)(2,1)S(1)}, u32[]{:S(2)}, u32[]{:S(2)}) async-start(bf16[16,64,512]{2,1,0:T(8,128)(2,1)} %reshape.801), calls=%async_computation | async-start | bytes 2097152 | tf_op jit(solution)/shard_map/all_to_all | solution.py:233
  66.5 63.3 %all-gather.9.cloned.1.call-start = ((), (), s32[]{:S(2)}) async-start(), calls=%async_computation.19 | async-start | bytes 1310720 | tf_op jit(solution)/shard_map/all_gather | solution.py:82
  97.2 19.0 %all-to-all-start.1 = ((bf16[4,256,512]{2,0,1:T(4,128)(2,1)}), bf16[4,256,512]{2,0,1:T(4,128)(2,1)S(1)}, u32[]{:S(2)}, u32[]{:S(2)}) async-start(bf16[4,256,512]{2,0,1:T(4,128)(2,1)} %copy.156), calls=%async_computation.1 | async-start | bytes 2097152 | tf_op jit(solution)/shard_map/all_to_all | solution.py:239
  100.7 38.6 %all-gather.7.cloned.1.call-start = ((), (), s32[]{:S(2)}) async-start(), calls=%async_computation.18 | async-start | bytes 1310720 | tf_op jit(solution)/shard_map/all_gather | solution.py:83
  101.6 55.1 %all-gather.17.cloned.1.call-start = ((), (), s32[]{:S(2)}) async-start(), calls=%async_computation.23 | async-start | bytes 2621440 | tf_op jit(solution)/shard_map/all_gather | solution.py:82
  121.6 139.4 %copy-start.63 = (s32[2,256]{1,0:T(2,128)}, s32[2,256]{1,0:T(2,128)S(1)}, u32[]{:S(2)}) copy-start(s32[2,256]{1,0:T(2,128)S(1)} %bitcast_add_fusion.3) | copy-start | bytes 6148
  125.7 71.5 %all-to-all-start.4 = ((bf16[16,64,512]{2,1,0:T(8,128)(2,1)}), bf16[16,64,512]{2,1,0:T(8,128)(2,1)S(1)}, u32[]{:S(2)}, u32[]{:S(2)}) async-start(bf16[16,64,512]{2,1,0:T(8,128)(2,1)} %reshape.811), calls=%async_computation.4 | async-start | bytes 2097152 | tf_op jit(solution)/shard_map/all_to_all | solution.py:260
  129.2 52.3 %all-gather.15.cloned.1.call-start = ((), (), s32[]{:S(2)}) async-start(), calls=%async_computation.22 | async-start | bytes 2621440 | tf_op jit(solution)/shard_map/all_gather | solution.py:83
  191.8 71.6 %copy-start.7 = (f32[2,256,512]{2,1,0:T(8,128)}, f32[2,256,512]{2,1,0:T(8,128)S(1)}, u32[]{:S(2)}) copy-start(f32[2,256,512]{2,1,0:T(8,128)S(1)} %get-tuple-element.108) | copy-start | bytes 3145732
  197.2 18.9 %all-to-all-start.2 = ((bf16[16,64,512]{2,1,0:T(8,128)(2,1)}), bf16[16,64,512]{2,1,0:T(8,128)(2,1)}, u32[]{:S(2)}, u32[]{:S(2)}) async-start(bf16[16,64,512]{2,1,0:T(8,128)(2,1)} %reshape.809), calls=%async_computation.2 | async-start | bytes 2097152 | tf_op jit(solution)/shard_map/all_to_all | solution.py:233
  239.5 18.0 %all-to-all-start.5 = ((bf16[4,256,512]{2,0,1:T(4,128)(2,1)}), bf16[4,256,512]{2,0,1:T(4,128)(2,1)S(1)}, u32[]{:S(2)}, u32[]{:S(2)}) async-start(bf16[4,256,512]{2,0,1:T(4,128)(2,1)} %copy.172), calls=%async_computation.5 | async-start | bytes 2097152 | tf_op jit(solution)/shard_map/all_to_all | solution.py:272
  243.0 69.4 %reduce-scatter.13.cloned.1.call-start = ((), (), s32[]{:S(2)}) async-start(), calls=%async_computation.25 | async-start | bytes 2621440 | tf_op jit(solution)/shard_map/reduce_scatter | solution.py:112
  276.9 66.3 %reduce-scatter.11.cloned.1.call-start = ((), (), s32[]{:S(2)}) async-start(), calls=%async_computation.24 | async-start | bytes 2621440 | tf_op jit(solution)/shard_map/reduce_scatter | solution.py:109
  350.9 18.0 %all-to-all-start.6 = ((bf16[16,64,512]{2,1,0:T(8,128)(2,1)}), bf16[16,64,512]{2,1,0:T(8,128)(2,1)S(1)}, u32[]{:S(2)}, u32[]{:S(2)}) async-start(bf16[16,64,512]{2,1,0:T(8,128)(2,1)} %reshape.817), calls=%async_computation.8 | async-start | bytes 2097152 | tf_op jit(solution)/shard_map/all_to_all | solution.py:260
  354.5 125.9 %reduce-scatter.21.cloned.1.call-start = ((), (), s32[]{:S(2)}) async-start(), calls=%async_computation.29 | async-start | bytes 1310720 | tf_op jit(solution)/shard_map/reduce_scatter | solution.py:112
  389.3 18.8 %all-to-all-start.7 = ((bf16[4,256,512]{2,0,1:T(4,128)(2,1)}), bf16[4,256,512]{2,0,1:T(4,128)(2,1)}, u32[]{:S(2)}, u32[]{:S(2)}) async-start(bf16[4,256,512]{2,0,1:T(4,128)(2,1)} %copy.182), calls=%async_computation.9 | async-start | bytes 2097152 | tf_op jit(solution)/shard_map/all_to_all | solution.py:272
  393.5 86.8 %reduce-scatter.19.cloned.1.call-start = ((), (), s32[]{:S(2)}) async-start(), calls=%async_computation.28 | async-start | bytes 1310720 | tf_op jit(solution)/shard_map/reduce_scatter | solution.py:109
  404.3 89.6 %reduce-scatter.17.cloned.1.call-start = ((), (), s32[]{:S(2)}) async-start(), calls=%async_computation.27 | async-start | bytes 1310720 | tf_op jit(solution)/shard_map/reduce_scatter | solution.py:112
  421.9 72.0 %reduce-scatter.15.cloned.1.call-start = ((), (), s32[]{:S(2)}) async-start(), calls=%async_computation.26 | async-start | bytes 1310720 | tf_op jit(solution)/shard_map/reduce_scatter | solution.py:109
  435.5 205.4 %reduce-scatter.29.cloned.1.call-start = ((), (), s32[]{:S(2)}) async-start(), calls=%async_computation.33 | async-start | bytes 9437184 | tf_op jit(solution)/shard_map/reduce_scatter | solution.py:372
  443.4 349.9 %reduce-scatter.27.cloned.1.call-start = ((), (), s32[]{:S(2)}) async-start(), calls=%async_computation.32 | async-start | bytes 9437184 | tf_op jit(solution)/shard_map/reduce_scatter | solution.py:369
  452.5 492.7 %reduce-scatter.25.cloned.1.call-start = ((), (), s32[]{:S(2)}) async-start(), calls=%async_computation.31 | async-start | bytes 9437184 | tf_op jit(solution)/shard_map/reduce_scatter | solution.py:366
  460.7 636.9 %reduce-scatter.23.cloned.1.call-start = ((), (), s32[]{:S(2)}) async-start(), calls=%async_computation.30 | async-start | bytes 9437184 | tf_op jit(solution)/shard_map/reduce_scatter | solution.py:363
  469.8 864.5 %all-reduce.4.cloned.1.call-start = ((), (), s32[]{:S(2)}) async-start(), calls=%async_computation.34 | async-start | bytes 25165824 | tf_op jit(solution)/shard_map/psum | solution.py:359
  512.9 18.2 %all-to-all-start.3 = ((bf16[4,256,512]{2,0,1:T(4,128)(2,1)}), bf16[4,256,512]{2,0,1:T(4,128)(2,1)S(1)}, u32[]{:S(2)}, u32[]{:S(2)}) async-start(bf16[4,256,512]{2,0,1:T(4,128)(2,1)} %copy.166), calls=%async_computation.3 | async-start | bytes 2097152 | tf_op jit(solution)/shard_map/all_to_all | solution.py:239
  (107 other events, 1327.7 us)
Sparse Core Ops, SparseCore 0:
  13.7 19.5 all-gather.12
  35.4 16.8 all-gather.10
  70.6 18.2 all-gather.8
  103.3 18.9 all-gather.6
  124.3 32.3 all-gather.16
  158.7 22.8 all-gather.14
  277.0 31.4 reduce-scatter.12
  311.7 31.4 reduce-scatter.10
  360.9 26.2 reduce-scatter.20
  404.4 26.2 reduce-scatter.18
  433.8 24.9 reduce-scatter.16
  461.8 24.8 reduce-scatter.14
  490.4 150.4 reduce-scatter.28
  644.9 148.3 reduce-scatter.26
  796.8 148.3 reduce-scatter.24
  949.1 148.3 reduce-scatter.22
  1104.4 229.8 all-reduce.3
where the time goes:
time: 1360 us; the launch traced here: 1350 us
  waiting for transfers between devices  872 us (64%)
  matrix products  243 us (18%)
  local copies, waits for them, and re-layouts  83.6 us (6%)
  other arithmetic  62.6 us (5%)
  blocking collectives  41.9 us (3%)
  starting transfers between devices  31.7 us (2%)
  between operations  16.4 us (1%)
    psum x1, waiting for transfers between devices, local(): lax.psum((inward_grads, outward_grads, gain_grads, counts), ('dp', 'exper...  234 us
    reduce_scatter x1, waiting for transfers between devices, local(): lax.psum_scatter(decoder_up_grad.astype(jnp.bfloat16), 'dp', scatter_dime...  150 us
    reduce_scatter x1, waiting for transfers between devices, local(): lax.psum_scatter(encoder_up_grad.astype(jnp.bfloat16), 'dp', scatter_dime...  150 us
    reduce_scatter x1, waiting for transfers between devices, local(): lax.psum_scatter(encoder_down_grad.astype(jnp.bfloat16), 'dp', scatter_di...  149 us
    reduce_scatter x1, waiting for transfers between devices, local(): lax.psum_scatter(decoder_down_grad.astype(jnp.bfloat16), 'dp', scatter_di...  53.7 us
    psum x1, blocking collectives, local(): lax.psum((inward_grads, outward_grads, gain_grads, counts), ('dp', 'exper...  41.9 us
    unnamed x232, local copies, waits for them, and re-layouts  39.6 us
    reduce_scatter x3, waiting for transfers between devices, attend_back(): lax.psum_scatter(keys_grad.astype(jnp.bfloat16), 'expert', scatter_dimens...  29.5 us
  transfers between devices with their start and end apart: 25, of which 17 were waited for; matrix products, arithmetic and copies ran while one was open for 21% of the time, Pallas kernels for 0%

commit v1 on v0

v1 whole, which is shorter than its diff:
```python
import functools

import jax
import jax.numpy as jnp
from jax import lax
from jax.experimental import pallas as pl
from jax.experimental.pallas import tpu as pltpu
from jax.sharding import PartitionSpec as P

HEAD_DIM = 64
EXPERTS = 16
NORM_EPSILON = 1e-05
MASKED = -1e30
F32 = jnp.float32
BF16 = jnp.bfloat16
VMEM_LIMIT = 58 << 20


def nn(a, b):
    return jnp.dot(a, b, preferred_element_type=F32)


def nt(a, b):
    return lax.dot_general(a, b, (((1,), (1,)), ((), ())), preferred_element_type=F32)


def tn(a, b):
    return lax.dot_general(a, b, (((0,), (0,)), ((), ())), preferred_element_type=F32)


def tt(a, b):
    return lax.dot_general(a, b, (((0,), (1,)), ((), ())), preferred_element_type=F32)


def norm_parts(x):
    mean = jnp.mean(x, axis=-1, keepdims=True)
    centered = x - mean
    spread = jnp.mean(centered * centered, axis=-1, keepdims=True)
    scale = lax.rsqrt(spread + NORM_EPSILON)
    return centered * scale, scale


def norm(x, gain):
    return norm_parts(x)[0] * gain


def norm_back(x, gain, grad):
    hat, scale = norm_parts(x)
    inner = grad * gain
    dx = scale * (
        inner
        - jnp.mean(inner, axis=-1, keepdims=True)
        - hat * jnp.mean(inner * hat, axis=-1, keepdims=True)
    )
    return dx, jnp.sum(grad * hat, axis=0, keepdims=True)


GELU_A = 0.7978845608028654
GELU_B = 0.044715


def gelu(x):
    return 0.5 * x * (1.0 + jnp.tanh(GELU_A * (x + GELU_B * (x * x * x))))


def gelu_both(x):
    sq = x * x
    th = jnp.tanh(x * (GELU_A + (GELU_A * GELU_B) * sq))
    half = 0.5 * (1.0 + th)
    slope = half + (0.5 * x) * (1.0 - th * th) * (GELU_A + (3.0 * GELU_A * GELU_B) * sq)
    return x * half, slope


def whole(shape):
    return pl.BlockSpec(shape, lambda *_: (0,) * len(shape))


def call(body, ins, outs, name, grid=None, in_specs=None, out_specs=None, scratch=(), scalars=(), flops=0):
    if in_specs is None:
        in_specs = [None] * len(ins)
    if out_specs is None:
        out_specs = [None] * len(outs)
    in_specs = [whole(a.shape) if s is None else s for a, s in zip(ins, in_specs)]
    out_specs = [whole(o[0]) if s is None else s for o, s in zip(outs, out_specs)]
    moved = sum(a.size * a.dtype.itemsize for a in ins) + sum(
        functools.reduce(lambda x, y: x * y, o[0], 1) * jnp.dtype(o[1]).itemsize for o in outs
    )
    spec = pltpu.PrefetchScalarGridSpec(
        num_scalar_prefetch=len(scalars),
        grid=(1,) if grid is None else grid,
        in_specs=in_specs,
        out_specs=out_specs,
        scratch_shapes=list(scratch),
    )
    return pl.pallas_call(
        body,
        out_shape=[jax.ShapeDtypeStruct(s, d) for s, d in outs],
        grid_spec=spec,
        name=name,
        compiler_params=pltpu.CompilerParams(vmem_limit_bytes=VMEM_LIMIT),
        cost_estimate=pl.CostEstimate(flops=flops, bytes_accessed=moved, transcendentals=0),
    )(*scalars, *ins)


def head_rows(values, h):
    rows = values[h * HEAD_DIM : (h + 1) * HEAD_DIM]
    zero = jnp.zeros_like(rows)
    return jnp.concatenate([rows, zero] if h % 2 == 0 else [zero, rows], axis=0)


def head_lanes(values, h):
    pair = values[:, (h // 2) * 128 : (h // 2 + 1) * 128]
    lane = lax.broadcasted_iota(jnp.int32, pair.shape, 1)
    keep = lane < HEAD_DIM if h % 2 == 0 else lane >= HEAD_DIM
    return jnp.where(keep, pair, jnp.zeros_like(pair))


def causal_allow(me, ids, rows):
    parts = []
    for r in ids:
        key = (me ^ r) * rows + lax.broadcasted_iota(jnp.int32, (rows, rows), 0)
        query = me * rows + lax.broadcasted_iota(jnp.int32, (rows, rows), 1)
        parts.append(key <= query)
    return jnp.concatenate([p.astype(F32) for p in parts], axis=0) > 0.5


def attend_forward(q_t, k, v_t, allow, o_t, lse):
    heads = q_t.shape[0] // HEAD_DIM
    for h in range(heads):
        pair = slice((h // 2) * 128, (h // 2 + 1) * 128)
        scores = nn(k[:, pair], head_rows(q_t, h))
        if allow is not None:
            scores = jnp.where(allow, scores, MASKED)
        top = jnp.max(scores, axis=0, keepdims=True)
        lifted = jnp.exp(scores - top)
        total = jnp.sum(lifted, axis=0, keepdims=True)
        rows = slice(h * HEAD_DIM, (h + 1) * HEAD_DIM)
        blended = nn(v_t[rows, :], lifted.astype(BF16)) * (1.0 / total)
        o_t[rows, :] = blended.astype(BF16)
        lse[h : h + 1, :] = top + jnp.log(total)


def attend_backward(q, k, v, k_t, do, lse, allow, dk, dv, dq_t):
    heads = q.shape[1] // HEAD_DIM
    q_t = q.astype(F32).T.astype(BF16)
    do_t = do.astype(F32).T.astype(BF16)
    for h2 in range(heads // 2):
        pair = slice(h2 * 128, (h2 + 1) * 128)
        dk_pair = None
        for h in (2 * h2, 2 * h2 + 1):
            rows = slice(h * HEAD_DIM, (h + 1) * HEAD_DIM)
            scores = nn(k[:, pair], head_rows(q_t, h))
            weights = jnp.exp(scores - lse[h : h + 1, :])
            if allow is not None:
                weights = jnp.where(allow, weights, 0.0)
            weights_grad = nn(v[:, pair], head_rows(do_t, h))
            centre = jnp.sum(weights * weights_grad, axis=0, keepdims=True)
            scores_grad = (weights * (weights_grad - centre)).astype(BF16)
            dv_part = nn(weights.astype(BF16), head_lanes(do, h))
            dk_part = nn(scores_grad, head_lanes(q, h))
            dq_t[rows, :] = (nn(k_t[rows, :], scores_grad) * HEAD_DIM ** (-0.5)).astype(BF16)
            if dk_pair is None:
                dk_pair, dv_pair = dk_part, dv_part
            else:
                dk_pair, dv_pair = dk_pair + dk_part, dv_pair + dv_part
        dk[:, pair] = dk_pair.astype(BF16)
        dv[:, pair] = dv_pair.astype(BF16)


def piece_blocks(pieces):
    return [(ref, i) for ref in pieces for i in range(ref.shape[0])]


def self_forward(pieces, ids, me, gain, gain_next, inward, outward, causal):
    rows, feature = pieces[0].shape[1:]
    length = len(ids) * rows
    heads = feature // HEAD_DIM
    count = len(pieces)

    def body(me_ref, *refs):
        parts = refs[:count]
        g, gn, win, wout, out, nxt, hm, k, k_t, v, q, o_t, lse, v_t = refs[count:]
        for b, (ref, i) in enumerate(piece_blocks(parts)):
            hm[b * rows : (b + 1) * rows, :] = norm(ref[i].astype(F32), g[...]).astype(BF16)
        hm_all = hm[...]
        k[...] = nn(hm_all, win[:, feature : 2 * feature]).astype(BF16)
        v[...] = nn(hm_all, win[:, 2 * feature :]).astype(BF16)
        k_t[...] = tt(win[:, feature : 2 * feature], hm_all).astype(BF16)
        v_t[...] = tt(win[:, 2 * feature :], hm_all).astype(BF16)
        q_scaled = nn(hm[0:rows, :], win[:, :feature]).astype(BF16).astype(F32) * HEAD_DIM ** (-0.5)
        q[...] = q_scaled.astype(BF16)
        allow = causal_allow(me_ref[0], ids, rows) if causal else None
        attend_forward(q_scaled.T.astype(BF16), k, v_t, allow, o_t, lse)
        merged = o_t[...].astype(F32).T.astype(BF16)
        after = parts[0][0].astype(F32) + nn(merged, wout[...])
        out[...] = after
        nxt[...] = norm(after, gn[...]).astype(BF16)

    return call(
        body,
        [*pieces, gain, gain_next, inward, outward],
        [
            ((rows, feature), F32),
            ((rows, feature), BF16),
            ((length, feature), BF16),
            ((length, feature), BF16),
            ((feature, length), BF16),
            ((length, feature), BF16),
            ((rows, feature), BF16),
            ((feature, rows), BF16),
            ((heads, rows), F32),
        ],
        "self_forward",
        scratch=[pltpu.VMEM((feature, length), BF16)],
        scalars=[me],
        flops=2 * length * feature * (4 * feature + 4 * rows),
    )


def weight_grad_store(dw, feature, hq, hm, dq, dk, dv, o_t, d_branch):
    dw[:, :feature] = tn(hq, dq).astype(BF16)
    dw[:, feature : 2 * feature] = tn(hm, dk).astype(BF16)
    dw[:, 2 * feature : 3 * feature] = tn(hm, dv).astype(BF16)
    dw[:, 3 * feature :] = nn(o_t, d_branch).astype(BF16)


def store_blocks(outs, values, rows):
    for b, (ref, i) in enumerate(piece_blocks(outs)):
        ref[i] = values[b * rows : (b + 1) * rows].astype(BF16)


def self_backward_core(me_ref, ids, causal, d_branch, saved, win, wout, outs, dw, scratch):
    hm, k, k_t, v, q, o_t, lse = saved
    dk, dv, dq_t = scratch
    rows, feature = q.shape
    do = nt(d_branch, wout[...]).astype(BF16)
    allow = causal_allow(me_ref[0], ids, rows) if causal else None
    attend_backward(q[...], k, v, k_t, do, lse, allow, dk, dv, dq_t)
    dq = dq_t[...].astype(F32).T.astype(BF16)
    for b, (ref, i) in enumerate(piece_blocks(outs)):
        span = slice(b * rows, (b + 1) * rows)
        part = nt(dk[span, :], win[:, feature : 2 * feature]) + nt(dv[span, :], win[:, 2 * feature :])
        if b == 0:
            part = part + nt(dq, win[:, :feature])
        ref[i] = part.astype(BF16)
    weight_grad_store(dw, feature, hm[0:rows, :], hm[...], dq, dk[...], dv[...], o_t[...], d_branch)


def self_backward(upstream, ids, sizes, me, saved, inward, outward, causal):
    rows, feature = upstream.shape
    length = len(ids) * rows
    count = len(sizes)

    def body(me_ref, up, hm, k, k_t, v, q, o_t, lse, win, wout, *refs):
        outs, dw, scratch = refs[:count], refs[count], refs[count + 1 :]
        self_backward_core(
            me_ref, ids, causal, up[...].astype(BF16), (hm, k, k_t, v, q, o_t, lse), win, wout, outs, dw, scratch
        )

    return call(
        body,
        [upstream, *saved, inward, outward],
        [((n, rows, feature), BF16) for n in sizes] + [((feature, 4 * feature), BF16)],
        "self_backward",
        scratch=[
            pltpu.VMEM((length, feature), BF16),
            pltpu.VMEM((length, feature), BF16),
            pltpu.VMEM((feature, rows), BF16),
        ],
        scalars=[me],
        flops=2 * length * feature * (4 * feature + 10 * rows),
    )


def gather_rows(me, experts, cap, col, returned):
    total = None
    slots = experts * cap
    for r, rows in returned:
        local = col - (me ^ r) * slots
        hot = (local == lax.broadcasted_iota(jnp.int32, (col.shape[0], slots), 1)).astype(BF16)
        part = nn(hot, rows.reshape(slots, rows.shape[-1]))
        total = part if total is None else total + part
    return total


def spread_rows(me, experts, cap, col, tokens):
    slots = experts * cap
    local = col - me * slots
    hot = (local == lax.broadcasted_iota(jnp.int32, (slots, col.shape[1]), 0)).astype(BF16)
    return nn(hot, tokens).astype(BF16)


def fill_buffers(me, experts, cap, cols, token_of, sources, dest):
    for s in range(sources):
        for p in range(2):
            rows = spread_rows(me, experts, cap, cols[2 * s + p], token_of(s, p))
            at = (2 * s + p) * cap
            for j in range(experts):
                dest[j, at : at + cap, :] = rows[j * cap : (j + 1) * cap]


def expert_forward(pieces, cols, me, weight_up, weight_down, ids):
    experts, hidden, feature = weight_up.shape
    rows = pieces[0].shape[1]
    cap = 2 * rows // EXPERTS
    count = len(pieces)
    sources = len(ids)
    length = sources * 2 * cap

    def body(me_ref, *refs):
        parts = refs[:count]
        col, up, down = refs[count : count + 3]
        outs = refs[count + 3 : count + 3 + sources]
        buf = refs[-1]
        j = pl.program_id(0)

        @pl.when(j == 0)
        def _():
            blocks = piece_blocks(parts)
            fill_buffers(me_ref[0], experts, cap, col, lambda s, p: blocks[s][0][blocks[s][1]], sources, buf)

        x = buf[j]
        act = gelu(nt(x, up[0])).astype(BF16)
        res = nn(act, down[0]).astype(BF16)
        for s in range(sources):
            for p in range(2):
                at = (2 * s + p) * cap
                outs[s][0, p] = res[at : at + cap]

    weight = pl.BlockSpec((1, hidden, feature), lambda j, *_: (j, 0, 0))
    return call(
        body,
        [*pieces, cols, weight_up, weight_down],
        [((experts, 2, cap, feature), BF16)] * sources,
        "expert_forward",
        grid=(experts,),
        in_specs=[None] * (count + 1) + [weight, weight],
        out_specs=[pl.BlockSpec((1, 2, cap, feature), lambda j, *_: (j, 0, 0, 0))] * sources,
        scratch=[pltpu.VMEM((experts, length, feature), BF16)],
        scalars=[me],
        flops=4 * experts * length * hidden * feature,
    )


def expert_backward(pieces, grads, cols, me, weight_up, weight_down, ids, with_result):
    experts, hidden, feature = weight_up.shape
    rows = grads[0].shape[2]
    cap = 2 * rows // EXPERTS
    count = len(pieces)
    sources = len(ids)
    length = sources * 2 * cap
    both = pieces[0].ndim == 4
    kinds = 2 if with_result else 1

    def body(me_ref, *refs):
        parts = refs[:count]
        gparts = refs[count : 2 * count]
        col, up, down = refs[2 * count : 2 * count + 3]
        outs = refs[2 * count + 3 : 2 * count + 3 + kinds * sources]
        buf, gbuf = refs[-2:]
        j = pl.program_id(0)

        @pl.when(j == 0)
        def _():
            blocks = piece_blocks(parts)
            gblocks = piece_blocks(gparts)
            pick = lambda s, p: blocks[s][0][blocks[s][1], p] if both else blocks[s][0][blocks[s][1]]
            fill_buffers(me_ref[0], experts, cap, col, pick, sources, buf)
            gpick = lambda s, p: gblocks[s][0][gblocks[s][1], p]
            fill_buffers(me_ref[0], experts, cap, col, gpick, sources, gbuf)

        value, slope = gelu_both(nt(buf[j], up[0]))
        hidden_grad = (slope * nt(gbuf[j], down[0])).astype(BF16)
        dx = nn(hidden_grad, up[0]).astype(BF16)
        results = [dx]
        if with_result:
            results.append(nn(value.astype(BF16), down[0]).astype(BF16))
        for n, res in enumerate(results):
            for s in range(sources):
                for p in range(2):
                    at = (2 * s + p) * cap
                    outs[n * sources + s][0, p] = res[at : at + cap]

    weight = pl.BlockSpec((1, hidden, feature), lambda j, *_: (j, 0, 0))
    outs = call(
        body,
        [*pieces, *grads, cols, weight_up, weight_down],
        [((experts, 2, cap, feature), BF16)] * (kinds * sources),
        "expert_backward",
        grid=(experts,),
        in_specs=[None] * (2 * count + 1) + [weight, weight],
        out_specs=[pl.BlockSpec((1, 2, cap, feature), lambda j, *_: (j, 0, 0, 0))] * (kinds * sources),
        scratch=[pltpu.VMEM((experts, length, feature), BF16)] * 2,
        scalars=[me],
        flops=(8 if with_result else 6) * experts * length * hidden * feature,
    )
    return outs[:sources], outs[sources:]


def expert_weights(pieces, grads, cols, place, weight_up, weight_down, sources, ny, nz):
    experts, hidden, feature = weight_up.shape
    rows = grads[0].shape[2]
    cap = 2 * rows // EXPERTS
    count, gcount = len(pieces), len(grads)
    length = sources * 2 * cap
    both = pieces[0].ndim == 4
    span = hidden // (ny * nz)

    def body(place_ref, *refs):
        parts = refs[:count]
        gparts = refs[count : count + gcount]
        col, up, down = refs[count + gcount : count + gcount + 3]
        up_out, down_out, buf, gbuf = refs[count + gcount + 3 :]
        j = pl.program_id(0)

        @pl.when((j == 0) & (pl.program_id(1) == 0))
        def _():
            blocks = piece_blocks(parts)
            gblocks = piece_blocks(gparts)
            pick = lambda s, p: blocks[s][0][blocks[s][1], p] if both else blocks[s][0][blocks[s][1]]
            fill_buffers(place_ref[0], experts, cap, col, pick, sources, buf)
            gpick = lambda s, p: gblocks[s][0][gblocks[s][1], p]
            fill_buffers(place_ref[0], experts, cap, col, gpick, sources, gbuf)

        x, g = buf[j], gbuf[j]
        value, slope = gelu_both(nt(up[0], x))
        hidden_grad = (slope * nt(down[0], g)).astype(BF16)
        up_out[0, 0] = nn(hidden_grad, x).astype(BF16)
        down_out[0, 0] = nn(value.astype(BF16), g).astype(BF16)

    weight = pl.BlockSpec((1, span, feature), lambda j, r, place_ref: (j, place_ref[1] * ny + (place_ref[2] ^ r), 0))
    out = pl.BlockSpec((1, 1, span, feature), lambda j, r, *_: (r, j, 0, 0))
    return call(
        body,
        [*pieces, *grads, cols, weight_up, weight_down],
        [((ny, experts, span, feature), BF16)] * 2,
        "expert_weights",
        grid=(experts, ny),
        in_specs=[None] * (count + gcount + 1) + [weight, weight],
        out_specs=[out, out],
        scratch=[pltpu.VMEM((experts, length, feature), BF16)] * 2,
        scalars=[place],
        flops=8 * experts * length * (hidden // nz) * feature,
    )


def combine_norm(returned, ids, col, me, residual, gain):
    experts, _, cap, feature = returned[0].shape
    rows = residual.shape[-2]
    count = len(ids)

    def body(me_ref, *refs):
        ret = refs[:count]
        c, res, g, out, nxt = refs[count:]
        for p in range(2):
            mixed = gather_rows(me_ref[0], experts, cap, c[p], [(r, ref[:, p]) for r, ref in zip(ids, ret)])
            after = res[...] + mixed
            out[p] = after
            nxt[p] = norm(after, g[...]).astype(BF16)

    return call(
        body,
        [*returned, col, residual, gain],
        [((2, rows, feature), F32), ((2, rows, feature), BF16)],
        "combine_norm",
        scalars=[me],
        flops=4 * rows * EXPERTS * cap * feature,
    )


def combine_output(returned, ids, col, me, residual):
    experts, _, cap, feature = returned[0].shape
    rows = residual.shape[-2]
    count = len(ids)

    def body(me_ref, *refs):
        ret = refs[:count]
        c, res, out = refs[count:]
        for p in range(2):
            mixed = gather_rows(me_ref[0], experts, cap, c[p], [(r, ref[:, p]) for r, ref in zip(ids, ret)])
            out[p] = (res[p] + mixed).astype(BF16)

    return call(
        body,
        [*returned, col, residual],
        [((2, rows, feature), BF16)],
        "combine_output",
        scalars=[me],
        flops=4 * rows * EXPERTS * cap * feature,
    )[0]


def cross_forward(hc, pieces, ids, mid, gain, inward, outward):
    rows, feature = hc.shape
    length = len(ids) * rows
    heads = feature // HEAD_DIM
    count = len(pieces)

    def body(*refs):
        h, *parts = refs[: count + 1]
        res, g, win, wout, out, nxt, hm, k, k_t, v, q, o_t, lse, v_t = refs[count + 1 :]
        for b, (ref, i) in enumerate(piece_blocks(parts)):
            hm[0, b * rows : (b + 1) * rows, :] = ref[i, 0]
        hm_all = hm[0]
        k[0] = nn(hm_all, win[:, feature : 2 * feature]).astype(BF16)
        v[0] = nn(hm_all, win[:, 2 * feature :]).astype(BF16)
        k_t[0] = tt(win[:, feature : 2 * feature], hm_all).astype(BF16)
        v_t[...] = tt(win[:, 2 * feature :], hm_all).astype(BF16)
        q_scaled = nn(h[...], win[:, :feature]).astype(BF16).astype(F32) * HEAD_DIM ** (-0.5)
        q[...] = q_scaled.astype(BF16)
        attend_forward(q_scaled.T.astype(BF16), k.at[0], v_t, None, o_t.at[0], lse.at[0])
        merged = o_t[0].astype(F32).T.astype(BF16)
        after = res[...] + nn(merged, wout[...])
        out[0] = after
        nxt[0] = norm(after, g[...]).astype(BF16)

    per = lambda *shape: pl.BlockSpec((1,) + shape, lambda p, *_: (p,) + (0,) * len(shape))
    return call(
        body,
        [hc, *pieces, mid, gain, inward, outward],
        [
            ((2, rows, feature), F32),
            ((2, rows, feature), BF16),
            ((2, length, feature), BF16),
            ((2, length, feature), BF16),
            ((2, feature, length), BF16),
            ((2, length, feature), BF16),
            ((rows, feature), BF16),
            ((2, feature, rows), BF16),
            ((2, heads, rows), F32),
        ],
        "cross_forward",
        grid=(2,),
        in_specs=[None]
        + [pl.BlockSpec((a.shape[0], 1, rows, feature), lambda p, *_: (0, p, 0, 0)) for a in pieces]
        + [None] * 4,
        out_specs=[
            per(rows, feature),
            per(rows, feature),
            per(length, feature),
            per(length, feature),
            per(feature, length),
            per(length, feature),
            None,
            per(feature, rows),
            per(heads, rows),
        ],
        scratch=[pltpu.VMEM((feature, length), BF16)],
        flops=4 * length * feature * (4 * feature + 4 * rows),
    )


def cross_backward(returned, ids, sizes, col, me, crossed, gain_w, out_grad, saved, hc, mid, gain_c, inward, outward):
    experts, _, cap, feature = returned[0].shape
    rows = mid.shape[0]
    length = len(ids) * rows
    heads = feature // HEAD_DIM
    count = len(ids)
    npieces = len(sizes)

    def body(me_ref, *refs):
        ret = refs[:count]
        c, t2, gw, og, hm, k, k_t, v, q, o_t, lse, h, t1, gc, win, wout = refs[count : count + 16]
        rest = refs[count + 16 :]
        outs = rest[:npieces]
        dw, dt1, dgw, dgc = rest[npieces : npieces + 4]
        dk, dv, dq_t, dw_acc, dh_acc = rest[npieces + 4 :]
        p = pl.program_id(0)
        dwr = gather_rows(me_ref[0], experts, cap, c[0], [(r, ref[:, 0]) for r, ref in zip(ids, ret)])
        dx, dg = norm_back(t2[0], gw[...], dwr)
        upstream = og[0] + dx
        d_branch = upstream.astype(BF16)
        do = nt(d_branch, wout[...]).astype(BF16)
        attend_backward(q[...], k.at[0], v.at[0], k_t.at[0], do, lse.at[0], None, dk, dv, dq_t)
        dq = dq_t[...].astype(F32).T.astype(BF16)
        for b, (ref, i) in enumerate(piece_blocks(outs)):
            span = slice(b * rows, (b + 1) * rows)
            part = nt(dk[span, :], win[:, feature : 2 * feature]) + nt(dv[span, :], win[:, 2 * feature :])
            ref[i, 0] = part.astype(BF16)
        dh = nt(dq, win[:, :feature])
        grads = [
            tn(h[...], dq),
            tn(hm[0], dk[...]),
            tn(hm[0], dv[...]),
            nn(o_t[0], d_branch),
        ]

        @pl.when(p == 0)
        def _():
            for n, value in enumerate(grads):
                dw_acc[:, n * feature : (n + 1) * feature] = value
            dh_acc[...] = dh
            dt1[...] = upstream
            dgw[...] = dg

        @pl.when(p == 1)
        def _():
            for n, value in enumerate(grads):
                at = slice(n * feature, (n + 1) * feature)
                dw[:, at] = (dw_acc[:, at] + value).astype(BF16)
            back, dg_c = norm_back(t1[...], gc[...], dh_acc[...] + dh)
            dt1[...] = dt1[...] + upstream + back
            dgw[...] = dgw[...] + dg
            dgc[...] = dg_c

    per = lambda *shape: pl.BlockSpec((1,) + shape, lambda p, *_: (p,) + (0,) * len(shape))
    return call(
        body,
        [*returned, col, crossed, gain_w, out_grad, *saved, hc, mid, gain_c, inward, outward],
        [((n, 2, rows, feature), BF16) for n in sizes]
        + [((feature, 4 * feature), BF16), ((rows, feature), F32), ((1, feature), F32), ((1, feature), F32)],
        "cross_backward",
        grid=(2,),
        in_specs=[pl.BlockSpec((experts, 1, cap, feature), lambda p, *_: (0, p, 0, 0))] * count
        + [
            per(rows, 1),
            per(rows, feature),
            None,
            per(rows, feature),
            per(length, feature),
            per(length, feature),
            per(feature, length),
            per(length, feature),
            None,
            per(feature, rows),
            per(heads, rows),
            None,
            None,
            None,
            None,
            None,
        ],
        out_specs=[pl.BlockSpec((n, 1, rows, feature), lambda p, *_: (0, p, 0, 0)) for n in sizes] + [None] * 4,
        scratch=[
            pltpu.VMEM((length, feature), BF16),
            pltpu.VMEM((length, feature), BF16),
            pltpu.VMEM((feature, rows), BF16),
            pltpu.VMEM((feature, 4 * feature), F32),
            pltpu.VMEM((rows, feature), F32),
        ],
        scalars=[me],
        flops=4 * length * feature * (4 * feature + 10 * rows),
    )


def memory_backward(parts, final, gain):
    _, rows, feature = final.shape
    count = len(parts)

    def body(*refs):
        p = refs[:count]
        x, g, out, low, dg = refs[count:]
        total = None
        for n in range(2):
            grad = p[0][n].astype(F32)
            for other in p[1:]:
                grad = grad + other[n].astype(F32)
            dx, dgain = norm_back(x[n], g[...], grad)
            out[n] = dx
            low[n] = dx.astype(BF16)
            total = dgain if total is None else total + dgain
        dg[...] = total

    return call(
        body,
        [*parts, final, gain],
        [((2, rows, feature), F32), ((2, rows, feature), BF16), ((1, feature), F32)],
        "memory_backward",
    )


def encoder_backward(returned, ids, sizes, col, me, attended, gain, final_grad, saved, inward, outward):
    experts, _, cap, feature = returned[0].shape
    rows = attended.shape[0]
    length = len(ids) * rows
    count = len(ids)
    npieces = len(sizes)

    def body(me_ref, *refs):
        ret = refs[:count]
        c, e1, g, fg, hm, k, k_t, v, q, o_t, lse, win, wout = refs[count : count + 13]
        rest = refs[count + 13 :]
        outs = rest[:npieces]
        dw, de1, dg = rest[npieces : npieces + 3]
        scratch = rest[npieces + 3 :]
        du = None
        for p in range(2):
            part = gather_rows(me_ref[0], experts, cap, c[p], [(r, ref[:, p]) for r, ref in zip(ids, ret)])
            du = part if du is None else du + part
        dx, dgain = norm_back(e1[...], g[...], du)
        upstream = fg[0] + fg[1] + dx
        de1[...] = upstream
        dg[...] = dgain
        self_backward_core(
            me_ref, ids, False, upstream.astype(BF16), (hm, k, k_t, v, q, o_t, lse), win, wout, outs, dw, scratch
        )

    return call(
        body,
        [*returned, col, attended, gain, final_grad, *saved, inward, outward],
        [((n, rows, feature), BF16) for n in sizes]
        + [((feature, 4 * feature), BF16), ((rows, feature), F32), ((1, feature), F32)],
        "encoder_backward",
        scratch=[
            pltpu.VMEM((length, feature), BF16),
            pltpu.VMEM((length, feature), BF16),
            pltpu.VMEM((feature, rows), BF16),
        ],
        scalars=[me],
        flops=2 * length * feature * (4 * feature + 10 * rows),
    )


def input_backward(parts, values, gain, upstream):
    rows, feature = upstream.shape
    count = len(parts)

    def body(*refs):
        p = refs[:count]
        x, g, up, out, dg = refs[count:]
        grad = p[0][...].reshape(rows, feature).astype(F32)
        for other in p[1:]:
            grad = grad + other[...].reshape(rows, feature).astype(F32)
        dx, dgain = norm_back(x[...].astype(F32), g[...], grad)
        out[...] = up[...] + dx
        dg[...] = dgain

    return call(
        body,
        [*parts, values, gain, upstream],
        [((rows, feature), F32), ((1, feature), F32)],
        "input_backward",
    )


AXES = ("dp", "expert")


def flip(value, n_dp, n_expert, dp_bits, expert_bits):
    pairs = []
    for d in range(n_dp):
        for e in range(n_expert):
            pairs.append((d * n_expert + e, (d ^ dp_bits) * n_expert + (e ^ expert_bits)))
    return lax.ppermute(value, AXES, pairs)


def bits_down(n):
    out, b = [], n // 2
    while b >= 1:
        out.append(b)
        b //= 2
    return out


def local(
    n_dp,
    n_expert,
    source,
    target,
    attention_in,
    attention_out,
    norm_gains,
    encoder_up,
    encoder_down,
    decoder_up,
    decoder_down,
    encoder_route,
    encoder_slot,
    decoder_route,
    decoder_slot,
    output_grad,
):
    _, rows, feature = source.shape
    cap = 2 * rows // EXPERTS
    ny = 2 if n_dp <= 8 else 4
    nz = n_dp // ny
    me = lax.axis_index("expert").astype(jnp.int32)
    dp = lax.axis_index("dp").astype(jnp.int32)
    place = jnp.stack([me, dp // ny, dp % ny])
    me1 = me[None]
    swap = lambda v, d, e: flip(v, n_dp, n_expert, d, e)

    ids, sizes = [0], [1]
    for b in bits_down(n_expert):
        sizes.append(len(ids))
        ids = ids + [i ^ b for i in ids]

    def gather_expert(value):
        pieces = [value]
        for b in bits_down(n_expert):
            joined = pieces[0] if len(pieces) == 1 else jnp.concatenate(pieces, axis=0)
            pieces.append(swap(joined, 0, b))
        return pieces

    def scatter_expert(pieces):
        pieces = list(pieces)
        bits = bits_down(n_expert)
        for b in reversed(bits):
            got = swap(pieces.pop(), 0, b)
            if len(pieces) == 1:
                return [pieces[0], got]
            at, fresh = 0, []
            for piece in pieces:
                n = piece.shape[0]
                fresh.append((piece.astype(F32) + got[at : at + n].astype(F32)).astype(BF16))
                at += n
            pieces = fresh

    def gather_far(value, keep):
        mine = [value]
        for b in bits_down(nz):
            joined = mine[0] if len(mine) == 1 else jnp.concatenate(mine, axis=0)
            mine.append(swap(joined, b * ny, 0))
        far = jnp.concatenate(mine[1:], axis=0)
        pieces = [far]
        for b in bits_down(n_expert):
            joined = pieces[0] if len(pieces) == 1 else jnp.concatenate(pieces, axis=0)
            pieces.append(swap(joined, 0, b))
        return list(keep) + pieces

    def give_back(blocks):
        return [b if r == 0 else swap(b, 0, r) for r, b in zip(ids, blocks)]

    def finish_weights(grads):
        blocks = [grads[i] for i in range(ny)]
        half = ny // 2
        while half >= 1:
            got = swap(jnp.concatenate([b[None] for b in blocks[half:]], axis=0), half, 0)
            if half > 1:
                blocks = [
                    (blocks[i].astype(F32) + got[i].astype(F32)).astype(BF16) for i in range(half)
                ]
            else:
                return blocks[0].astype(F32) + got[0].astype(F32)
            half //= 2

    columns = jnp.stack(
        [encoder_route * cap + encoder_slot, decoder_route * cap + decoder_slot]
    ).reshape(2, 2, rows)
    near = gather_expert(columns[None])
    all_columns = gather_far(columns[None], near)
    near = jnp.concatenate(near, axis=0)
    all_columns = jnp.concatenate(all_columns, axis=0)
    near_cols = [near[:, l].reshape(-1, 1, rows) for l in range(2)]
    far_cols = [all_columns[:, l].reshape(-1, 1, rows) for l in range(2)]
    own_cols = [columns[l].reshape(2, rows, 1) for l in range(2)]
    sources = n_expert * nz

    gains = [norm_gains[i : i + 1] for i in range(6)]
    source_pieces = gather_expert(source)
    target_pieces = gather_expert(target)
    out_grad = output_grad.reshape(2, rows, feature)
    og = out_grad.astype(BF16)[None]
    og_near = gather_expert(og)
    og_all = gather_far(og, og_near)

    e1, u, *enc_saved = self_forward(
        source_pieces, ids, me1, gains[0], gains[1], attention_in[0], attention_out[0], False
    )
    u_near = gather_expert(u[None])
    u_all = gather_far(u[None], u_near)
    t1, hc, *dec_saved = self_forward(
        target_pieces, ids, me1, gains[3], gains[4], attention_in[1], attention_out[1], True
    )
    returned = give_back(expert_forward(u_near, near_cols[0], me1, encoder_up, encoder_down, ids))
    e2, memory = combine_norm(returned, ids, own_cols[0], me1, e1, gains[2])
    memory_near = gather_expert(memory[None])
    t2, w, *cross_saved = cross_forward(
        hc, memory_near, ids, t1, gains[5], attention_in[2], attention_out[2]
    )
    w_near = gather_expert(w[None])
    w_all = gather_far(w[None], w_near)
    dx_blocks, res_blocks = expert_backward(
        w_near, og_near, near_cols[1], me1, decoder_up, decoder_down, ids, True
    )

    dx_back = give_back(dx_blocks)
    res_back = give_back(res_blocks)
    *dmem, cross_dw, dt1, dg5, dg4 = cross_backward(
        dx_back,
        ids,
        sizes,
        own_cols[1],
        me1,
        t2,
        gains[5],
        out_grad,
        cross_saved,
        hc,
        t1,
        gains[4],
        attention_in[2],
        attention_out[2],
    )
    decoder_output = combine_output(res_back, ids, own_cols[1], me1, t2)
    dmem_parts = scatter_expert(dmem)
    fg, fg_low, dg2 = memory_backward(
        [d.reshape(2, rows, feature) for d in dmem_parts], e2, gains[2]
    )
    fg_near = gather_expert(fg_low[None])
    fg_all = gather_far(fg_low[None], fg_near)
    du_blocks, _ = expert_backward(
        u_near, fg_near, near_cols[0], me1, encoder_up, encoder_down, ids, False
    )
    du_back = give_back(du_blocks)
    *dht, dec_dw = self_backward(
        dt1, ids, sizes, me1, dec_saved, attention_in[1], attention_out[1], True
    )
    target_grad, dg3 = input_backward(scatter_expert(dht), target[0], gains[3], dt1)
    dec_up_g, dec_down_g = expert_weights(
        w_all, og_all, far_cols[1], place, decoder_up, decoder_down, sources, ny, nz
    )
    *dhs, enc_dw, de1, dg1 = encoder_backward(
        du_back,
        ids,
        sizes,
        own_cols[0],
        me1,
        e1,
        gains[1],
        fg,
        enc_saved,
        attention_in[0],
        attention_out[0],
    )
    source_grad, dg0 = input_backward(scatter_expert(dhs), source[0], gains[0], de1)
    enc_up_g, enc_down_g = expert_weights(
        u_all, fg_all, far_cols[0], place, encoder_up, encoder_down, sources, ny, nz
    )

    counts = jnp.sum(
        (
            jnp.stack([encoder_route, decoder_route]).reshape(2, 2, rows, 1)
            == jnp.arange(EXPERTS, dtype=jnp.int32)
        ).astype(F32),
        axis=2,
    )
    gain_grads = jnp.concatenate([dg0, dg1, dg2, dg3, dg4, dg5], axis=0)
    dw = jnp.stack([enc_dw, dec_dw, cross_dw])
    dw = lax.psum(dw, AXES).astype(F32)
    gain_grads, counts = lax.psum((gain_grads, counts), AXES)

    return (
        decoder_output.reshape(2, 1, rows, feature),
        source_grad[None],
        target_grad[None],
        dw[..., : 3 * feature],
        dw[..., 3 * feature :],
        gain_grads,
        finish_weights(enc_up_g),
        finish_weights(enc_down_g),
        finish_weights(dec_up_g),
        finish_weights(dec_down_g),
        counts.astype(jnp.int32),
    )


def solution(mesh):
    n_dp, n_expert = mesh.shape["dp"], mesh.shape["expert"]
    in_specs = (
        P("dp", "expert", None),
        P("dp", "expert", None),
        P(),
        P(),
        P(),
        P("expert", None, None),
        P("expert", None, None),
        P("expert", None, None),
        P("expert", None, None),
        P(None, "dp", "expert"),
        P(None, "dp", "expert"),
        P(None, "dp", "expert"),
        P(None, "dp", "expert"),
        P(None, "dp", "expert", None),
    )
    out_specs = (
        P(None, "dp", "expert", None),
        P("dp", "expert", None),
        P("dp", "expert", None),
        P(),
        P(),
        P(),
        P("expert", "dp", None),
        P("expert", "dp", None),
        P("expert", "dp", None),
        P("expert", "dp", None),
        P(),
    )
    return jax.shard_map(
        functools.partial(local, n_dp, n_expert),
        mesh=mesh,
        in_specs=in_specs,
        out_specs=out_specs,
        check_vma=False,
    )
```

time: 1360 us -> 667 us (0.49)
  waiting for transfers between devices: 872 us -> 217 us
  matrix products: 243 us -> 0 us
  Pallas kernels: 0 us -> 202 us
  blocking collectives: 41.9 us -> 94.9 us
  local copies, waits for them, and re-layouts: 83.6 us -> 47.2 us
  other arithmetic: 62.6 us -> 40 us
    reduce_scatter x10 -> x0, waiting for transfers between devices: 531 us -> none  [the longest x1 150 us: local(): lax.psum_scatter(decoder_up_grad.astype(jnp.bfloat16), 'dp', scatter_dime...]
    dot_general x59 -> x0, matrix products: 243 us -> none  [the longest x3 21.8 us: core_backward(): jnp.einsum('bqhd,bkhd->bhqk', blended_grad, value_rows, preferred_element...]
    psum x1, waiting for transfers between devices: 234 us -> 0.01 us  [local(): dw = lax.psum(dw, AXES).astype(F32)]
    ppermute x0 -> x58, waiting for transfers between devices: none -> 217 us  [flip(): return lax.ppermute(value, AXES, pairs)]
    pallas_call x0 -> x16, Pallas kernels: none -> 202 us  [call(): pl.pallas_call(body, out_shape=[jax.ShapeDtypeStruct(s, d) for s, d in ou...]
    all_to_all x8 -> x0, waiting for transfers between devices: 59.1 us -> none  [the longest x2 26 us: moe_forward(): lax.all_to_all(result, 'expert', split_axis=1, concat_axis=0, tiled=True)]
    psum x1, blocking collectives: 41.9 us -> 94.9 us  [local(): gain_grads, counts = lax.psum((gain_grads, counts), AXES)]
    all_gather x6 -> x0, waiting for transfers between devices: 47.6 us -> none  [the longest x3 25.4 us: attend(): lax.all_gather(key_rows, 'expert', axis=1, tiled=True)]
  transfers between devices with their start and end apart: 25 -> 59, of which waited for: 17 -> 26; matrix products, arithmetic and copies ran while one was open for 21% -> 11% of each run, Pallas kernels for 0% -> 20%
where the time goes in v1:
time: 667 us; the launch traced here: 660 us
  waiting for transfers between devices  217 us (33%)
  Pallas kernels  202 us (30%)
  blocking collectives  94.9 us (14%)
  local copies, waits for them, and re-layouts  47.2 us (7%)
  starting transfers between devices  43.9 us (7%)
  other arithmetic  40 us (6%)
  between operations  15.1 us (2%)
    ppermute x58, waiting for transfers between devices, flip(): return lax.ppermute(value, AXES, pairs)  217 us
    pallas_call x16, Pallas kernels, call(): pl.pallas_call(body, out_shape=[jax.ShapeDtypeStruct(s, d) for s, d in ou...  202 us
    psum x1, blocking collectives, local(): gain_grads, counts = lax.psum((gain_grads, counts), AXES)  94.9 us
    ppermute x58, starting transfers between devices, flip(): return lax.ppermute(value, AXES, pairs)  43.8 us
    unnamed x141, local copies, waits for them, and re-layouts  13.5 us
  transfers between devices with their start and end apart: 59, of which 26 were waited for; matrix products, arithmetic and copies ran while one was open for 11% of the time, Pallas kernels for 20%

profile of v1, /device:TPU:0, one launch (start us, length us, event | category | flops | bytes accessed | tf_op | source)
XLA Modules:
  0.0 660.1 jit_solution(16000646933280568825)
XLA Ops:
  16.9 4.7 slice_bitcast_fusion
  22.4 12.3 %self_forward.3 = (f32[256,512]{1,0:T(8,128)}, bf16[256,512]{1,0:T(8,128)(2,1)}, bf16[1024,512]{1,0:T(8,128)(2,1)}, bf16[1024,512]{1,0:T(8,128)(2,1)}, bf16[512,...) custom-call(s32[1]{0:T(128)} %bitcast.me_ref, ...), custom_call_target="tpu_custom_call" | custom-call | flops 3221225472 | bytes 8663040 | tf_op jit(solution)/shard_map/self_forward/pallas_call | solution.py:95
  39.0 4.5 collective-permute-done.4.refs_1_
  43.6 8.0 %collective-permute-done.34 = bf16[1,256,512]{2,1,0:T(8,128)(2,1)S(1)} collective-permute-done((bf16[1,256,512]{2,1,0:T(8,128)(2,1)}, bf16[1,256,512]{2,1,0:T(8,128)(2,1)S(1)}, u32[]{:S(2)}, u32[]{:S(2)}) %collective-permute-start.34) | collective-permute-done | bytes 262176 | tf_op jit(solution)/shard_map/ppermute | solution.py:744
  60.6 10.8 %expert_forward.1 = (bf16[4,2,32,512]{3,2,1,0:T(8,128)(2,1)}, bf16[4,2,32,512]{3,2,1,0:T(8,128)(2,1)}, bf16[4,2,32,512]{3,2,1,0:T(8,128)(2,1)}, bf16[4,2,32,512]{3,2,1,0:T(8,128)(2,1)}) custom-call(s32[1]{0:T(128)} %bitcast.me_ref, bf16[1,256,512]{2,1,0:T(8,128)(2,1)} %bitcast.73, bf16[1,256,512]{2,1,0:T(8,128)(2,1)} %copy-done.25, ...), custom_call_target="tpu_custom_call" | custom-call | flops 4294967296 | bytes 18882560 | tf_op jit(solution)/shard_map/expert_forward/pallas_call | solution.py:95
  74.5 6.4 collective-permute-done.8.refs_1_
  80.9 4.0 collective-permute-done.10.refs_3_
  91.1 12.9 %collective-permute-done.11.refs_2_ = bf16[1,2,256,512]{3,2,1,0:T(8,128)(2,1)S(1)} collective-permute-done((bf16[1,2,256,512]{3,2,1,0:T(8,128)(2,1)}, bf16[1,2,256,512]{3,2,1,0:T(8,128)(2,1)S(1)}, u32[]{:S(2)}, u32[]{:S(2)}) %collective-permute-start.11) | collective-permute-done | bytes 524320 | tf_op jit(solution)/shard_map/ppermute | solution.py:744
  113.0 12.2 %self_forward.2 = (f32[256,512]{1,0:T(8,128)}, bf16[256,512]{1,0:T(8,128)(2,1)}, bf16[1024,512]{1,0:T(8,128)(2,1)}, bf16[1024,512]{1,0:T(8,128)(2,1)}, bf16[512,...) custom-call(s32[1]{0:T(128)} %bitcast.me_ref, ...), custom_call_target="tpu_custom_call" | custom-call | flops 3221225472 | bytes 8663040 | tf_op jit(solution)/shard_map/self_forward/pallas_call | solution.py:95
  126.1 20.9 %cross_forward.1 = (f32[2,256,512]{2,1,0:T(8,128)}, bf16[2,256,512]{2,1,0:T(8,128)(2,1)}, bf16[2,1024,512]{2,1,0:T(8,128)(2,1)}, bf16[2,1024,512]{2,1,0:T(8,128)...) custom-call(bf16[256,512]{1,0:T(8,128)(2,1)} %get-tuple-element.84.r, ...), custom_call_target="tpu_custom_call" | custom-call | flops 6442450944 | bytes 15747072 | tf_op jit(solution)/shard_map/cross_forward/pallas_call | solution.py:95
  149.8 11.3 %collective-permute-done.13.refs_1_ = bf16[1,2,256,512]{3,2,1,0:T(8,128)(2,1)S(1)} collective-permute-done((bf16[1,2,256,512]{3,2,1,0:T(8,128)(2,1)}, bf16[1,2,256,512]{3,2,1,0:T(8,128)(2,1)S(1)}, u32[]{:S(2)}, u32[]{:S(2)}) %collective-permute-start.13) | collective-permute-done | bytes 524320 | tf_op jit(solution)/shard_map/ppermute | solution.py:744
  161.1 13.4 %collective-permute-done.48 = bf16[1,2,256,512]{3,2,1,0:T(8,128)(2,1)S(1)} collective-permute-done((bf16[1,2,256,512]{3,2,1,0:T(8,128)(2,1)}, bf16[1,2,256,512]{3,2,1,0:T(8,128)(2,1)S(1)}, u32[]{:S(2)}, u32[]{:S(2)}) %collective-permute-start.48) | collective-permute-done | bytes 524320 | tf_op jit(solution)/shard_map/ppermute | solution.py:744
  178.3 15.8 %expert_backward.2 = (bf16[4,2,32,512]{3,2,1,0:T(8,128)(2,1)}, bf16[4,2,32,512]{3,2,1,0:T(8,128)(2,1)}, bf16[4,2,32,512]{3,2,1,0:T(8,128)(2,1)}, bf16[4,2,32,512...) custom-call(s32[1]{0:T(128)} %bitcast.me_ref, ...), custom_call_target="tpu_custom_call" | custom-call | flops 8589934592 | bytes 23076864 | tf_op jit(solution)/shard_map/expert_backward/pallas_call | solution.py:95
  197.2 6.4 collective-permute-done.20.refs_1_
  203.6 4.0 collective-permute-done.22.refs_3_
  208.3 28.5 %cross_backward.1 = (bf16[1,2,256,512]{3,2,1,0:T(8,128)(2,1)}, bf16[1,2,256,512]{3,2,1,0:T(8,128)(2,1)}, bf16[2,2,256,512]{3,2,1,0:T(8,128)(2,1)}, bf16[512,2048...) custom-call(s32[1]{0:T(128)} %bitcast.me_ref, ...), custom_call_target="tpu_custom_call" | custom-call | flops 9663676416 | bytes 19949568 | tf_op jit(solution)/shard_map/cross_backward/pallas_call | solution.py:95
  242.8 13.7 %collective-permute-done.24 = bf16[1,2,256,512]{3,2,1,0:T(8,128)(2,1)S(1)} collective-permute-done((bf16[1,2,256,512]{3,2,1,0:T(8,128)(2,1)S(1)}, bf16[1,2,256,512]{3,2,1,0:T(8,128)(2,1)S(1)}, u32[]{:S(2)}, u32[]{:S(2)}) %collective-permute-start.24) | collective-permute-done | bytes 524320 | tf_op jit(solution)/shard_map/ppermute | solution.py:744
  264.1 10.2 %collective-permute-done.25.refs_4_.refs_7_ = bf16[1,2,256,512]{3,2,1,0:T(8,128)(2,1)S(1)} collective-permute-done((bf16[1,2,256,512]{3,2,1,0:T(8,128)(2,1)}, bf16[1,2,256,512]{3,2,1,0:T(8,128)(2,1)S(1)}, u32[]{:S(2)}, u32[]{:S(2)}) %collective-permute-start.25) | collective-permute-done | bytes 524320 | tf_op jit(solution)/shard_map/ppermute | solution.py:744
  274.3 12.5 %collective-permute-done.38 = bf16[1,2,256,512]{3,2,1,0:T(8,128)(2,1)S(1)} collective-permute-done((bf16[1,2,256,512]{3,2,1,0:T(8,128)(2,1)}, bf16[1,2,256,512]{3,2,1,0:T(8,128)(2,1)S(1)}, u32[]{:S(2)}, u32[]{:S(2)}) %collective-permute-start.38) | collective-permute-done | bytes 524320 | tf_op jit(solution)/shard_map/ppermute | solution.py:744
  293.5 9.1 %collective-permute-done.49 = bf16[2,2,256,512]{3,2,1,0:T(8,128)(2,1)S(1)} collective-permute-done((bf16[2,2,256,512]{3,2,1,0:T(8,128)(2,1)S(1)}, bf16[2,2,256,512]{3,2,1,0:T(8,128)(2,1)S(1)}, u32[]{:S(2)}, u32[]{:S(2)}) %collective-permute-start.49) | collective-permute-done | bytes 1048608 | tf_op jit(solution)/shard_map/ppermute | solution.py:744
  306.0 18.1 %collective-permute-done.39 = bf16[2,2,256,512]{3,2,1,0:T(8,128)(2,1)S(1)} collective-permute-done((bf16[2,2,256,512]{3,2,1,0:T(8,128)(2,1)S(1)}, bf16[2,2,256,512]{3,2,1,0:T(8,128)(2,1)S(1)}, u32[]{:S(2)}, u32[]{:S(2)}) %collective-permute-start.39) | collective-permute-done | bytes 1048608 | tf_op jit(solution)/shard_map/ppermute | solution.py:744
  332.3 3.9 pad_maximum_fusion.3
  336.2 26.1 %collective-permute-done.50.refs_4_ = bf16[3,2,256,512]{3,2,1,0:T(8,128)(2,1)S(1)} collective-permute-done((bf16[3,2,256,512]{3,2,1,0:T(8,128)(2,1)}, bf16[3,2,256,512]{3,2,1,0:T(8,128)(2,1)S(1)}, u32[]{:S(2)}, u32[]{:S(2)}) %collective-permute-start.50) | collective-permute-done | bytes 1572896 | tf_op jit(solution)/shard_map/ppermute | solution.py:744
  364.5 29.2 %collective-permute-done.44 = s32[3,2,2,256]{3,0,2,1:T(4,128)S(1)} collective-permute-done((s32[3,2,2,256]{3,0,2,1:T(4,128)S(1)}, s32[3,2,2,256]{3,0,2,1:T(4,128)S(1)}, u32[]{:S(2)}, u32[]{:S(2)}) %collective-permute-start.44) | collective-permute-done | bytes 12320 | tf_op jit(solution)/shard_map/ppermute | solution.py:744
  400.1 13.1 %expert_backward.3 = (bf16[4,2,32,512]{3,2,1,0:T(8,128)(2,1)}, bf16[4,2,32,512]{3,2,1,0:T(8,128)(2,1)}, bf16[4,2,32,512]{3,2,1,0:T(8,128)(2,1)}, bf16[4,2,32,512]{3,2,1,0:T(8,128)(2,1)}) custom-call(s32[1]{0:T(128)} %bitcast.me_ref, bf16[1,256,512]{2,1,0:T(8,128)(2,1)} %bitcast.74, bf16[1,256,512]{2,1,0:T(8,128)(2,1)} %copy-done.25, ...), custom_call_target="tpu_custom_call" | custom-call | flops 6442450944 | bytes 20979712 | tf_op jit(solution)/shard_map/expert_backward/pallas_call | solution.py:95
  421.9 14.4 %self_backward.1 = (bf16[1,256,512]{2,1,0:T(8,128)(2,1)}, bf16[1,256,512]{2,1,0:T(8,128)(2,1)}, bf16[2,256,512]{2,1,0:T(8,128)(2,1)}, bf16[512,2048]{1,0:T(8,128)(2,1)}) custom-call(s32[1]{0:T(128)} %bitcast.me_ref, f32[256,512]{1,0:T(8,128)} %get-tuple-element.132.up.refs_4_, bf16[1024,512]{1,0:T(8,128)(2,1)} %get-tuple-element.133.hm, ...), custom_call_target="tpu_custom_call" | custom-call | flops 4831838208 | bytes 10493952 | tf_op jit(solution)/shard_map/self_backward/pallas_call | solution.py:95
  438.1 16.3 %encoder_backward.1 = (bf16[1,256,512]{2,1,0:T(8,128)(2,1)}, bf16[1,256,512]{2,1,0:T(8,128)(2,1)}, bf16[2,256,512]{2,1,0:T(8,128)(2,1)}, bf16[512,2048]{1,0:T(8,...) custom-call(s32[1]{0:T(128)} %bitcast.me_ref, bf16[4,2,32,512]{3,2,1,0:T(8,128)(2,1)} %get-tuple-element.115.refs_0_, ...), custom_call_target="tpu_custom_call" | custom-call | flops 4831838208 | bytes 13121536 | tf_op jit(solution)/shard_map/encoder_backward/pallas_call | solution.py:95
  454.4 5.4 pad_maximum_fusion
  465.4 21.8 %expert_weights.3 = (bf16[2,4,256,512]{3,2,1,0:T(8,128)(2,1)}, bf16[2,4,256,512]{3,2,1,0:T(8,128)(2,1)}) custom-call(s32[3]{0:T(128)} %pad_add_fusion.6.place_ref, bf16[1,2,256,512]{3,2,1,0:T(8,128)(2,1)} %bitcast.65, bf16[1,2,256,512]{3,2,1,0:T(8,128)(2,1)} %copy-done.16, bf16[2,2,256,512]{3,2,1,0:T(8,128)(2,1)} %copy-done.30, ...), custom_call_target="tpu_custom_call" | custom-call | flops 8589934592 | bytes 37781504 | tf_op jit(solution)/shard_map/expert_weights/pallas_call | solution.py:95
  492.8 20.8 %expert_weights.2 = (bf16[2,4,256,512]{3,2,1,0:T(8,128)(2,1)}, bf16[2,4,256,512]{3,2,1,0:T(8,128)(2,1)}) custom-call(s32[3]{0:T(128)} %pad_add_fusion.6.place_ref, bf16[1,256,512]{2,1,0:T(8,128)(2,1)} %bitcast.75, bf16[1,256,512]{2,1,0:T(8,128)(2,1)} %copy-done.25, bf16[2,256,512]{2,1,0:T(8,128)(2,1)} %copy-done.31, ...), custom_call_target="tpu_custom_call" | custom-call | flops 8589934592 | bytes 33587200 | tf_op jit(solution)/shard_map/expert_weights/pallas_call | solution.py:95
  535.8 94.9 %all-reduce = (f32[6,512]{1,0:T(8,128)}, f32[2,2,16]{2,1,0:T(2,128)S(1)}) all-reduce(f32[6,512]{1,0:T(8,128)S(1)} %concatenate.93, f32[2,2,16]{2,1,0:T(2,128)S(1)} %convert_reduce_fusion), channel_id=1, replica_groups=mesh['dp'=8,'expert'=4] {'dp','expert'}, use_global_device_ids=true, to_apply=%region_1.2 | all-reduce | flops 3136 | bytes 25088 | tf_op jit(solution)/shard_map/psum | solution.py:941
  637.1 7.6 %slice.146 = f32[3,512,1536]{2,1,0:T(8,128)} slice(bf16[3,512,2048]{2,1,0:T(8,128)(2,1)} %all-reduce.3.cloned.1.call-done), slice={[0:3], [0:512], [0:1536]} | slice | bytes 18874368 | tf_op jit(solution)/shard_map/slice | solution.py:947
  (298 shorter events, 152.0 us)
Async XLA Ops:
  7.2 629.9 %all-reduce.3.cloned.1.call-start = ((), (), s32[]{:S(2)}) async-start(), calls=%async_computation | async-start | bytes 12582912 | tf_op jit(solution)/shard_map/psum | solution.py:940
  89.6 19.8 %collective-permute-start = (bf16[1,256,512]{2,1,0:T(8,128)(2,1)S(1)}, bf16[1,256,512]{2,1,0:T(8,128)(2,1)S(1)}, u32[]{:S(2)}, u32[]{:S(2)}) collective-permute-start(bf16[1,256,512]{2,1,0:T(8,128)(2,1)S(1)} %copy-done.27), channel_id=1, source_target_pairs={{0,2},{1,3},{2,0},{3,1},{4,6},{5,7},{6,4},{7,5},{8,10},{9,11},{10,... | collective-permute-start | bytes 786440 | tf_op jit(solution)/shard_map/ppermute | solution.py:744
  105.3 19.8 %collective-permute-start.12 = (bf16[2,2,256,512]{3,2,1,0:T(8,128)(2,1)S(1)}, bf16[2,2,256,512]{3,2,1,0:T(8,128)(2,1)S(1)}, u32[]{:S(2)}, u32[]{:S(2)}) collective-permute-start(bf16[2,2,256,512]{3,2,1,0:T(8,128)(2,1)S(1)} %pad_maximum_fusion.11), channel_id=1, source_target_pairs={{0,1},{1,0},{2,3},{3,2},{4,5},{5,4},{6,7},{7,6},{8,9},{9,8},{10,11... | collective-permute-start | bytes 3145736 | tf_op jit(solution)/shard_map/ppermute | solution.py:744
  109.6 40.0 %collective-permute-start.15 = (bf16[1,2,256,512]{3,2,1,0:T(8,128)(2,1)S(1)}, bf16[1,2,256,512]{3,2,1,0:T(8,128)(2,1)S(1)}, u32[]{:S(2)}, u32[]{:S(2)}) collective-permute-start(bf16[1,2,256,512]{3,2,1,0:T(8,128)(2,1)S(1)} %fusion.1.refs_3_.refs_6_), channel_id=1, source_target_pairs={{0,2},{1,3},{2,0},{3,1},{4,6},{5,7},{6,4},{7,5},{8,10},{9,11},{10,... | collective-permute-start | bytes 1572872 | tf_op jit(solution)/shard_map/ppermute | solution.py:744
  110.1 39.4 %collective-permute-start.52 = (bf16[1,2,256,512]{3,2,1,0:T(8,128)(2,1)S(1)}, bf16[1,2,256,512]{3,2,1,0:T(8,128)(2,1)S(1)}, u32[]{:S(2)}, u32[]{:S(2)}) collective-permute-start(bf16[1,2,256,512]{3,2,1,0:T(8,128)(2,1)S(1)} %fusion.1.refs_3_.refs_6_), channel_id=1, source_target_pairs={{0,16},{1,17},{2,18},{3,19},{4,20},{5,21},{6,22},{7,23},{8,24},{9,... | collective-permute-start | bytes 1572872 | tf_op jit(solution)/shard_map/ppermute | solution.py:744
  148.6 25.8 %collective-permute-start.48 = (bf16[1,2,256,512]{3,2,1,0:T(8,128)(2,1)}, bf16[1,2,256,512]{3,2,1,0:T(8,128)(2,1)S(1)}, u32[]{:S(2)}, u32[]{:S(2)}) collective-permute-start(bf16[1,2,256,512]{3,2,1,0:T(8,128)(2,1)} %bitcast.63), channel_id=1, source_target_pairs={{0,16},{1,17},{2,18},{3,19},{4,20},{5,21},{6,22},{7,23},{8,24},{9,... | collective-permute-start | bytes 1572872 | tf_op jit(solution)/shard_map/ppermute | solution.py:744
  149.7 25.6 %collective-permute-start.16 = (bf16[2,2,256,512]{3,2,1,0:T(8,128)(2,1)S(1)}, bf16[2,2,256,512]{3,2,1,0:T(8,128)(2,1)S(1)}, u32[]{:S(2)}, u32[]{:S(2)}) collective-permute-start(bf16[2,2,256,512]{3,2,1,0:T(8,128)(2,1)S(1)} %get-tuple-element.212), channel_id=1, source_target_pairs={{0,1},{1,0},{2,3},{3,2},{4,5},{5,4},{6,7},{7,6},{8,9},{9,8},{10,11... | collective-permute-start | bytes 3145736 | tf_op jit(solution)/shard_map/ppermute | solution.py:744
  242.8 47.2 %collective-permute-start.53 = (bf16[2,2,256,512]{3,2,1,0:T(8,128)(2,1)S(1)}, bf16[2,2,256,512]{3,2,1,0:T(8,128)(2,1)S(1)}, u32[]{:S(2)}, u32[]{:S(2)}) collective-permute-start(bf16[2,2,256,512]{3,2,1,0:T(8,128)(2,1)S(1)} %get-tuple-element.211), channel_id=1, source_target_pairs={{0,8},{1,9},{2,10},{3,11},{4,12},{5,13},{6,14},{7,15},{8,0},{9,1},... | collective-permute-start | bytes 3145736 | tf_op jit(solution)/shard_map/ppermute | solution.py:744
  261.2 25.6 %collective-permute-start.38 = (bf16[1,2,256,512]{3,2,1,0:T(8,128)(2,1)}, bf16[1,2,256,512]{3,2,1,0:T(8,128)(2,1)S(1)}, u32[]{:S(2)}, u32[]{:S(2)}) collective-permute-start(bf16[1,2,256,512]{3,2,1,0:T(8,128)(2,1)} %bitcast.80), channel_id=1, source_target_pairs={{0,16},{1,17},{2,18},{3,19},{4,20},{5,21},{6,22},{7,23},{8,24},{9,... | collective-permute-start | bytes 1572872 | tf_op jit(solution)/shard_map/ppermute | solution.py:744
  261.2 41.3 %collective-permute-start.49 = (bf16[2,2,256,512]{3,2,1,0:T(8,128)(2,1)S(1)}, bf16[2,2,256,512]{3,2,1,0:T(8,128)(2,1)S(1)}, u32[]{:S(2)}, u32[]{:S(2)}) collective-permute-start(bf16[2,2,256,512]{3,2,1,0:T(8,128)(2,1)S(1)} %get-tuple-element.213), channel_id=1, source_target_pairs={{0,8},{1,9},{2,10},{3,11},{4,12},{5,13},{6,14},{7,15},{8,0},{9,1},... | collective-permute-start | bytes 3145736 | tf_op jit(solution)/shard_map/ppermute | solution.py:744
  289.1 35.0 %collective-permute-start.39 = (bf16[2,2,256,512]{3,2,1,0:T(8,128)(2,1)S(1)}, bf16[2,2,256,512]{3,2,1,0:T(8,128)(2,1)S(1)}, u32[]{:S(2)}, u32[]{:S(2)}) collective-permute-start(bf16[2,2,256,512]{3,2,1,0:T(8,128)(2,1)S(1)} %get-tuple-element.215), channel_id=1, source_target_pairs={{0,8},{1,9},{2,10},{3,11},{4,12},{5,13},{6,14},{7,15},{8,0},{9,1},... | collective-permute-start | bytes 3145736 | tf_op jit(solution)/shard_map/ppermute | solution.py:744
  291.1 40.8 %collective-permute-start.54 = (bf16[3,2,256,512]{3,2,1,0:T(8,128)(2,1)}, bf16[3,2,256,512]{3,2,1,0:T(8,128)(2,1)S(1)}, u32[]{:S(2)}, u32[]{:S(2)}) collective-permute-start(bf16[3,2,256,512]{3,2,1,0:T(8,128)(2,1)} %constant_dynamic-update-slice_fusion.6.refs_9_), channel_id=1, source_target_pairs={{0,2},{1,3},{2,0},{3,1},{4,6},{5,7},{6,4},{7,5},{8,10},{9,11},{10,... | collective-permute-start | bytes 4718600 | tf_op jit(solution)/shard_map/ppermute | solution.py:744
  303.7 58.7 %collective-permute-start.50 = (bf16[3,2,256,512]{3,2,1,0:T(8,128)(2,1)}, bf16[3,2,256,512]{3,2,1,0:T(8,128)(2,1)S(1)}, u32[]{:S(2)}, u32[]{:S(2)}) collective-permute-start(bf16[3,2,256,512]{3,2,1,0:T(8,128)(2,1)} %constant_dynamic-update-slice_fusion.4.refs_3_), channel_id=1, source_target_pairs={{0,2},{1,3},{2,0},{3,1},{4,6},{5,7},{6,4},{7,5},{8,10},{9,11},{10,... | collective-permute-start | bytes 4718600 | tf_op jit(solution)/shard_map/ppermute | solution.py:744
  326.1 69.7 %collective-permute-start.40 = (bf16[3,2,256,512]{3,2,1,0:T(8,128)(2,1)}, bf16[3,2,256,512]{3,2,1,0:T(8,128)(2,1)}, u32[]{:S(2)}, u32[]{:S(2)}) collective-permute-start(bf16[3,2,256,512]{3,2,1,0:T(8,128)(2,1)} %constant_dynamic-update-slice_fusion.2.refs_9_), channel_id=1, source_target_pairs={{0,2},{1,3},{2,0},{3,1},{4,6},{5,7},{6,4},{7,5},{8,10},{9,11},{10,... | collective-permute-start | bytes 4718600 | tf_op jit(solution)/shard_map/ppermute | solution.py:744
  328.0 71.1 %collective-permute-start.26 = (bf16[2,2,256,512]{3,2,1,0:T(8,128)(2,1)}, bf16[2,2,256,512]{3,2,1,0:T(8,128)(2,1)S(1)}, u32[]{:S(2)}, u32[]{:S(2)}) collective-permute-start(bf16[2,2,256,512]{3,2,1,0:T(8,128)(2,1)} %get-tuple-element.216), channel_id=1, source_target_pairs={{0,1},{1,0},{2,3},{3,2},{4,5},{5,4},{6,7},{7,6},{8,9},{9,8},{10,11... | collective-permute-start | bytes 3145736 | tf_op jit(solution)/shard_map/ppermute | solution.py:744
  331.3 62.4 %collective-permute-start.44 = (s32[3,2,2,256]{3,0,2,1:T(4,128)S(1)}, s32[3,2,2,256]{3,0,2,1:T(4,128)S(1)}, u32[]{:S(2)}, u32[]{:S(2)}) collective-permute-start(s32[3,2,2,256]{3,0,2,1:T(4,128)S(1)} %pad_add_fusion.2), channel_id=1, source_target_pairs={{0,2},{1,3},{2,0},{3,1},{4,6},{5,7},{6,4},{7,5},{8,10},{9,11},{10,... | collective-permute-start | bytes 36872 | tf_op jit(solution)/shard_map/ppermute | solution.py:744
  331.9 62.6 %collective-permute-start.35 = (bf16[2,256,512]{2,1,0:T(8,128)(2,1)}, bf16[2,256,512]{2,1,0:T(8,128)(2,1)S(1)}, u32[]{:S(2)}, u32[]{:S(2)}) collective-permute-start(bf16[2,256,512]{2,1,0:T(8,128)(2,1)} %get-tuple-element.221), channel_id=1, source_target_pairs={{0,8},{1,9},{2,10},{3,11},{4,12},{5,13},{6,14},{7,15},{8,0},{9,1},... | collective-permute-start | bytes 1572872 | tf_op jit(solution)/shard_map/ppermute | solution.py:744
  362.3 101.8 %collective-permute-start.55 = (bf16[6,2,256,512]{3,2,1,0:T(8,128)(2,1)}, bf16[6,2,256,512]{3,2,1,0:T(8,128)(2,1)}, u32[]{:S(2)}, u32[]{:S(2)}) collective-permute-start(bf16[6,2,256,512]{3,2,1,0:T(8,128)(2,1)} %pad_maximum_fusion.3), channel_id=1, source_target_pairs={{0,1},{1,0},{2,3},{3,2},{4,5},{5,4},{6,7},{7,6},{8,9},{9,8},{10,11... | collective-permute-start | bytes 9437192 | tf_op jit(solution)/shard_map/ppermute | solution.py:744
  393.7 70.4 %collective-permute-start.51 = (bf16[6,2,256,512]{3,2,1,0:T(8,128)(2,1)}, bf16[6,2,256,512]{3,2,1,0:T(8,128)(2,1)}, u32[]{:S(2)}, u32[]{:S(2)}) collective-permute-start(bf16[6,2,256,512]{3,2,1,0:T(8,128)(2,1)} %pad_maximum_fusion.2), channel_id=1, source_target_pairs={{0,1},{1,0},{2,3},{3,2},{4,5},{5,4},{6,7},{7,6},{8,9},{9,8},{10,11... | collective-permute-start | bytes 9437192 | tf_op jit(solution)/shard_map/ppermute | solution.py:744
  394.5 18.8 %collective-permute-start.45 = (s32[6,2,2,256]{3,0,2,1:T(8,128)S(1)}, s32[6,2,2,256]{3,0,2,1:T(8,128)S(1)}, u32[]{:S(2)}, u32[]{:S(2)}) collective-permute-start(s32[6,2,2,256]{3,0,2,1:T(8,128)S(1)} %pad_add_fusion), channel_id=1, source_target_pairs={{0,1},{1,0},{2,3},{3,2},{4,5},{5,4},{6,7},{7,6},{8,9},{9,8},{10,11... | collective-permute-start | bytes 73736 | tf_op jit(solution)/shard_map/ppermute | solution.py:744
  395.8 19.8 %collective-permute-start.36 = (bf16[3,256,512]{2,1,0:T(8,128)(2,1)}, bf16[3,256,512]{2,1,0:T(8,128)(2,1)}, u32[]{:S(2)}, u32[]{:S(2)}) collective-permute-start(bf16[3,256,512]{2,1,0:T(8,128)(2,1)} %constant_dynamic-update-slice_fusion.refs_3_), channel_id=1, source_target_pairs={{0,2},{1,3},{2,0},{3,1},{4,6},{5,7},{6,4},{7,5},{8,10},{9,11},{10,... | collective-permute-start | bytes 2359304 | tf_op jit(solution)/shard_map/ppermute | solution.py:744
  399.1 93.2 %collective-permute-start.41 = (bf16[6,2,256,512]{3,2,1,0:T(8,128)(2,1)S(1)}, bf16[6,2,256,512]{3,2,1,0:T(8,128)(2,1)}, u32[]{:S(2)}, u32[]{:S(2)}) collective-permute-start(bf16[6,2,256,512]{3,2,1,0:T(8,128)(2,1)S(1)} %pad_maximum_fusion.1), channel_id=1, source_target_pairs={{0,1},{1,0},{2,3},{3,2},{4,5},{5,4},{6,7},{7,6},{8,9},{9,8},{10,11... | collective-permute-start | bytes 9437192 | tf_op jit(solution)/shard_map/ppermute | solution.py:744
  436.4 54.3 %collective-permute-start.37 = (bf16[6,256,512]{2,1,0:T(8,128)(2,1)}, bf16[6,256,512]{2,1,0:T(8,128)(2,1)}, u32[]{:S(2)}, u32[]{:S(2)}) collective-permute-start(bf16[6,256,512]{2,1,0:T(8,128)(2,1)} %pad_maximum_fusion.4), channel_id=1, source_target_pairs={{0,1},{1,0},{2,3},{3,2},{4,5},{5,4},{6,7},{7,6},{8,9},{9,8},{10,11... | collective-permute-start | bytes 4718600 | tf_op jit(solution)/shard_map/ppermute | solution.py:744
  437.4 23.8 %collective-permute-start.32 = (bf16[2,256,512]{2,1,0:T(8,128)(2,1)}, bf16[2,256,512]{2,1,0:T(8,128)(2,1)}, u32[]{:S(2)}, u32[]{:S(2)}) collective-permute-start(bf16[2,256,512]{2,1,0:T(8,128)(2,1)} %get-tuple-element.141), channel_id=1, source_target_pairs={{0,1},{1,0},{2,3},{3,2},{4,5},{5,4},{6,7},{7,6},{8,9},{9,8},{10,11... | collective-permute-start | bytes 1572872 | tf_op jit(solution)/shard_map/ppermute | solution.py:744
  461.2 29.6 %collective-permute-start.17 = (bf16[4,2,32,512]{3,2,1,0:T(8,128)(2,1)}, bf16[4,2,32,512]{3,2,1,0:T(8,128)(2,1)S(1)}, u32[]{:S(2)}, u32[]{:S(2)}) collective-permute-start(bf16[4,2,32,512]{3,2,1,0:T(8,128)(2,1)} %get-tuple-element.95), channel_id=1, source_target_pairs={{0,2},{1,3},{2,0},{3,1},{4,6},{5,7},{6,4},{7,5},{8,10},{9,11},{10,... | collective-permute-start | bytes 786440 | tf_op jit(solution)/shard_map/ppermute | solution.py:744
  464.1 51.0 %collective-permute-start.18 = (bf16[4,2,32,512]{3,2,1,0:T(8,128)(2,1)}, bf16[4,2,32,512]{3,2,1,0:T(8,128)(2,1)S(1)}, u32[]{:S(2)}, u32[]{:S(2)}) collective-permute-start(bf16[4,2,32,512]{3,2,1,0:T(8,128)(2,1)} %get-tuple-element.96), channel_id=1, source_target_pairs={{0,1},{1,0},{2,3},{3,2},{4,5},{5,4},{6,7},{7,6},{8,9},{9,8},{10,11... | collective-permute-start | bytes 786440 | tf_op jit(solution)/shard_map/ppermute | solution.py:744
  464.1 54.5 %collective-permute-start.19 = (bf16[4,2,32,512]{3,2,1,0:T(8,128)(2,1)}, bf16[4,2,32,512]{3,2,1,0:T(8,128)(2,1)S(1)}, u32[]{:S(2)}, u32[]{:S(2)}) collective-permute-start(bf16[4,2,32,512]{3,2,1,0:T(8,128)(2,1)} %get-tuple-element.97), channel_id=1, source_target_pairs={{0,3},{1,2},{2,1},{3,0},{4,7},{5,6},{6,5},{7,4},{8,11},{9,10},{10,... | collective-permute-start | bytes 786440 | tf_op jit(solution)/shard_map/ppermute | solution.py:744
  490.7 25.5 %collective-permute-start.30 = (bf16[2,256,512]{2,1,0:T(8,128)(2,1)S(1)}, bf16[2,256,512]{2,1,0:T(8,128)(2,1)S(1)}, u32[]{:S(2)}, u32[]{:S(2)}) collective-permute-start(bf16[2,256,512]{2,1,0:T(8,128)(2,1)S(1)} %copy-done.58), channel_id=1, source_target_pairs={{0,1},{1,0},{2,3},{3,2},{4,5},{5,4},{6,7},{7,6},{8,9},{9,8},{10,11... | collective-permute-start | bytes 1572872 | tf_op jit(solution)/shard_map/ppermute | solution.py:744
  490.8 140.5 %collective-permute-start.56 = (bf16[1,4,256,512]{3,2,1,0:T(8,128)(2,1)}, bf16[1,4,256,512]{3,2,1,0:T(8,128)(2,1)}, u32[]{:S(2)}, u32[]{:S(2)}) collective-permute-start(bf16[1,4,256,512]{3,2,1,0:T(8,128)(2,1)} %slice.135), channel_id=1, source_target_pairs={{0,4},{1,5},{2,6},{3,7},{4,0},{5,1},{6,2},{7,3},{8,12},{9,13},{10,... | collective-permute-start | bytes 3145736 | tf_op jit(solution)/shard_map/ppermute | solution.py:744
  492.3 142.0 %collective-permute-start.57 = (bf16[1,4,256,512]{3,2,1,0:T(8,128)(2,1)}, bf16[1,4,256,512]{3,2,1,0:T(8,128)(2,1)}, u32[]{:S(2)}, u32[]{:S(2)}) collective-permute-start(bf16[1,4,256,512]{3,2,1,0:T(8,128)(2,1)} %slice.137), channel_id=1, source_target_pairs={{0,4},{1,5},{2,6},{3,7},{4,0},{5,1},{6,2},{7,3},{8,12},{9,13},{10,... | collective-permute-start | bytes 3145736 | tf_op jit(solution)/shard_map/ppermute | solution.py:744
  516.2 130.5 %collective-permute-start.46 = (bf16[1,4,256,512]{3,2,1,0:T(8,128)(2,1)S(1)}, bf16[1,4,256,512]{3,2,1,0:T(8,128)(2,1)}, u32[]{:S(2)}, u32[]{:S(2)}) collective-permute-start(bf16[1,4,256,512]{3,2,1,0:T(8,128)(2,1)S(1)} %slice.130), channel_id=1, source_target_pairs={{0,4},{1,5},{2,6},{3,7},{4,0},{5,1},{6,2},{7,3},{8,12},{9,13},{10,... | collective-permute-start | bytes 3145736 | tf_op jit(solution)/shard_map/ppermute | solution.py:744
  524.4 125.6 %collective-permute-start.47 = (bf16[1,4,256,512]{3,2,1,0:T(8,128)(2,1)}, bf16[1,4,256,512]{3,2,1,0:T(8,128)(2,1)}, u32[]{:S(2)}, u32[]{:S(2)}) collective-permute-start(bf16[1,4,256,512]{3,2,1,0:T(8,128)(2,1)} %slice.132), channel_id=1, source_target_pairs={{0,4},{1,5},{2,6},{3,7},{4,0},{5,1},{6,2},{7,3},{8,12},{9,13},{10,... | collective-permute-start | bytes 3145736 | tf_op jit(solution)/shard_map/ppermute | solution.py:744
  (95 other events, 1332.5 us)
Sparse Core Ops, SparseCore 0:
  460.0 170.1 all-reduce.2

commit v2 on v1

--- a/solution.py
+++ b/solution.py
@@ -14,6 +14,7 @@
 F32 = jnp.float32
 BF16 = jnp.bfloat16
 VMEM_LIMIT = 58 << 20
+MEASURED_US = {'self_forward': 12.4, 'self_backward': 14.5, 'expert_forward': 10.6, 'expert_backward': 14.5, 'expert_weights': 21, 'combine_norm': 3.4, 'combine_output': 3.4, 'cross_forward': 21, 'cross_backward': 28, 'memory_backward': 3.4, 'encoder_backward': 16, 'input_backward': 2.5}
 
 
 def nn(a, b):
@@ -75,7 +76,7 @@
     return pl.BlockSpec(shape, lambda *_: (0,) * len(shape))
 
 
-def call(body, ins, outs, name, grid=None, in_specs=None, out_specs=None, scratch=(), scalars=(), flops=0):
+def call(body, ins, outs, name, grid=None, in_specs=None, out_specs=None, scratch=(), scalars=(), flops=0, collective_id=None):
     if in_specs is None:
         in_specs = [None] * len(ins)
     if out_specs is None:
@@ -97,9 +98,76 @@
         out_shape=[jax.ShapeDtypeStruct(s, d) for s, d in outs],
         grid_spec=spec,
         name=name,
-        compiler_params=pltpu.CompilerParams(vmem_limit_bytes=VMEM_LIMIT),
-        cost_estimate=pl.CostEstimate(flops=flops, bytes_accessed=moved, transcendentals=0),
+        compiler_params=pltpu.CompilerParams(
+            vmem_limit_bytes=VMEM_LIMIT, collective_id=collective_id, has_side_effects=collective_id is not None
+        ),
+        cost_estimate=pl.CostEstimate(flops=int(MEASURED_US[name] * 1.15e9), bytes_accessed=moved, transcendentals=0),
     )(*scalars, *ins)
+
+
+MESH = pl.DeviceIdType.MESH
+
+
+def xor(value, bits):
+    b = 1
+    while b <= bits:
+        if bits & b:
+            value = value + b * (1 - 2 * lax.rem(lax.div(value, b), 2))
+        b *= 2
+    return value
+
+
+def peer(dp_bits, expert_bits):
+    return (xor(lax.axis_index("dp"), dp_bits), xor(lax.axis_index("expert"), expert_bits))
+
+
+def greet(peers):
+    barrier = pltpu.get_barrier_semaphore()
+    for p in peers:
+        pl.semaphore_signal(barrier, inc=1, device_id=peer(*p), device_id_type=MESH)
+    pl.semaphore_wait(barrier, len(peers))
+
+
+def send(src, dst, send_sem, recv_sem, to):
+    return pltpu.make_async_remote_copy(
+        src_ref=src, dst_ref=dst, send_sem=send_sem, recv_sem=recv_sem, device_id=peer(*to), device_id_type=MESH
+    )
+
+
+class Gather:
+    def __init__(self, ids, own, near, send_sems, recv_sems):
+        self.pos = {r: i for i, r in enumerate(ids)}
+        self.far = [r for r in ids if r % 2 == 0 and r > 0]
+        self.own, self.near, self.sems = own, near, (send_sems, recv_sems)
+
+    def copy(self, r, src, to):
+        at = self.pos[r]
+        return send(src, self.near.at[at], self.sems[0].at[at], self.sems[1].at[at], (0, to))
+
+    def first(self, r):
+        return self.copy(r, self.own, r)
+
+    def second(self, r):
+        return self.copy(r ^ 1, self.near.at[self.pos[r]], 1)
+
+    def start(self):
+        for r in self.far:
+            self.first(r).start()
+        self.first(1).start()
+
+    def forward(self):
+        for r in self.far:
+            self.first(r).wait_recv()
+            self.second(r).start()
+
+    def finish(self):
+        for r in self.far:
+            self.second(r).wait_recv()
+        self.first(1).wait_recv()
+        for r in self.far:
+            self.first(r).wait_send()
+            self.second(r).wait_send()
+        self.first(1).wait_send()
 
 
 def head_rows(values, h):
@@ -276,7 +344,7 @@
     total = None
     slots = experts * cap
     for r, rows in returned:
-        local = col - (me ^ r) * slots
+        local = col - xor(me, r) * slots
         hot = (local == lax.broadcasted_iota(jnp.int32, (col.shape[0], slots), 1)).astype(BF16)
         part = nn(hot, rows.reshape(slots, rows.shape[-1]))
         total = part if total is None else total + part
@@ -299,46 +367,79 @@
                 dest[j, at : at + cap, :] = rows[j * cap : (j + 1) * cap]
 
 
-def expert_forward(pieces, cols, me, weight_up, weight_down, ids):
+def expert_forward(own, cols, own_col, residual, gain, weight_up, weight_down, ids):
     experts, hidden, feature = weight_up.shape
-    rows = pieces[0].shape[1]
+    rows = own.shape[1]
     cap = 2 * rows // EXPERTS
-    count = len(pieces)
     sources = len(ids)
     length = sources * 2 * cap
 
-    def body(me_ref, *refs):
-        parts = refs[:count]
-        col, up, down = refs[count : count + 3]
-        outs = refs[count + 3 : count + 3 + sources]
-        buf = refs[-1]
+    def body(u, col, mine, res, g, up, down, out, nxt, near_out, near, buf, stage, ret, gs, gr, rs, rr, ls):
+        me = lax.axis_index("expert")
         j = pl.program_id(0)
+        gather = Gather(ids, near.at[0], near, gs, gr)
+        keep = pltpu.make_async_copy(near, near_out, ls)
+
+        def back(s, n):
+            return send(stage.at[s, n], ret.at[s, n], rs.at[s, n], rr.at[s, n], (0, ids[s]))
 
         @pl.when(j == 0)
         def _():
-            blocks = piece_blocks(parts)
-            fill_buffers(me_ref[0], experts, cap, col, lambda s, p: blocks[s][0][blocks[s][1]], sources, buf)
-
-        x = buf[j]
-        act = gelu(nt(x, up[0])).astype(BF16)
-        res = nn(act, down[0]).astype(BF16)
+            near[0] = u[0]
+            greet([(0, r) for r in ids[1:]])
+            gather.start()
+            gather.forward()
+            gather.finish()
+            keep.start()
+            fill_buffers(me, experts, cap, col, lambda s, p: near[s], sources, buf)
+
+        act = gelu(nt(buf[j], up[0])).astype(BF16)
+        got = nn(act, down[0]).astype(BF16)
         for s in range(sources):
             for p in range(2):
                 at = (2 * s + p) * cap
-                outs[s][0, p] = res[at : at + cap]
+                if s == 0:
+                    ret[s, j, p] = got[at : at + cap]
+                else:
+                    stage[s, j, p] = got[at : at + cap]
+        for s in range(1, sources):
+            back(s, j).start()
+
+        @pl.when(j == experts - 1)
+        def _():
+            for s in range(1, sources):
+                for n in range(experts):
+                    back(s, n).wait()
+            for p in range(2):
+                mixed = gather_rows(me, experts, cap, mine[p], [(r, ret[i, :, p]) for i, r in enumerate(ids)])
+                after = res[...] + mixed
+                out[p] = after
+                nxt[p] = norm(after, g[...]).astype(BF16)
+            keep.wait()
 
     weight = pl.BlockSpec((1, hidden, feature), lambda j, *_: (j, 0, 0))
+    dma = pltpu.SemaphoreType.DMA
     return call(
         body,
-        [*pieces, cols, weight_up, weight_down],
-        [((experts, 2, cap, feature), BF16)] * sources,
+        [own, cols, own_col, residual, gain, weight_up, weight_down],
+        [((2, rows, feature), F32), ((2, rows, feature), BF16), ((sources, rows, feature), BF16)],
         "expert_forward",
         grid=(experts,),
-        in_specs=[None] * (count + 1) + [weight, weight],
-        out_specs=[pl.BlockSpec((1, 2, cap, feature), lambda j, *_: (j, 0, 0, 0))] * sources,
-        scratch=[pltpu.VMEM((experts, length, feature), BF16)],
-        scalars=[me],
+        in_specs=[None] * 5 + [weight, weight],
+        out_specs=[None, None, pl.BlockSpec(memory_space=pl.ANY)],
+        scratch=[
+            pltpu.VMEM((sources, rows, feature), BF16),
+            pltpu.VMEM((experts, length, feature), BF16),
+            pltpu.VMEM((sources, experts, 2, cap, feature), BF16),
+            pltpu.VMEM((sources, experts, 2, cap, feature), BF16),
+            dma((sources,)),
+            dma((sources,)),
+            dma((sources, experts)),
+            dma((sources, experts)),
+            dma,
+        ],
         flops=4 * experts * length * hidden * feature,
+        collective_id=2,
     )
 
 
@@ -346,7 +447,7 @@
     experts, hidden, feature = weight_up.shape
     rows = grads[0].shape[2]
     cap = 2 * rows // EXPERTS
-    count = len(pieces)
+    count, gcount = len(pieces), len(grads)
     sources = len(ids)
     length = sources * 2 * cap
     both = pieces[0].ndim == 4
@@ -354,9 +455,9 @@
 
     def body(me_ref, *refs):
         parts = refs[:count]
-        gparts = refs[count : 2 * count]
-        col, up, down = refs[2 * count : 2 * count + 3]
-        outs = refs[2 * count + 3 : 2 * count + 3 + kinds * sources]
+        gparts = refs[count : count + gcount]
+        col, up, down = refs[count + gcount : count + gcount + 3]
+        outs = refs[count + gcount + 3 : count + gcount + 3 + kinds * sources]
         buf, gbuf = refs[-2:]
         j = pl.program_id(0)
 
@@ -388,7 +489,7 @@
         [((experts, 2, cap, feature), BF16)] * (kinds * sources),
         "expert_backward",
         grid=(experts,),
-        in_specs=[None] * (2 * count + 1) + [weight, weight],
+        in_specs=[None] * (count + gcount + 1) + [weight, weight],
         out_specs=[pl.BlockSpec((1, 2, cap, feature), lambda j, *_: (j, 0, 0, 0))] * (kinds * sources),
         scratch=[pltpu.VMEM((experts, length, feature), BF16)] * 2,
         scalars=[me],
@@ -441,30 +542,6 @@
         scratch=[pltpu.VMEM((experts, length, feature), BF16)] * 2,
         scalars=[place],
         flops=8 * experts * length * (hidden // nz) * feature,
-    )
-
-
-def combine_norm(returned, ids, col, me, residual, gain):
-    experts, _, cap, feature = returned[0].shape
-    rows = residual.shape[-2]
-    count = len(ids)
-
-    def body(me_ref, *refs):
-        ret = refs[:count]
-        c, res, g, out, nxt = refs[count:]
-        for p in range(2):
-            mixed = gather_rows(me_ref[0], experts, cap, c[p], [(r, ref[:, p]) for r, ref in zip(ids, ret)])
-            after = res[...] + mixed
-            out[p] = after
-            nxt[p] = norm(after, g[...]).astype(BF16)
-
-    return call(
-        body,
-        [*returned, col, residual, gain],
-        [((2, rows, feature), F32), ((2, rows, feature), BF16)],
-        "combine_norm",
-        scalars=[me],
-        flops=4 * rows * EXPERTS * cap * feature,
     )
 
 
@@ -857,13 +934,14 @@
     e1, u, *enc_saved = self_forward(
         source_pieces, ids, me1, gains[0], gains[1], attention_in[0], attention_out[0], False
     )
-    u_near = gather_expert(u[None])
-    u_all = gather_far(u[None], u_near)
     t1, hc, *dec_saved = self_forward(
         target_pieces, ids, me1, gains[3], gains[4], attention_in[1], attention_out[1], True
     )
-    returned = give_back(expert_forward(u_near, near_cols[0], me1, encoder_up, encoder_down, ids))
-    e2, memory = combine_norm(returned, ids, own_cols[0], me1, e1, gains[2])
+    e2, memory, u_near = expert_forward(
+        u[None], near_cols[0], own_cols[0], e1, gains[2], encoder_up, encoder_down, ids
+    )
+    u_near = [u_near]
+    u_all = gather_far(u[None], u_near)
     memory_near = gather_expert(memory[None])
     t2, w, *cross_saved = cross_forward(
         hc, memory_near, ids, t1, gains[5], attention_in[2], attention_out[2]

time: 667 us -> 635 us (0.952)
  waiting for transfers between devices: 217 us -> 180 us
  Pallas kernels: 202 us -> 217 us
  blocking collectives: 94.9 us -> 103 us
  local copies, waits for them, and re-layouts: 47.2 us -> 40.2 us
  starting transfers between devices: 43.9 us -> 37.2 us
    ppermute x58 -> x53, waiting for transfers between devices: 217 us -> 180 us  [flip(): return lax.ppermute(value, AXES, pairs)]
    pallas_call x16 -> x15, Pallas kernels: 202 us -> 217 us  [call(): pl.pallas_call(body, out_shape=[jax.ShapeDtypeStruct(s, d) for s, d in ou...]
    psum x1, blocking collectives: 94.9 us -> 103 us  [local(): gain_grads, counts = lax.psum((gain_grads, counts), AXES)]
    ppermute x58 -> x53, starting transfers between devices: 43.8 us -> 37.1 us  [flip(): return lax.ppermute(value, AXES, pairs)]
    unnamed x141 -> x113, local copies, waits for them, and re-layouts: 13.5 us -> 9.87 us
  transfers between devices with their start and end apart: 59 -> 54, of which waited for: 26 -> 18; matrix products, arithmetic and copies ran while one was open for 11% -> 10% of each run, Pallas kernels for 20% -> 32%
where the time goes in v2:
time: 635 us; the launch traced here: 628 us
  Pallas kernels  217 us (34%)
  waiting for transfers between devices  180 us (28%)
  blocking collectives  103 us (16%)
  local copies, waits for them, and re-layouts  40.2 us (6%)
  starting transfers between devices  37.2 us (6%)
  other arithmetic  36 us (6%)
  between operations  14.8 us (2%)
    pallas_call x15, Pallas kernels, call(): pl.pallas_call(body, out_shape=[jax.ShapeDtypeStruct(s, d) for s, d in ou...  217 us
    ppermute x53, waiting for transfers between devices, flip(): return lax.ppermute(value, AXES, pairs)  180 us
    psum x1, blocking collectives, local(): gain_grads, counts = lax.psum((gain_grads, counts), AXES)  103 us
    ppermute x53, starting transfers between devices, flip(): return lax.ppermute(value, AXES, pairs)  37.1 us
  transfers between devices with their start and end apart: 54, of which 18 were waited for; matrix products, arithmetic and copies ran while one was open for 10% of the time, Pallas kernels for 32%

profile of v2, /device:TPU:0, one launch (start us, length us, event | category | flops | bytes accessed | tf_op | source)
XLA Modules:
  0.0 628.1 jit_solution(5944347803087616517)
XLA Ops:
  8.0 4.1 collective-permute-start.37
  15.6 4.6 slice_bitcast_fusion
  21.6 5.4 collective-permute-done.2.refs_1_
  30.0 12.2 %self_forward.3 = (f32[256,512]{1,0:T(8,128)}, bf16[256,512]{1,0:T(8,128)(2,1)}, bf16[1024,512]{1,0:T(8,128)(2,1)}, bf16[1024,512]{1,0:T(8,128)(2,1)}, bf16[512,...) custom-call(s32[1]{0:T(128)} %bitcast.me_ref, ...), custom_call_target="tpu_custom_call" | custom-call | flops 14259999744 | bytes 8663040 | tf_op jit(solution)/shard_map/self_forward/pallas_call | solution.py:96
  42.1 29.9 %expert_forward.1 = (f32[2,256,512]{2,1,0:T(8,128)}, bf16[2,256,512]{2,1,0:T(8,128)(2,1)}, bf16[4,256,512]{2,1,0:T(8,128)(2,1)}) custom-call(bf16[1,256,512]{2,1,0:T(8,128)(2,1)} %bitcast.81, s32[8,1,256]{2,1,0:T(1,128)} %bitcast.87, s32[2,256,1]{2,1,0:T(8,128)} %reshape_squeeze.24.mine.refs_4_, f32[256,512]{1,0:T(8,128)} %get-tuple-element.83.res.refs_5_, ...), custom_call_target="tpu_custom_call" | custom-call | flops 12190000128 | bytes 20197376 | tf_op jit(solution)/shard_map/expert_forward/pallas_call | solution.py:96
  74.8 12.3 %collective-permute-done.6.refs_2_ = bf16[1,2,256,512]{3,2,1,0:T(8,128)(2,1)S(1)} collective-permute-done((bf16[1,2,256,512]{3,2,1,0:T(8,128)(2,1)}, bf16[1,2,256,512]{3,2,1,0:T(8,128)(2,1)S(1)}, u32[]{:S(2)}, u32[]{:S(2)}) %collective-permute-start.6) | collective-permute-done | bytes 524320 | tf_op jit(solution)/shard_map/ppermute | solution.py:821
  88.1 12.2 %self_forward.2 = (f32[256,512]{1,0:T(8,128)}, bf16[256,512]{1,0:T(8,128)(2,1)}, bf16[1024,512]{1,0:T(8,128)(2,1)}, bf16[1024,512]{1,0:T(8,128)(2,1)}, bf16[512,...) custom-call(s32[1]{0:T(128)} %bitcast.me_ref, ...), custom_call_target="tpu_custom_call" | custom-call | flops 14259999744 | bytes 8663040 | tf_op jit(solution)/shard_map/self_forward/pallas_call | solution.py:96
  101.3 20.9 %cross_forward.1 = (f32[2,256,512]{2,1,0:T(8,128)}, bf16[2,256,512]{2,1,0:T(8,128)(2,1)}, bf16[2,1024,512]{2,1,0:T(8,128)(2,1)}, bf16[2,1024,512]{2,1,0:T(8,128)...) custom-call(bf16[256,512]{1,0:T(8,128)(2,1)} %get-tuple-element.81.r, ...), custom_call_target="tpu_custom_call" | custom-call | flops 24149999616 | bytes 15747072 | tf_op jit(solution)/shard_map/cross_forward/pallas_call | solution.py:96
  125.3 11.5 %collective-permute-done.8.refs_1_ = bf16[1,2,256,512]{3,2,1,0:T(8,128)(2,1)S(1)} collective-permute-done((bf16[1,2,256,512]{3,2,1,0:T(8,128)(2,1)}, bf16[1,2,256,512]{3,2,1,0:T(8,128)(2,1)S(1)}, u32[]{:S(2)}, u32[]{:S(2)}) %collective-permute-start.8) | collective-permute-done | bytes 524320 | tf_op jit(solution)/shard_map/ppermute | solution.py:821
  136.8 13.3 %collective-permute-done.43 = bf16[1,2,256,512]{3,2,1,0:T(8,128)(2,1)S(1)} collective-permute-done((bf16[1,2,256,512]{3,2,1,0:T(8,128)(2,1)}, bf16[1,2,256,512]{3,2,1,0:T(8,128)(2,1)S(1)}, u32[]{:S(2)}, u32[]{:S(2)}) %collective-permute-start.43) | collective-permute-done | bytes 524320 | tf_op jit(solution)/shard_map/ppermute | solution.py:821
  155.0 15.8 %expert_backward.2 = (bf16[4,2,32,512]{3,2,1,0:T(8,128)(2,1)}, bf16[4,2,32,512]{3,2,1,0:T(8,128)(2,1)}, bf16[4,2,32,512]{3,2,1,0:T(8,128)(2,1)}, bf16[4,2,32,512...) custom-call(s32[1]{0:T(128)} %bitcast.me_ref, ...), custom_call_target="tpu_custom_call" | custom-call | flops 16675000320 | bytes 23076864 | tf_op jit(solution)/shard_map/expert_backward/pallas_call | solution.py:96
  173.9 6.4 %collective-permute-done.15.refs_1_ = bf16[4,2,32,512]{3,2,1,0:T(8,128)(2,1)S(1)} collective-permute-done((bf16[4,2,32,512]{3,2,1,0:T(8,128)(2,1)}, bf16[4,2,32,512]{3,2,1,0:T(8,128)(2,1)S(1)}, u32[]{:S(2)}, u32[]{:S(2)}) %collective-permute-start.15) | collective-permute-done | bytes 262176 | tf_op jit(solution)/shard_map/ppermute | solution.py:821
  180.2 4.0 collective-permute-done.17.refs_3_
  185.0 28.1 %cross_backward.1 = (bf16[1,2,256,512]{3,2,1,0:T(8,128)(2,1)}, bf16[1,2,256,512]{3,2,1,0:T(8,128)(2,1)}, bf16[2,2,256,512]{3,2,1,0:T(8,128)(2,1)}, bf16[512,2048...) custom-call(s32[1]{0:T(128)} %bitcast.me_ref, ...), custom_call_target="tpu_custom_call" | custom-call | flops 32199999488 | bytes 19949568 | tf_op jit(solution)/shard_map/cross_backward/pallas_call | solution.py:96
  219.3 9.7 %collective-permute-done.29 = bf16[1,256,512]{2,1,0:T(8,128)(2,1)S(1)} collective-permute-done((bf16[1,256,512]{2,1,0:T(8,128)(2,1)S(1)}, bf16[1,256,512]{2,1,0:T(8,128)(2,1)S(1)}, u32[]{:S(2)}, u32[]{:S(2)}) %collective-permute-start.29) | collective-permute-done | bytes 262176 | tf_op jit(solution)/shard_map/ppermute | solution.py:821
  235.2 6.9 %collective-permute-done.30 = bf16[2,256,512]{2,1,0:T(8,128)(2,1)S(1)} collective-permute-done((bf16[2,256,512]{2,1,0:T(8,128)(2,1)S(1)}, bf16[2,256,512]{2,1,0:T(8,128)(2,1)S(1)}, u32[]{:S(2)}, u32[]{:S(2)}) %collective-permute-start.30) | collective-permute-done | bytes 524320 | tf_op jit(solution)/shard_map/ppermute | solution.py:821
  247.1 32.0 %collective-permute-done.19 = bf16[1,2,256,512]{3,2,1,0:T(8,128)(2,1)} collective-permute-done((bf16[1,2,256,512]{3,2,1,0:T(8,128)(2,1)S(1)}, bf16[1,2,256,512]{3,2,1,0:T(8,128)(2,1)}, u32[]{:S(2)}, u32[]{:S(2)}) %collective-permute-start.19) | collective-permute-done | bytes 524320 | tf_op jit(solution)/shard_map/ppermute | solution.py:821
  279.1 3.4 memory_backward.1
  285.0 11.0 %collective-permute-done.31.refs_2_ = bf16[3,256,512]{2,1,0:T(8,128)(2,1)} collective-permute-done((bf16[3,256,512]{2,1,0:T(8,128)(2,1)}, bf16[3,256,512]{2,1,0:T(8,128)(2,1)}, u32[]{:S(2)}, u32[]{:S(2)}) %collective-permute-start.31) | collective-permute-done | bytes 786464 | tf_op jit(solution)/shard_map/ppermute | solution.py:821
  299.2 3.5 pad_maximum_fusion.3
  307.8 14.4 %self_backward.1 = (bf16[1,256,512]{2,1,0:T(8,128)(2,1)}, bf16[1,256,512]{2,1,0:T(8,128)(2,1)}, bf16[2,256,512]{2,1,0:T(8,128)(2,1)}, bf16[512,2048]{1,0:T(8,128)(2,1)}) custom-call(s32[1]{0:T(128)} %bitcast.me_ref, f32[256,512]{1,0:T(8,128)} %get-tuple-element.126.up.refs_4_, bf16[1024,512]{1,0:T(8,128)(2,1)} %get-tuple-element.127.hm, ...), custom_call_target="tpu_custom_call" | custom-call | flops 16675000320 | bytes 10493952 | tf_op jit(solution)/shard_map/self_backward/pallas_call | solution.py:96
  322.8 3.4 combine_output.1
  326.1 24.0 %collective-permute-done.45.refs_4_ = bf16[3,2,256,512]{3,2,1,0:T(8,128)(2,1)S(1)} collective-permute-done((bf16[3,2,256,512]{3,2,1,0:T(8,128)(2,1)}, bf16[3,2,256,512]{3,2,1,0:T(8,128)(2,1)S(1)}, u32[]{:S(2)}, u32[]{:S(2)}) %collective-permute-start.45) | collective-permute-done | bytes 1572896 | tf_op jit(solution)/shard_map/ppermute | solution.py:821
  354.1 13.2 %expert_backward.3 = (bf16[4,2,32,512]{3,2,1,0:T(8,128)(2,1)}, bf16[4,2,32,512]{3,2,1,0:T(8,128)(2,1)}, bf16[4,2,32,512]{3,2,1,0:T(8,128)(2,1)}, bf16[4,2,32,512]{3,2,1,0:T(8,128)(2,1)}) custom-call(s32[1]{0:T(128)} %bitcast.me_ref, bf16[4,256,512]{2,1,0:T(8,128)(2,1)} %get-tuple-element.92.refs_0_, bf16[1,2,256,512]{3,2,1,0:T(8,128)(2,1)} %bitcast.73, ...), custom_call_target="tpu_custom_call" | custom-call | flops 16675000320 | bytes 20979712 | tf_op jit(solution)/shard_map/expert_backward/pallas_call | solution.py:96
  367.8 10.1 %collective-permute-done.34 = bf16[2,2,256,512]{3,2,1,0:T(8,128)(2,1)S(1)} collective-permute-done((bf16[2,2,256,512]{3,2,1,0:T(8,128)(2,1)S(1)}, bf16[2,2,256,512]{3,2,1,0:T(8,128)(2,1)S(1)}, u32[]{:S(2)}, u32[]{:S(2)}) %collective-permute-start.34) | collective-permute-done | bytes 1048608 | tf_op jit(solution)/shard_map/ppermute | solution.py:821
  378.9 7.8 %collective-permute-done.24.refs_3_ = bf16[4,2,32,512]{3,2,1,0:T(8,128)(2,1)S(1)} collective-permute-done((bf16[4,2,32,512]{3,2,1,0:T(8,128)(2,1)}, bf16[4,2,32,512]{3,2,1,0:T(8,128)(2,1)S(1)}, u32[]{:S(2)}, u32[]{:S(2)}) %collective-permute-start.24) | collective-permute-done | bytes 262176 | tf_op jit(solution)/shard_map/ppermute | solution.py:821
  387.3 15.9 %encoder_backward.1 = (bf16[1,256,512]{2,1,0:T(8,128)(2,1)}, bf16[1,256,512]{2,1,0:T(8,128)(2,1)}, bf16[2,256,512]{2,1,0:T(8,128)(2,1)}, bf16[512,2048]{1,0:T(8,...) custom-call(s32[1]{0:T(128)} %bitcast.me_ref, bf16[4,2,32,512]{3,2,1,0:T(8,128)(2,1)} %get-tuple-element.109.refs_0_, ...), custom_call_target="tpu_custom_call" | custom-call | flops 18400000000 | bytes 13121536 | tf_op jit(solution)/shard_map/encoder_backward/pallas_call | solution.py:96
  403.2 19.7 %collective-permute-done.35.refs_8_ = bf16[3,2,256,512]{3,2,1,0:T(8,128)(2,1)S(1)} collective-permute-done((bf16[3,2,256,512]{3,2,1,0:T(8,128)(2,1)S(1)}, bf16[3,2,256,512]{3,2,1,0:T(8,128)(2,1)S(1)}, u32[]{:S(2)}, u32[]{:S(2)}) %collective-permute-start.35) | collective-permute-done | bytes 1572896 | tf_op jit(solution)/shard_map/ppermute | solution.py:821
  435.8 21.8 %expert_weights.3 = (bf16[2,4,256,512]{3,2,1,0:T(8,128)(2,1)}, bf16[2,4,256,512]{3,2,1,0:T(8,128)(2,1)}) custom-call(s32[3]{0:T(128)} %pad_add_fusion.6.place_ref, bf16[1,2,256,512]{3,2,1,0:T(8,128)(2,1)} %bitcast.69, bf16[1,2,256,512]{3,2,1,0:T(8,128)(2,1)} %copy-done.17, bf16[2,2,256,512]{3,2,1,0:T(8,128)(2,1)} %copy-done.41, ...), custom_call_target="tpu_custom_call" | custom-call | flops 24149999616 | bytes 37781504 | tf_op jit(solution)/shard_map/expert_weights/pallas_call | solution.py:96
  463.1 20.6 %expert_weights.2 = (bf16[2,4,256,512]{3,2,1,0:T(8,128)(2,1)}, bf16[2,4,256,512]{3,2,1,0:T(8,128)(2,1)}) custom-call(s32[3]{0:T(128)} %pad_add_fusion.6.place_ref, bf16[4,256,512]{2,1,0:T(8,128)(2,1)} %get-tuple-element.92.refs_0_, bf16[3,256,512]{2,1,0:T(8,128)(2,1)} %constant_dynamic-update-slice_fusion.refs_1_, ...), custom_call_target="tpu_custom_call" | custom-call | flops 24149999616 | bytes 33587200 | tf_op jit(solution)/shard_map/expert_weights/pallas_call | solution.py:96
  495.6 103.4 %all-reduce = (f32[6,512]{1,0:T(8,128)}, f32[2,2,16]{2,1,0:T(2,128)S(1)}) all-reduce(f32[6,512]{1,0:T(8,128)S(1)} %concatenate.89, f32[2,2,16]{2,1,0:T(2,128)S(1)} %convert_reduce_fusion), channel_id=1, replica_groups=mesh['dp'=8,'expert'=4] {'dp','expert'}, use_global_device_ids=true, to_apply=%region_1.2 | all-reduce | flops 3136 | bytes 25088 | tf_op jit(solution)/shard_map/psum | solution.py:1019
  605.4 7.6 %slice.146 = f32[3,512,1536]{2,1,0:T(8,128)} slice(bf16[3,512,2048]{2,1,0:T(8,128)(2,1)} %all-reduce.3.cloned.1.call-done), slice={[0:3], [0:512], [0:1536]} | slice | bytes 18874368 | tf_op jit(solution)/shard_map/slice | solution.py:1025
  (259 shorter events, 104.4 us)
Async XLA Ops:
  7.2 598.2 %all-reduce.3.cloned.1.call-start = ((), (), s32[]{:S(2)}) async-start(), calls=%async_computation | async-start | bytes 12582912 | tf_op jit(solution)/shard_map/psum | solution.py:1018
  13.6 60.0 %collective-permute-start = (bf16[1,256,512]{2,1,0:T(8,128)(2,1)}, bf16[1,256,512]{2,1,0:T(8,128)(2,1)S(1)}, u32[]{:S(2)}, u32[]{:S(2)}) collective-permute-start(bf16[1,256,512]{2,1,0:T(8,128)(2,1)} %refs_0_.2), channel_id=1, source_target_pairs={{0,2},{1,3},{2,0},{3,1},{4,6},{5,7},{6,4},{7,5},{8,10},{9,11},{10,... | collective-permute-start | bytes 786440 | tf_op jit(solution)/shard_map/ppermute | solution.py:821
  73.8 50.3 %collective-permute-start.10 = (bf16[1,2,256,512]{3,2,1,0:T(8,128)(2,1)S(1)}, bf16[1,2,256,512]{3,2,1,0:T(8,128)(2,1)S(1)}, u32[]{:S(2)}, u32[]{:S(2)}) collective-permute-start(bf16[1,2,256,512]{3,2,1,0:T(8,128)(2,1)S(1)} %fusion.1.refs_3_.refs_6_), channel_id=1, source_target_pairs={{0,2},{1,3},{2,0},{3,1},{4,6},{5,7},{6,4},{7,5},{8,10},{9,11},{10,... | collective-permute-start | bytes 1572872 | tf_op jit(solution)/shard_map/ppermute | solution.py:821
  74.4 49.6 %collective-permute-start.47 = (bf16[1,2,256,512]{3,2,1,0:T(8,128)(2,1)S(1)}, bf16[1,2,256,512]{3,2,1,0:T(8,128)(2,1)S(1)}, u32[]{:S(2)}, u32[]{:S(2)}) collective-permute-start(bf16[1,2,256,512]{3,2,1,0:T(8,128)(2,1)S(1)} %fusion.1.refs_3_.refs_6_), channel_id=1, source_target_pairs={{0,16},{1,17},{2,18},{3,19},{4,20},{5,21},{6,22},{7,23},{8,24},{9,... | collective-permute-start | bytes 1572872 | tf_op jit(solution)/shard_map/ppermute | solution.py:821
  123.7 26.4 %collective-permute-start.43 = (bf16[1,2,256,512]{3,2,1,0:T(8,128)(2,1)}, bf16[1,2,256,512]{3,2,1,0:T(8,128)(2,1)S(1)}, u32[]{:S(2)}, u32[]{:S(2)}) collective-permute-start(bf16[1,2,256,512]{3,2,1,0:T(8,128)(2,1)} %bitcast.67), channel_id=1, source_target_pairs={{0,16},{1,17},{2,18},{3,19},{4,20},{5,21},{6,22},{7,23},{8,24},{9,... | collective-permute-start | bytes 1572872 | tf_op jit(solution)/shard_map/ppermute | solution.py:821
  125.3 26.7 %collective-permute-start.11 = (bf16[2,2,256,512]{3,2,1,0:T(8,128)(2,1)S(1)}, bf16[2,2,256,512]{3,2,1,0:T(8,128)(2,1)S(1)}, u32[]{:S(2)}, u32[]{:S(2)}) collective-permute-start(bf16[2,2,256,512]{3,2,1,0:T(8,128)(2,1)S(1)} %get-tuple-element.206), channel_id=1, source_target_pairs={{0,1},{1,0},{2,3},{3,2},{4,5},{5,4},{6,7},{7,6},{8,9},{9,8},{10,11... | collective-permute-start | bytes 3145736 | tf_op jit(solution)/shard_map/ppermute | solution.py:821
  173.9 55.3 %collective-permute-start.48 = (bf16[2,2,256,512]{3,2,1,0:T(8,128)(2,1)}, bf16[2,2,256,512]{3,2,1,0:T(8,128)(2,1)S(1)}, u32[]{:S(2)}, u32[]{:S(2)}) collective-permute-start(bf16[2,2,256,512]{3,2,1,0:T(8,128)(2,1)} %get-tuple-element.205), channel_id=1, source_target_pairs={{0,8},{1,9},{2,10},{3,11},{4,12},{5,13},{6,14},{7,15},{8,0},{9,1},... | collective-permute-start | bytes 3145736 | tf_op jit(solution)/shard_map/ppermute | solution.py:821
  217.8 25.7 %collective-permute-start.39 = (s32[3,2,2,256]{3,0,2,1:T(4,128)S(1)}, s32[3,2,2,256]{3,0,2,1:T(4,128)S(1)}, u32[]{:S(2)}, u32[]{:S(2)}) collective-permute-start(s32[3,2,2,256]{3,0,2,1:T(4,128)S(1)} %pad_add_fusion.2), channel_id=1, source_target_pairs={{0,2},{1,3},{2,0},{3,1},{4,6},{5,7},{6,4},{7,5},{8,10},{9,11},{10,... | collective-permute-start | bytes 36872 | tf_op jit(solution)/shard_map/ppermute | solution.py:821
  230.2 69.0 %collective-permute-start.49 = (bf16[3,2,256,512]{3,2,1,0:T(8,128)(2,1)}, bf16[3,2,256,512]{3,2,1,0:T(8,128)(2,1)}, u32[]{:S(2)}, u32[]{:S(2)}) collective-permute-start(bf16[3,2,256,512]{3,2,1,0:T(8,128)(2,1)} %constant_dynamic-update-slice_fusion.6.refs_9_), channel_id=1, source_target_pairs={{0,2},{1,3},{2,0},{3,1},{4,6},{5,7},{6,4},{7,5},{8,10},{9,11},{10,... | collective-permute-start | bytes 4718600 | tf_op jit(solution)/shard_map/ppermute | solution.py:821
  233.7 45.3 %collective-permute-start.19 = (bf16[1,2,256,512]{3,2,1,0:T(8,128)(2,1)S(1)}, bf16[1,2,256,512]{3,2,1,0:T(8,128)(2,1)}, u32[]{:S(2)}, u32[]{:S(2)}) collective-permute-start(bf16[1,2,256,512]{3,2,1,0:T(8,128)(2,1)S(1)} %get-tuple-element.203), channel_id=1, source_target_pairs={{0,2},{1,3},{2,0},{3,1},{4,6},{5,7},{6,4},{7,5},{8,10},{9,11},{10,... | collective-permute-start | bytes 1572872 | tf_op jit(solution)/shard_map/ppermute | solution.py:821
  243.0 52.9 %collective-permute-start.31 = (bf16[3,256,512]{2,1,0:T(8,128)(2,1)}, bf16[3,256,512]{2,1,0:T(8,128)(2,1)}, u32[]{:S(2)}, u32[]{:S(2)}) collective-permute-start(bf16[3,256,512]{2,1,0:T(8,128)(2,1)} %constant_dynamic-update-slice_fusion.refs_1_), channel_id=1, source_target_pairs={{0,2},{1,3},{2,0},{3,1},{4,6},{5,7},{6,4},{7,5},{8,10},{9,11},{10,... | collective-permute-start | bytes 2359304 | tf_op jit(solution)/shard_map/ppermute | solution.py:821
  245.5 57.8 %collective-permute-start.44 = (bf16[2,2,256,512]{3,2,1,0:T(8,128)(2,1)}, bf16[2,2,256,512]{3,2,1,0:T(8,128)(2,1)S(1)}, u32[]{:S(2)}, u32[]{:S(2)}) collective-permute-start(bf16[2,2,256,512]{3,2,1,0:T(8,128)(2,1)} %get-tuple-element.207), channel_id=1, source_target_pairs={{0,8},{1,9},{2,10},{3,11},{4,12},{5,13},{6,14},{7,15},{8,0},{9,1},... | collective-permute-start | bytes 3145736 | tf_op jit(solution)/shard_map/ppermute | solution.py:821
  282.5 24.5 %collective-permute-start.20 = (bf16[1,2,256,512]{3,2,1,0:T(8,128)(2,1)}, bf16[1,2,256,512]{3,2,1,0:T(8,128)(2,1)S(1)}, u32[]{:S(2)}, u32[]{:S(2)}) collective-permute-start(bf16[1,2,256,512]{3,2,1,0:T(8,128)(2,1)} %bitcast.71), channel_id=1, source_target_pairs={{0,2},{1,3},{2,0},{3,1},{4,6},{5,7},{6,4},{7,5},{8,10},{9,11},{10,... | collective-permute-start | bytes 1572872 | tf_op jit(solution)/shard_map/ppermute | solution.py:821
  283.0 24.6 %collective-permute-start.33 = (bf16[1,2,256,512]{3,2,1,0:T(8,128)(2,1)}, bf16[1,2,256,512]{3,2,1,0:T(8,128)(2,1)S(1)}, u32[]{:S(2)}, u32[]{:S(2)}) collective-permute-start(bf16[1,2,256,512]{3,2,1,0:T(8,128)(2,1)} %bitcast.72), channel_id=1, source_target_pairs={{0,16},{1,17},{2,18},{3,19},{4,20},{5,21},{6,22},{7,23},{8,24},{9,... | collective-permute-start | bytes 1572872 | tf_op jit(solution)/shard_map/ppermute | solution.py:821
  302.7 19.6 %collective-permute-start.12 = (bf16[4,2,32,512]{3,2,1,0:T(8,128)(2,1)}, bf16[4,2,32,512]{3,2,1,0:T(8,128)(2,1)}, u32[]{:S(2)}, u32[]{:S(2)}) collective-permute-start(bf16[4,2,32,512]{3,2,1,0:T(8,128)(2,1)} %get-tuple-element.88), channel_id=1, source_target_pairs={{0,2},{1,3},{2,0},{3,1},{4,6},{5,7},{6,4},{7,5},{8,10},{9,11},{10,... | collective-permute-start | bytes 786440 | tf_op jit(solution)/shard_map/ppermute | solution.py:821
  303.2 19.5 %collective-permute-start.13 = (bf16[4,2,32,512]{3,2,1,0:T(8,128)(2,1)}, bf16[4,2,32,512]{3,2,1,0:T(8,128)(2,1)}, u32[]{:S(2)}, u32[]{:S(2)}) collective-permute-start(bf16[4,2,32,512]{3,2,1,0:T(8,128)(2,1)} %get-tuple-element.89), channel_id=1, source_target_pairs={{0,1},{1,0},{2,3},{3,2},{4,5},{5,4},{6,7},{7,6},{8,9},{9,8},{10,11... | collective-permute-start | bytes 786440 | tf_op jit(solution)/shard_map/ppermute | solution.py:821
  303.2 19.5 %collective-permute-start.14 = (bf16[4,2,32,512]{3,2,1,0:T(8,128)(2,1)S(1)}, bf16[4,2,32,512]{3,2,1,0:T(8,128)(2,1)}, u32[]{:S(2)}, u32[]{:S(2)}) collective-permute-start(bf16[4,2,32,512]{3,2,1,0:T(8,128)(2,1)S(1)} %copy-done.45), channel_id=1, source_target_pairs={{0,3},{1,2},{2,1},{3,0},{4,7},{5,6},{6,5},{7,4},{8,11},{9,10},{10,... | collective-permute-start | bytes 786440 | tf_op jit(solution)/shard_map/ppermute | solution.py:821
  307.1 43.1 %collective-permute-start.45 = (bf16[3,2,256,512]{3,2,1,0:T(8,128)(2,1)}, bf16[3,2,256,512]{3,2,1,0:T(8,128)(2,1)S(1)}, u32[]{:S(2)}, u32[]{:S(2)}) collective-permute-start(bf16[3,2,256,512]{3,2,1,0:T(8,128)(2,1)} %constant_dynamic-update-slice_fusion.4.refs_3_), channel_id=1, source_target_pairs={{0,2},{1,3},{2,0},{3,1},{4,6},{5,7},{6,4},{7,5},{8,10},{9,11},{10,... | collective-permute-start | bytes 4718600 | tf_op jit(solution)/shard_map/ppermute | solution.py:821
  307.8 46.3 %collective-permute-start.21 = (bf16[2,2,256,512]{3,2,1,0:T(8,128)(2,1)S(1)}, bf16[2,2,256,512]{3,2,1,0:T(8,128)(2,1)}, u32[]{:S(2)}, u32[]{:S(2)}) collective-permute-start(bf16[2,2,256,512]{3,2,1,0:T(8,128)(2,1)S(1)} %get-tuple-element.210), channel_id=1, source_target_pairs={{0,1},{1,0},{2,3},{3,2},{4,5},{5,4},{6,7},{7,6},{8,9},{9,8},{10,11... | collective-permute-start | bytes 3145736 | tf_op jit(solution)/shard_map/ppermute | solution.py:821
  322.3 112.1 %collective-permute-start.50 = (bf16[6,2,256,512]{3,2,1,0:T(8,128)(2,1)}, bf16[6,2,256,512]{3,2,1,0:T(8,128)(2,1)}, u32[]{:S(2)}, u32[]{:S(2)}) collective-permute-start(bf16[6,2,256,512]{3,2,1,0:T(8,128)(2,1)} %pad_maximum_fusion.3), channel_id=1, source_target_pairs={{0,1},{1,0},{2,3},{3,2},{4,5},{5,4},{6,7},{7,6},{8,9},{9,8},{10,11... | collective-permute-start | bytes 9437192 | tf_op jit(solution)/shard_map/ppermute | solution.py:821
  352.3 83.4 %collective-permute-start.46 = (bf16[6,2,256,512]{3,2,1,0:T(8,128)(2,1)}, bf16[6,2,256,512]{3,2,1,0:T(8,128)(2,1)}, u32[]{:S(2)}, u32[]{:S(2)}) collective-permute-start(bf16[6,2,256,512]{3,2,1,0:T(8,128)(2,1)} %pad_maximum_fusion.2), channel_id=1, source_target_pairs={{0,1},{1,0},{2,3},{3,2},{4,5},{5,4},{6,7},{7,6},{8,9},{9,8},{10,11... | collective-permute-start | bytes 9437192 | tf_op jit(solution)/shard_map/ppermute | solution.py:821
  352.3 25.6 %collective-permute-start.34 = (bf16[2,2,256,512]{3,2,1,0:T(8,128)(2,1)S(1)}, bf16[2,2,256,512]{3,2,1,0:T(8,128)(2,1)S(1)}, u32[]{:S(2)}, u32[]{:S(2)}) collective-permute-start(bf16[2,2,256,512]{3,2,1,0:T(8,128)(2,1)S(1)} %get-tuple-element.209), channel_id=1, source_target_pairs={{0,8},{1,9},{2,10},{3,11},{4,12},{5,13},{6,14},{7,15},{8,0},{9,1},... | collective-permute-start | bytes 3145736 | tf_op jit(solution)/shard_map/ppermute | solution.py:821
  378.1 84.6 %collective-permute-start.32 = (bf16[6,256,512]{2,1,0:T(8,128)(2,1)}, bf16[6,256,512]{2,1,0:T(8,128)(2,1)}, u32[]{:S(2)}, u32[]{:S(2)}) collective-permute-start(bf16[6,256,512]{2,1,0:T(8,128)(2,1)} %pad_maximum_fusion.4), channel_id=1, source_target_pairs={{0,1},{1,0},{2,3},{3,2},{4,5},{5,4},{6,7},{7,6},{8,9},{9,8},{10,11... | collective-permute-start | bytes 4718600 | tf_op jit(solution)/shard_map/ppermute | solution.py:821
  378.8 47.2 %collective-permute-start.27 = (bf16[2,256,512]{2,1,0:T(8,128)(2,1)}, bf16[2,256,512]{2,1,0:T(8,128)(2,1)}, u32[]{:S(2)}, u32[]{:S(2)}) collective-permute-start(bf16[2,256,512]{2,1,0:T(8,128)(2,1)} %get-tuple-element.135), channel_id=1, source_target_pairs={{0,1},{1,0},{2,3},{3,2},{4,5},{5,4},{6,7},{7,6},{8,9},{9,8},{10,11... | collective-permute-start | bytes 1572872 | tf_op jit(solution)/shard_map/ppermute | solution.py:821
  386.6 36.3 %collective-permute-start.35 = (bf16[3,2,256,512]{3,2,1,0:T(8,128)(2,1)S(1)}, bf16[3,2,256,512]{3,2,1,0:T(8,128)(2,1)S(1)}, u32[]{:S(2)}, u32[]{:S(2)}) collective-permute-start(bf16[3,2,256,512]{3,2,1,0:T(8,128)(2,1)S(1)} %constant_dynamic-update-slice_fusion.2.refs_7_), channel_id=1, source_target_pairs={{0,2},{1,3},{2,0},{3,1},{4,6},{5,7},{6,4},{7,5},{8,10},{9,11},{10,... | collective-permute-start | bytes 4718600 | tf_op jit(solution)/shard_map/ppermute | solution.py:821
  426.0 37.1 %collective-permute-start.36 = (bf16[6,2,256,512]{3,2,1,0:T(8,128)(2,1)S(1)}, bf16[6,2,256,512]{3,2,1,0:T(8,128)(2,1)}, u32[]{:S(2)}, u32[]{:S(2)}) collective-permute-start(bf16[6,2,256,512]{3,2,1,0:T(8,128)(2,1)S(1)} %pad_maximum_fusion.1), channel_id=1, source_target_pairs={{0,1},{1,0},{2,3},{3,2},{4,5},{5,4},{6,7},{7,6},{8,9},{9,8},{10,11... | collective-permute-start | bytes 9437192 | tf_op jit(solution)/shard_map/ppermute | solution.py:821
  431.7 54.9 %collective-permute-start.28 = (bf16[1,256,512]{2,1,0:T(8,128)(2,1)S(1)}, bf16[1,256,512]{2,1,0:T(8,128)(2,1)S(1)}, u32[]{:S(2)}, u32[]{:S(2)}) collective-permute-start(bf16[1,256,512]{2,1,0:T(8,128)(2,1)S(1)} %get-tuple-element.211), channel_id=1, source_target_pairs={{0,2},{1,3},{2,0},{3,1},{4,6},{5,7},{6,4},{7,5},{8,10},{9,11},{10,... | collective-permute-start | bytes 786440 | tf_op jit(solution)/shard_map/ppermute | solution.py:821
  434.4 57.0 %collective-permute-start.26 = (bf16[1,256,512]{2,1,0:T(8,128)(2,1)S(1)}, bf16[1,256,512]{2,1,0:T(8,128)(2,1)S(1)}, u32[]{:S(2)}, u32[]{:S(2)}) collective-permute-start(bf16[1,256,512]{2,1,0:T(8,128)(2,1)S(1)} %get-tuple-element.213), channel_id=1, source_target_pairs={{0,2},{1,3},{2,0},{3,1},{4,6},{5,7},{6,4},{7,5},{8,10},{9,11},{10,... | collective-permute-start | bytes 786440 | tf_op jit(solution)/shard_map/ppermute | solution.py:821
  460.0 139.5 %collective-permute-start.51 = (bf16[1,4,256,512]{3,2,1,0:T(8,128)(2,1)}, bf16[1,4,256,512]{3,2,1,0:T(8,128)(2,1)}, u32[]{:S(2)}, u32[]{:S(2)}) collective-permute-start(bf16[1,4,256,512]{3,2,1,0:T(8,128)(2,1)} %slice.135), channel_id=1, source_target_pairs={{0,4},{1,5},{2,6},{3,7},{4,0},{5,1},{6,2},{7,3},{8,12},{9,13},{10,... | collective-permute-start | bytes 3145736 | tf_op jit(solution)/shard_map/ppermute | solution.py:821
  462.6 139.9 %collective-permute-start.52 = (bf16[1,4,256,512]{3,2,1,0:T(8,128)(2,1)}, bf16[1,4,256,512]{3,2,1,0:T(8,128)(2,1)}, u32[]{:S(2)}, u32[]{:S(2)}) collective-permute-start(bf16[1,4,256,512]{3,2,1,0:T(8,128)(2,1)} %slice.137), channel_id=1, source_target_pairs={{0,4},{1,5},{2,6},{3,7},{4,0},{5,1},{6,2},{7,3},{8,12},{9,13},{10,... | collective-permute-start | bytes 3145736 | tf_op jit(solution)/shard_map/ppermute | solution.py:821
  485.0 130.0 %collective-permute-start.41 = (bf16[1,4,256,512]{3,2,1,0:T(8,128)(2,1)S(1)}, bf16[1,4,256,512]{3,2,1,0:T(8,128)(2,1)}, u32[]{:S(2)}, u32[]{:S(2)}) collective-permute-start(bf16[1,4,256,512]{3,2,1,0:T(8,128)(2,1)S(1)} %slice.130), channel_id=1, source_target_pairs={{0,4},{1,5},{2,6},{3,7},{4,0},{5,1},{6,2},{7,3},{8,12},{9,13},{10,... | collective-permute-start | bytes 3145736 | tf_op jit(solution)/shard_map/ppermute | solution.py:821
  491.0 127.2 %collective-permute-start.42 = (bf16[1,4,256,512]{3,2,1,0:T(8,128)(2,1)}, bf16[1,4,256,512]{3,2,1,0:T(8,128)(2,1)}, u32[]{:S(2)}, u32[]{:S(2)}) collective-permute-start(bf16[1,4,256,512]{3,2,1,0:T(8,128)(2,1)} %slice.132), channel_id=1, source_target_pairs={{0,4},{1,5},{2,6},{3,7},{4,0},{5,1},{6,2},{7,3},{8,12},{9,13},{10,... | collective-permute-start | bytes 3145736 | tf_op jit(solution)/shard_map/ppermute | solution.py:821
  (76 other events, 825.7 us)
Sparse Core Ops, SparseCore 0:
  431.8 169.5 all-reduce.2

commit v3 on v0

v3 whole, which is shorter than its diff:
```python
import functools

import jax
import jax.numpy as jnp
from jax import lax
from jax.experimental import pallas as pl
from jax.experimental.pallas import tpu as pltpu
from jax.sharding import PartitionSpec as P

HEAD_DIM = 64
EXPERTS = 16
NORM_EPSILON = 1e-05
MASKED = -1e30
F32 = jnp.float32
BF16 = jnp.bfloat16
VMEM_LIMIT = 60 << 20
MESH = pl.DeviceIdType.MESH
DMA = pltpu.SemaphoreType.DMA


def nn(a, b):
    return jnp.dot(a, b, preferred_element_type=F32)


def nt(a, b):
    return lax.dot_general(a, b, (((1,), (1,)), ((), ())), preferred_element_type=F32)


def tn(a, b):
    return lax.dot_general(a, b, (((0,), (0,)), ((), ())), preferred_element_type=F32)


def tt(a, b):
    return lax.dot_general(a, b, (((0,), (1,)), ((), ())), preferred_element_type=F32)


def norm_parts(x):
    mean = jnp.mean(x, axis=-1, keepdims=True)
    centered = x - mean
    spread = jnp.mean(centered * centered, axis=-1, keepdims=True)
    scale = lax.rsqrt(spread + NORM_EPSILON)
    return centered * scale, scale


def norm(x, gain):
    return norm_parts(x)[0] * gain


def norm_back(x, gain, grad):
    hat, scale = norm_parts(x)
    inner = grad * gain
    dx = scale * (
        inner
        - jnp.mean(inner, axis=-1, keepdims=True)
        - hat * jnp.mean(inner * hat, axis=-1, keepdims=True)
    )
    return dx, jnp.sum(grad * hat, axis=0, keepdims=True)


GELU_A = 0.7978845608028654
GELU_B = 0.044715


def gelu(x):
    return 0.5 * x * (1.0 + jnp.tanh(x * (GELU_A + (GELU_A * GELU_B) * (x * x))))


def gelu_both(x):
    sq = x * x
    th = jnp.tanh(x * (GELU_A + (GELU_A * GELU_B) * sq))
    half = 0.5 * (1.0 + th)
    slope = half + (0.5 * x) * (1.0 - th * th) * (GELU_A + (3.0 * GELU_A * GELU_B) * sq)
    return x * half, slope


def xor(value, bits):
    b = 1
    while b <= bits:
        if bits & b:
            value = value + b * (1 - 2 * lax.rem(lax.div(value, b), 2))
        b *= 2
    return value


def peer(to):
    return (xor(lax.axis_index("dp"), to[0]), xor(lax.axis_index("expert"), to[1]))


def send(src, dst, send_sem, recv_sem, to):
    return pltpu.make_async_remote_copy(
        src_ref=src, dst_ref=dst, send_sem=send_sem, recv_sem=recv_sem, device_id=peer(to), device_id_type=MESH
    )


def expert_peers(ids):
    return [(0, r) for r in ids[1:]]


class Gather:
    def __init__(self, ids, near, send_sems, recv_sems):
        self.pos = {r: i for i, r in enumerate(ids)}
        self.far = [r for r in ids if r % 2 == 0 and r > 0]
        self.near, self.sems = near, (send_sems, recv_sems)

    def copy(self, r, src, to):
        at = self.pos[r]
        return send(src, self.near.at[at], self.sems[0].at[at], self.sems[1].at[at], (0, to))

    def first(self, r):
        return self.copy(r, self.near.at[0], r)

    def second(self, r):
        return self.copy(r ^ 1, self.near.at[self.pos[r]], 1)

    def start(self):
        for r in self.far:
            self.first(r).start()
        self.first(1).start()

    def forward(self):
        for r in self.far:
            self.first(r).wait_recv()
            self.second(r).start()

    def finish(self):
        for r in self.far:
            self.second(r).wait_recv()
        self.first(1).wait_recv()
        for r in self.far:
            self.first(r).wait_send()
            self.second(r).wait_send()
        self.first(1).wait_send()


class Scatter:
    def __init__(self, ids, parts, got, send_sems, recv_sems):
        self.pos = {r: i for i, r in enumerate(ids)}
        self.odd = [r for r in ids if r % 2]
        self.even = [r for r in ids if r % 2 == 0]
        self.parts, self.got, self.sems = parts, got, (send_sems, recv_sems)

    def copy(self, r, to):
        at = self.pos[r]
        return send(
            self.parts.at[at], self.got.at[self.pos[r ^ 1]], self.sems[0].at[at], self.sems[1].at[at], (0, to)
        )

    def start(self):
        for r in self.odd:
            self.copy(r, 1).start()

    def middle(self):
        for r in self.odd:
            self.copy(r, 1).wait_recv()
        for r in self.even[1:]:
            at = self.pos[r]
            self.parts[at] = (self.parts[at].astype(F32) + self.got[at].astype(F32)).astype(BF16)
            self.copy(r, r).start()

    def finish(self):
        total = self.parts[0].astype(F32) + self.got[0].astype(F32)
        for r in self.even[1:]:
            self.copy(r, r).wait_recv()
            total = total + self.got[self.pos[r ^ 1]].astype(F32)
        for r in self.odd:
            self.copy(r, 1).wait_send()
        for r in self.even[1:]:
            self.copy(r, r).wait_send()
        return total


class Job:
    def __init__(self, own, far, z=(), x=(), c=()):
        self.own, self.far, self.z, self.x, self.c = own, far, list(z), list(x), list(c)


class Plan:
    def __init__(self, n_dp, n_expert):
        self.n_dp, self.n_expert = n_dp, n_expert
        self.ny = 2 if n_dp <= 8 else 4
        self.nz = n_dp // self.ny
        ids, bit = [0], n_expert // 2
        while bit >= 1:
            ids = ids + [i ^ bit for i in ids]
            bit //= 2
        self.ids = ids
        self.zr = list(range(1, self.nz))


class Background:
    def __init__(self, plan, jobs, owns, fars, send_sems, recv_sems, peers):
        self.plan, self.jobs, self.peers = plan, jobs, peers
        self.owns, self.fars, self.sems = owns, fars, (send_sems, recv_sems)

    def copies(self):
        plan = self.plan
        pos = {r: i for i, r in enumerate(plan.ids)}
        across = [r for r in plan.ids if r % 2 == 0 and r > 0]
        n = 0
        for job, own, far in zip(self.jobs, self.owns, self.fars):
            moves = []
            for zr in job.z:
                moves.append((own, far.at[zr - 1, 0], (zr * plan.ny, 0)))
            for zr in job.x:
                for r in across:
                    moves.append((far.at[zr - 1, 0], far.at[zr - 1, pos[r]], (0, r)))
            for zr in job.c:
                for r in [0] + across:
                    moves.append((far.at[zr - 1, pos[r]], far.at[zr - 1, pos[r ^ 1]], (0, 1)))
            for src, dst, to in moves:
                yield send(src, dst, self.sems[0].at[n], self.sems[1].at[n], to)
                n += 1

    def greet(self):
        barrier = pltpu.get_barrier_semaphore()
        for p in self.peers:
            pl.semaphore_signal(barrier, inc=1, device_id=peer(p), device_id_type=MESH)
        pl.semaphore_wait(barrier, len(self.peers))

    def start(self):
        for copy in self.copies():
            copy.start()

    def finish(self):
        for copy in self.copies():
            copy.wait()


def vmem(shape):
    return pl.BlockSpec(shape, lambda *_: (0,) * len(shape))


ANYWHERE = pl.BlockSpec(memory_space=pl.ANY)


def fused(
    plan, body, ins, outs, name, cid=None, peers=(), jobs=(), grid=None, in_specs=None, out_specs=None, scratch=(), us=10
):
    whole = (lambda shape: pl.BlockSpec(memory_space=pltpu.VMEM)) if grid is None else vmem
    in_specs = [None] * len(ins) if in_specs is None else in_specs
    out_specs = [None] * len(outs) if out_specs is None else out_specs
    in_specs = [whole(a.shape) if s is None else s for a, s in zip(ins, in_specs)]
    out_specs = [whole(o[0]) if s is None else s for o, s in zip(outs, out_specs)]
    ins, outs, scratch = list(ins), list(outs), list(scratch)
    n_in, n_out, n_scratch = len(ins), len(outs), len(scratch)
    aliases, places, count, peers = {}, [], 0, list(peers)
    across = [r for r in plan.ids if r % 2 == 0 and r > 0]
    for k, job in enumerate(jobs):
        place = None
        if job.z:
            place = len(ins)
            ins.append(job.own)
            in_specs.append(ANYWHERE)
        if job.far is not None:
            aliases[len(ins)] = n_out + k
            ins.append(job.far)
            in_specs.append(ANYWHERE)
            outs.append((job.far.shape, job.far.dtype))
        else:
            outs.append(((plan.nz - 1, plan.n_expert) + job.own.shape, job.own.dtype))
        out_specs.append(ANYWHERE)
        places.append(place)
        count += len(job.z) + len(job.x) * len(across) + len(job.c) * (1 + len(across))
        wanted = [(zr * plan.ny, 0) for zr in job.z]
        wanted += [(0, r) for r in across] if job.x else []
        wanted += [(0, 1)] if job.c else []
        peers += [p for p in wanted if p not in peers]
    if jobs:
        scratch += [DMA((count,)), DMA((count,))]

    def run(*refs):
        i, o, s = refs[: len(ins)], refs[len(ins) : len(ins) + len(outs)], refs[len(ins) + len(outs) :]
        if cid is None:
            return body(*i, *o, *s)
        sems = s[n_scratch:] if jobs else (None, None)
        bg = Background(plan, jobs, [None if p is None else i[p] for p in places], o[n_out:], *sems, peers)
        body(bg, *i[:n_in], *o[:n_out], *s[:n_scratch])

    moved = sum(a.size * a.dtype.itemsize for a in ins[:n_in])
    extra = {} if grid is None else {"grid": grid}
    got = pl.pallas_call(
        run,
        out_shape=[jax.ShapeDtypeStruct(s, d) for s, d in outs],
        in_specs=in_specs,
        out_specs=out_specs,
        scratch_shapes=scratch,
        input_output_aliases=aliases,
        name=name,
        compiler_params=pltpu.CompilerParams(
            vmem_limit_bytes=VMEM_LIMIT, collective_id=cid, has_side_effects=cid is not None
        ),
        cost_estimate=pl.CostEstimate(flops=int(us * 1.15e9), bytes_accessed=moved, transcendentals=0),
        **extra,
    )(*ins)
    return got[:n_out], got[n_out:]


def head_rows(values, h):
    rows = values[h * HEAD_DIM : (h + 1) * HEAD_DIM]
    zero = jnp.zeros_like(rows)
    return jnp.concatenate([rows, zero] if h % 2 == 0 else [zero, rows], axis=0)


def head_lanes(values, h):
    pair = values[:, (h // 2) * 128 : (h // 2 + 1) * 128]
    lane = lax.broadcasted_iota(jnp.int32, pair.shape, 1)
    keep = lane < HEAD_DIM if h % 2 == 0 else lane >= HEAD_DIM
    return jnp.where(keep, pair, jnp.zeros_like(pair))


def causal_allow(ids, rows):
    me = lax.axis_index("expert")
    parts = []
    for r in ids:
        key = xor(me, r) * rows + lax.broadcasted_iota(jnp.int32, (rows, rows), 0)
        query = me * rows + lax.broadcasted_iota(jnp.int32, (rows, rows), 1)
        parts.append((key <= query).astype(F32))
    return jnp.concatenate(parts, axis=0) > 0.5


def attend_forward(q_t, k, v_t, allow, o_t, lse, between=None):
    heads = q_t.shape[0] // HEAD_DIM
    for h in range(heads):
        if between is not None and h == heads // 2:
            between()
        pair = slice((h // 2) * 128, (h // 2 + 1) * 128)
        scores = nn(k[:, pair], head_rows(q_t, h))
        if allow is not None:
            scores = jnp.where(allow, scores, MASKED)
        top = jnp.max(scores, axis=0, keepdims=True)
        lifted = jnp.exp(scores - top)
        total = jnp.sum(lifted, axis=0, keepdims=True)
        rows = slice(h * HEAD_DIM, (h + 1) * HEAD_DIM)
        blended = nn(v_t[rows, :], lifted.astype(BF16)) * (1.0 / total)
        o_t[rows, :] = blended.astype(BF16)
        lse[h : h + 1, :] = top + jnp.log(total)


def attend_backward(q, k, v, k_t, do, lse, allow, dk, dv, dq_t, between=()):
    heads = q.shape[1] // HEAD_DIM
    q_t = q.astype(F32).T.astype(BF16)
    do_t = do.astype(F32).T.astype(BF16)
    for h2 in range(heads // 2):
        for at, act in between:
            if at == h2:
                act()
        pair = slice(h2 * 128, (h2 + 1) * 128)
        dk_pair = None
        for h in (2 * h2, 2 * h2 + 1):
            rows = slice(h * HEAD_DIM, (h + 1) * HEAD_DIM)
            scores = nn(k[:, pair], head_rows(q_t, h))
            weights = jnp.exp(scores - lse[h : h + 1, :])
            if allow is not None:
                weights = jnp.where(allow, weights, 0.0)
            weights_grad = nn(v[:, pair], head_rows(do_t, h))
            centre = jnp.sum(weights * weights_grad, axis=0, keepdims=True)
            scores_grad = (weights * (weights_grad - centre)).astype(BF16)
            dv_part = nn(weights.astype(BF16), head_lanes(do, h))
            dk_part = nn(scores_grad, head_lanes(q, h))
            dq_t[rows, :] = (nn(k_t[rows, :], scores_grad) * HEAD_DIM ** (-0.5)).astype(BF16)
            if dk_pair is None:
                dk_pair, dv_pair = dk_part, dv_part
            else:
                dk_pair, dv_pair = dk_pair + dk_part, dv_pair + dv_part
        dk[:, pair] = dk_pair.astype(BF16)
        dv[:, pair] = dv_pair.astype(BF16)


def project_rows(hm, win, k, k_t, v, v_t):
    feature = hm.shape[1]
    w_k, w_v = win[:, feature : 2 * feature], win[:, 2 * feature :]
    k[...] = nn(hm, w_k).astype(BF16)
    v[...] = nn(hm, w_v).astype(BF16)
    k_t[...] = tt(w_k, hm).astype(BF16)
    v_t[...] = tt(w_v, hm).astype(BF16)


def project_query(rows, win):
    return nn(rows, win[:, : rows.shape[1]]).astype(BF16).astype(F32) * HEAD_DIM ** (-0.5)


def attention_shapes(plan, rows, feature):
    length = plan.n_expert * rows
    return [
        ((length, feature), BF16),
        ((feature, length), BF16),
        ((length, feature), BF16),
        ((rows, feature), BF16),
        ((feature, rows), BF16),
        ((feature // HEAD_DIM, rows), F32),
    ]


def gather_rows(ids, col, returned):
    me = lax.axis_index("expert")
    total = None
    for r, rows in zip(ids, returned):
        slots = rows.shape[0] * rows.shape[1]
        local = col - xor(me, r) * slots
        hot = (local == lax.broadcasted_iota(jnp.int32, (col.shape[0], slots), 1)).astype(BF16)
        part = nn(hot, rows.reshape(slots, rows.shape[-1]))
        total = part if total is None else total + part
    return total


def fill_buffers(cap, col_of, token_of, sources, dest):
    experts = dest.shape[0]
    slots = experts * cap
    me = lax.axis_index("expert")
    for s in range(sources):
        for p in range(2):
            local = col_of(s, p) - me * slots
            hot = (local == lax.broadcasted_iota(jnp.int32, (slots, local.shape[1]), 0)).astype(BF16)
            rows = nn(hot, token_of(s, p)).astype(BF16)
            at = (2 * s + p) * cap
            for j in range(experts):
                dest[j, at : at + cap, :] = rows[j * cap : (j + 1) * cap]


def column(ref, s, layer, p):
    return ref[s, pl.ds(2 * layer + p, 1), :]


class Return:
    def __init__(self, ids, stage, ret, send_sems, recv_sems):
        self.ids, self.stage, self.ret, self.sems = ids, stage, ret, (send_sems, recv_sems)

    def copy(self, s, n):
        return send(
            self.stage.at[s, n], self.ret.at[s, n], self.sems[0].at[s, n], self.sems[1].at[s, n], (0, self.ids[s])
        )

    def put(self, j, rows, cap):
        for s in range(len(self.ids)):
            for p in range(2):
                at = (2 * s + p) * cap
                (self.ret if s == 0 else self.stage)[s, j, p] = rows[at : at + cap]

    def start(self, j):
        for s in range(1, len(self.ids)):
            self.copy(s, j).start()

    def finish(self, experts):
        for n in range(experts):
            for s in range(1, len(self.ids)):
                self.copy(s, n).wait()

    def rows(self, p):
        return [self.ret[s, :, p] for s in range(len(self.ids))]


def load(src, dst, sem):
    return pltpu.make_async_copy(src, dst, sem)


def self_forward(plan, source, target, cols, out_grad, gains, inward, outward, jobs):
    ids, count = plan.ids, plan.n_expert
    _, rows, feature = source.shape
    length = count * rows

    def body(bg, *refs):
        src, tgt, col, og, g, win_any, wout_any = refs[:7]
        enc, dec = refs[7:16], refs[16:25]
        u_near, og_near, col_near = refs[25:28]
        near_s, near_t, v_t, win, wout, lsem, *sems = refs[28:]
        weights = [load(win_any.at[n], win.at[n], lsem.at[n]) for n in range(2)]
        weights += [load(wout_any.at[n], wout.at[n], lsem.at[2 + n]) for n in range(2)]
        for w in weights:
            w.start()
        g_s, g_t, g_u, g_og, g_col = [
            Gather(ids, ref, sems[2 * n], sems[2 * n + 1])
            for n, ref in enumerate((near_s, near_t, u_near, og_near, col_near))
        ]
        near_s[0] = src[0]
        near_t[0] = tgt[0]
        col_near[0] = col[...]
        og_near[0] = og[...]
        bg.greet()
        g_s.start()
        g_t.start()
        g_col.start()
        bg.start()

        def attend(near, outs, n, gain, gain_next, allow, first, between):
            after, nxt, hm, k, k_t, v, q, o_t, lse = outs
            hm[0:rows, :] = norm(near[0].astype(F32), g[gain : gain + 1]).astype(BF16)
            if n == 0:
                for w in weights:
                    w.wait()
            q_scaled = project_query(hm[0:rows, :], win[n])
            q[...] = q_scaled.astype(BF16)
            first()
            for b in range(1, count):
                hm[b * rows : (b + 1) * rows, :] = norm(near[b].astype(F32), g[gain : gain + 1]).astype(BF16)
            project_rows(hm[...], win[n], k, k_t, v, v_t)
            attend_forward(q_scaled.T.astype(BF16), k, v_t, allow, o_t, lse, between)
            merged = o_t[...].astype(F32).T.astype(BF16)
            after[...] = near[0].astype(F32) + nn(merged, wout[n])
            nxt[...] = norm(after[...], g[gain_next : gain_next + 1]).astype(BF16)

        def first_enc():
            g_s.forward()
            g_s.finish()
            g_og.start()

        def mid_enc():
            g_t.forward()
            g_col.forward()

        attend(near_s, enc, 0, 0, 1, None, first_enc, mid_enc)
        u_near[0] = enc[1][...]
        g_u.start()

        def mid_dec():
            g_u.forward()
            g_og.forward()

        attend(near_t, dec, 1, 3, 4, causal_allow(ids, rows), g_t.finish, mid_dec)
        g_u.finish()
        g_og.finish()
        g_col.finish()
        bg.finish()

    shapes = [((rows, feature), F32), ((rows, feature), BF16), ((length, feature), BF16)]
    shapes += attention_shapes(plan, rows, feature)
    outs, fars = fused(
        plan,
        body,
        [source, target, cols, out_grad, gains, inward, outward],
        shapes
        + shapes
        + [
            ((count, rows, feature), BF16),
            ((count, 2, rows, feature), BF16),
            ((count,) + cols.shape, jnp.int32),
        ],
        "self_forward",
        cid=1,
        peers=expert_peers(ids),
        jobs=jobs,
        in_specs=[None] * 5 + [ANYWHERE] * 2,
        scratch=[
            pltpu.VMEM((count, rows, feature), BF16),
            pltpu.VMEM((count, rows, feature), BF16),
            pltpu.VMEM((feature, length), BF16),
            pltpu.VMEM((2, feature, 3 * feature), BF16),
            pltpu.VMEM((2, feature, feature), BF16),
            DMA((4,)),
        ]
        + [DMA((count,))] * 10,
        us=35,
    )
    return outs[:9], outs[9:18], outs[18:], fars


def return_scratch(plan, experts, cap, feature):
    shape = (plan.n_expert, experts, 2, cap, feature)
    return [pltpu.VMEM(shape, BF16), pltpu.VMEM(shape, BF16), DMA(shape[:2]), DMA(shape[:2])]


def expert_forward(plan, near, col_near, own_col, residual, gains, weight_up, weight_down, jobs):
    ids, count = plan.ids, plan.n_expert
    experts, hidden, feature = weight_up.shape
    rows = near.shape[1]
    cap = 2 * rows // EXPERTS
    length = count * 2 * cap

    def body(bg, u, col, mine, res, g, up, down, out, nxt, buf, *scratch):
        j = pl.program_id(0)
        back = Return(ids, *scratch)

        @pl.when(j == 0)
        def _():
            bg.greet()
            bg.start()
            fill_buffers(cap, lambda s, p: col[s, p : p + 1, :], lambda s, p: u[s], count, buf)

        act = gelu(nt(buf[j], up[0])).astype(BF16)
        back.put(j, nn(act, down[0]).astype(BF16), cap)
        back.start(j)

        @pl.when(j == experts - 1)
        def _():
            back.finish(experts)
            for p in range(2):
                after = res[...] + gather_rows(ids, mine[p], back.rows(p))
                out[p] = after
                nxt[p] = norm(after, g[2:3]).astype(BF16)
            bg.finish()

    weight = pl.BlockSpec((1, hidden, feature), lambda j: (j, 0, 0))
    return fused(
        plan,
        body,
        [near, col_near, own_col, residual, gains, weight_up, weight_down],
        [((2, rows, feature), F32), ((2, rows, feature), BF16)],
        "expert_forward",
        cid=2,
        peers=expert_peers(ids),
        jobs=jobs,
        grid=(experts,),
        in_specs=[None] * 5 + [weight, weight],
        scratch=[pltpu.VMEM((experts, length, feature), BF16)] + return_scratch(plan, experts, cap, feature),
        us=22,
    )


def cross_forward(plan, hc, mid, memory, gains, inward, outward, jobs):
    ids, count = plan.ids, plan.n_expert
    rows, feature = hc.shape
    length = count * rows

    def body(bg, h, res, mem, g, win_any, wout_any, t2, w, w_near, hm, k, k_t, v, q, o_t, lse, v_t, win, wout, lsem, *sems):
        weights = [load(win_any.at[2], win, lsem.at[0]), load(wout_any.at[2], wout, lsem.at[1])]
        for x in weights:
            x.start()
        gather_m = [Gather(ids, hm.at[p], sems[p].at[0], sems[p].at[1]) for p in range(2)]
        gather_w = [Gather(ids, w_near.at[p], sems[2 + p].at[0], sems[2 + p].at[1]) for p in range(2)]
        for p in range(2):
            hm[p, 0] = mem[p]
        bg.greet()
        gather_m[0].start()
        gather_m[1].start()
        for x in weights:
            x.wait()
        q_scaled = project_query(h[...], win[...])
        q[...] = q_scaled.astype(BF16)
        q_t = q_scaled.T.astype(BF16)
        gather_m[0].forward()
        gather_m[0].finish()
        bg.start()
        for p in range(2):
            project_rows(hm[p].reshape(length, feature), win[...], k.at[p], k_t.at[p], v.at[p], v_t)
            between = gather_m[1].forward if p == 0 else gather_w[0].forward
            attend_forward(q_t, k.at[p], v_t, None, o_t.at[p], lse.at[p], between)
            after = res[...] + nn(o_t[p].astype(F32).T.astype(BF16), wout[...])
            t2[p] = after
            nxt = norm(after, g[5:6]).astype(BF16)
            w[p] = nxt
            w_near[p, 0] = nxt
            gather_w[p].start()
            if p == 0:
                gather_m[1].finish()
        gather_w[1].forward()
        gather_w[0].finish()
        gather_w[1].finish()
        bg.finish()

    saved = attention_shapes(plan, rows, feature)
    saved = [((2,) + s, d) if n != 3 else (s, d) for n, (s, d) in enumerate(saved)]
    return fused(
        plan,
        body,
        [hc, mid, memory, gains, inward, outward],
        [
            ((2, rows, feature), F32),
            ((2, rows, feature), BF16),
            ((2, count, rows, feature), BF16),
            ((2, count, rows, feature), BF16),
        ]
        + saved,
        "cross_forward",
        cid=3,
        peers=expert_peers(ids),
        jobs=jobs,
        in_specs=[None] * 4 + [ANYWHERE] * 2,
        scratch=[
            pltpu.VMEM((feature, length), BF16),
            pltpu.VMEM((feature, 3 * feature), BF16),
            pltpu.VMEM((feature, feature), BF16),
            DMA((2,)),
        ]
        + [DMA((2, count))] * 4,
        us=35,
    )


def decoder_experts(plan, w_near, og_near, col_near, own_col, crossed, out_grad, gains, weight_up, weight_down, jobs):
    ids, count = plan.ids, plan.n_expert
    experts, hidden, feature = weight_up.shape
    rows = crossed.shape[1]
    cap = 2 * rows // EXPERTS
    length = count * 2 * cap

    def body(bg, w, og, col, mine, t2, og_own, g, up, down, upstream, dg, result, buf, gbuf, *scratch):
        j = pl.program_id(0)
        back = Return(ids, *scratch)

        @pl.when(j == 0)
        def _():
            bg.greet()
            bg.start()
            fill_buffers(cap, lambda s, p: col[s, 2 + p : 3 + p, :], lambda s, p: w[p, s], count, buf)
            fill_buffers(cap, lambda s, p: col[s, 2 + p : 3 + p, :], lambda s, p: og[s, p], count, gbuf)

        value, slope = gelu_both(nt(buf[j], up[0]))
        hidden_grad = (slope * nt(gbuf[j], down[0])).astype(BF16)
        back.put(j, nn(hidden_grad, up[0]).astype(BF16), cap)
        back.start(j)
        res = nn(value.astype(BF16), down[0]).astype(BF16)
        for s in range(count):
            for p in range(2):
                at = (2 * s + p) * cap
                result[s, 0, p] = res[at : at + cap]

        @pl.when(j == experts - 1)
        def _():
            back.finish(experts)
            total = None
            for p in range(2):
                dw = gather_rows(ids, mine[p], back.rows(p))
                dx, gain = norm_back(t2[p], g[5:6], dw)
                upstream[p] = og_own[p] + dx
                total = gain if total is None else total + gain
            dg[...] = total
            bg.finish()

    weight = pl.BlockSpec((1, hidden, feature), lambda j: (j, 0, 0))
    return fused(
        plan,
        body,
        [w_near, og_near, col_near, own_col, crossed, out_grad, gains, weight_up, weight_down],
        [((2, rows, feature), F32), ((1, feature), F32), ((count, experts, 2, cap, feature), BF16)],
        "decoder_experts",
        cid=4,
        peers=expert_peers(ids),
        jobs=jobs,
        grid=(experts,),
        in_specs=[None] * 7 + [weight, weight],
        out_specs=[None, None, pl.BlockSpec((count, 1, 2, cap, feature), lambda j: (0, j, 0, 0, 0))],
        scratch=[pltpu.VMEM((experts, length, feature), BF16)] * 2 + return_scratch(plan, experts, cap, feature),
        us=30,
    )


def weight_grads(hq, hm, dq, dk, dv, o_t, d_branch):
    return [tn(hq, dq), tn(hm, dk), tn(hm, dv), nn(o_t, d_branch)]


def cross_backward(
    plan, upstream, result, own_col, crossed, final, hc, mid, gains, saved, inward, outward, jobs
):
    ids, count = plan.ids, plan.n_expert
    rows, feature = mid.shape
    length = count * rows
    experts, _, cap = result.shape[1:4]

    def body(bg, *refs):
        up, res_any, mine, t2, e2, h, t1, g = refs[:8]
        hm, k, k_t, v, q, o_t, lse, win_any, wout_any = refs[8:17]
        y, fg, fg_low, fg_near, dt1, dw, dg2, dg4 = refs[17:25]
        ret, dk, dv, dq_t, dw_acc, parts, got, win, wout, lsem, rs, rr, *sems = refs[25:]
        weights = [load(win_any.at[2], win, lsem.at[0]), load(wout_any.at[2], wout, lsem.at[1])]
        own = load(res_any.at[0], ret.at[0], lsem.at[2])
        for x in weights + [own]:
            x.start()
        scatter = [Scatter(ids, parts.at[p], got.at[p], sems[p].at[0], sems[p].at[1]) for p in range(2)]
        gather = [Gather(ids, fg_near.at[p], sems[2 + p].at[0], sems[2 + p].at[1]) for p in range(2)]

        def bring(s):
            return send(res_any.at[s], ret.at[s], rs.at[s], rr.at[s], (0, ids[s]))

        def memory_back(p):
            dx, gain = norm_back(e2[p], g[2:3], scatter[p].finish())
            fg[p] = dx
            fg_low[p] = dx.astype(BF16)
            fg_near[p, 0] = dx.astype(BF16)
            gather[p].start()
            if p == 0:
                dg2[...] = gain
            else:
                dg2[...] = dg2[...] + gain

        bg.greet()
        bg.start()
        for s in range(1, count):
            bring(s).start()
        for x in weights:
            x.wait()
        dh = None
        for p in range(2):
            d_branch = up[p].astype(BF16)
            do = nt(d_branch, wout[...]).astype(BF16)
            between = () if p == 0 else ((1, scatter[0].middle), (3, lambda: memory_back(0)))
            attend_backward(
                q[...], k.at[p], v.at[p], k_t.at[p], do, lse.at[p], None, dk, dv, dq_t, between
            )
            for b in range(count):
                span = slice(b * rows, (b + 1) * rows)
                part = nt(dk[span, :], win[:, feature : 2 * feature]) + nt(dv[span, :], win[:, 2 * feature :])
                parts[p, b] = part.astype(BF16)
            scatter[p].start()
            dq = dq_t[...].astype(F32).T.astype(BF16)
            back = nt(dq, win[:, :feature])
            dh = back if dh is None else dh + back
            if p == 1:
                scatter[1].middle()
                gather[0].forward()
            grads = weight_grads(
                h[...], hm[p].reshape(length, feature), dq, dk[...], dv[...], o_t[p], d_branch
            )
            for n, value in enumerate(grads):
                at = slice(n * feature, (n + 1) * feature)
                if p == 0:
                    dw_acc[:, at] = value
                else:
                    dw[:, at] = (dw_acc[:, at] + value).astype(BF16)
        memory_back(1)
        dx, gain = norm_back(t1[...], g[4:5], dh)
        dt1[...] = up[0] + up[1] + dx
        dg4[...] = gain
        own.wait()
        for s in range(1, count):
            bring(s).wait()
        gather[1].forward()
        for p in range(2):
            mixed = gather_rows(ids, mine[p], [ret[s, :, p] for s in range(count)])
            y[p] = (t2[p] + mixed).astype(BF16)
        gather[0].finish()
        gather[1].finish()
        bg.finish()

    block = (rows, feature)
    return fused(
        plan,
        body,
        [upstream, result, own_col, crossed, final, hc, mid, gains, *saved, inward, outward],
        [
            ((2,) + block, BF16),
            ((2,) + block, F32),
            ((2,) + block, BF16),
            ((2, count) + block, BF16),
            (block, F32),
            ((feature, 4 * feature), BF16),
            ((1, feature), F32),
            ((1, feature), F32),
        ],
        "cross_backward",
        cid=5,
        peers=expert_peers(ids),
        jobs=jobs,
        in_specs=[None, ANYWHERE] + [None] * 13 + [ANYWHERE] * 2,
        scratch=[
            pltpu.VMEM((count, experts, 2, cap, feature), BF16),
            pltpu.VMEM((length, feature), BF16),
            pltpu.VMEM((length, feature), BF16),
            pltpu.VMEM((feature, rows), BF16),
            pltpu.VMEM((feature, 4 * feature), F32),
            pltpu.VMEM((2, count) + block, BF16),
            pltpu.VMEM((2, count) + block, BF16),
            pltpu.VMEM((feature, 3 * feature), BF16),
            pltpu.VMEM((feature, feature), BF16),
            DMA((3,)),
            DMA((count,)),
            DMA((count,)),
        ]
        + [DMA((2, count))] * 4,
        us=45,
    )


def encoder_experts(plan, u_near, fg_near, col_near, own_col, attended, final_grad, gains, weight_up, weight_down, jobs):
    ids, count = plan.ids, plan.n_expert
    experts, hidden, feature = weight_up.shape
    rows = attended.shape[0]
    cap = 2 * rows // EXPERTS
    length = count * 2 * cap

    def body(bg, u, fgn, col, mine, e1, fg, g, up, down, de1, dg, buf, gbuf, *scratch):
        j = pl.program_id(0)
        back = Return(ids, *scratch)

        @pl.when(j == 0)
        def _():
            bg.greet()
            bg.start()
            fill_buffers(cap, lambda s, p: col[s, p : p + 1, :], lambda s, p: u[s], count, buf)
            fill_buffers(cap, lambda s, p: col[s, p : p + 1, :], lambda s, p: fgn[p, s], count, gbuf)

        _, slope = gelu_both(nt(buf[j], up[0]))
        hidden_grad = (slope * nt(gbuf[j], down[0])).astype(BF16)
        back.put(j, nn(hidden_grad, up[0]).astype(BF16), cap)
        back.start(j)

        @pl.when(j == experts - 1)
        def _():
            back.finish(experts)
            du = gather_rows(ids, mine[0], back.rows(0)) + gather_rows(ids, mine[1], back.rows(1))
            dx, gain = norm_back(e1[...], g[1:2], du)
            de1[...] = fg[0] + fg[1] + dx
            dg[...] = gain
            bg.finish()

    weight = pl.BlockSpec((1, hidden, feature), lambda j: (j, 0, 0))
    return fused(
        plan,
        body,
        [u_near, fg_near, col_near, own_col, attended, final_grad, gains, weight_up, weight_down],
        [((rows, feature), F32), ((1, feature), F32)],
        "encoder_experts",
        cid=6,
        peers=expert_peers(ids),
        jobs=jobs,
        grid=(experts,),
        in_specs=[None] * 7 + [weight, weight],
        scratch=[pltpu.VMEM((experts, length, feature), BF16)] * 2 + return_scratch(plan, experts, cap, feature),
        us=30,
    )


def self_backward(plan, enc_up, dec_up, source, target, gains, enc_saved, dec_saved, inward, outward, jobs):
    ids, count = plan.ids, plan.n_expert
    _, rows, feature = source.shape
    length = count * rows

    def body(bg, *refs):
        ups, srcs, g = refs[:2], refs[2:4], refs[4]
        saved = (refs[5:12], refs[12:19])
        win_any, wout_any = refs[19:21]
        grads, dws, dgs = refs[21:23], refs[23:25], refs[25:27]
        dk, dv, dq_t, parts, got, win, wout, lsem, *sems = refs[27:]
        weights = [load(win_any.at[n], win.at[n], lsem.at[n]) for n in range(2)]
        weights += [load(wout_any.at[n], wout.at[n], lsem.at[2 + n]) for n in range(2)]
        for x in weights:
            x.start()
        scatter = [Scatter(ids, parts.at[n], got.at[n], sems[n].at[0], sems[n].at[1]) for n in range(2)]

        def finish(n):
            gain = 3 * n
            dx, dgain = norm_back(srcs[n][0].astype(F32), g[gain : gain + 1], scatter[n].finish())
            grads[n][...] = ups[n][...] + dx
            dgs[n][...] = dgain

        bg.greet()
        bg.start()
        for x in weights:
            x.wait()
        for n in range(2):
            hm, k, k_t, v, q, o_t, lse = saved[n]
            d_branch = ups[n][...].astype(BF16)
            do = nt(d_branch, wout[n]).astype(BF16)
            allow = causal_allow(ids, rows) if n == 1 else None
            between = () if n == 0 else ((1, scatter[0].middle), (3, lambda: finish(0)))
            attend_backward(q[...], k, v, k_t, do, lse, allow, dk, dv, dq_t, between)
            dq = dq_t[...].astype(F32).T.astype(BF16)
            for b in range(count):
                span = slice(b * rows, (b + 1) * rows)
                part = nt(dk[span, :], win[n, :, feature : 2 * feature])
                part = part + nt(dv[span, :], win[n, :, 2 * feature :])
                if b == 0:
                    part = part + nt(dq, win[n, :, :feature])
                parts[n, b] = part.astype(BF16)
            scatter[n].start()
            if n == 1:
                scatter[1].middle()
            for i, value in enumerate(
                weight_grads(hm[0:rows, :], hm[...], dq, dk[...], dv[...], o_t[...], d_branch)
            ):
                dws[n][:, i * feature : (i + 1) * feature] = value.astype(BF16)
        finish(1)
        bg.finish()

    block = (rows, feature)
    return fused(
        plan,
        body,
        [enc_up, dec_up, source, target, gains, *enc_saved, *dec_saved, inward, outward],
        [(block, F32)] * 2 + [((feature, 4 * feature), BF16)] * 2 + [((1, feature), F32)] * 2,
        "self_backward",
        cid=7,
        peers=expert_peers(ids),
        jobs=jobs,
        in_specs=[None] * 19 + [ANYWHERE] * 2,
        scratch=[
            pltpu.VMEM((length, feature), BF16),
            pltpu.VMEM((length, feature), BF16),
            pltpu.VMEM((feature, rows), BF16),
            pltpu.VMEM((2, count) + block, BF16),
            pltpu.VMEM((2, count) + block, BF16),
            pltpu.VMEM((2, feature, 3 * feature), BF16),
            pltpu.VMEM((2, feature, feature), BF16),
            DMA((4,)),
        ]
        + [DMA((2, count))] * 2,
        us=40,
    )


def transfers(plan, name, cid, jobs):
    def body(bg):
        bg.greet()
        bg.start()
        bg.finish()

    return fused(plan, body, [], [], name, cid=cid, jobs=jobs, us=30)[1]


def expert_weights(plan, place, layer, tokens, grads, cols, weight_up, weight_down):
    count, ny, nz = plan.n_expert, plan.ny, plan.nz
    experts, hidden, feature = weight_up.shape
    rows = tokens[0].shape[-2]
    cap = 2 * rows // EXPERTS
    sources = count * nz
    length = sources * 2 * cap
    span = hidden // (ny * nz)
    at = [(None, s) if s < count else (s // count - 1, s % count) for s in range(sources)]

    def body(place_ref, tn_, tf, gn, gf, cn, cf, up, down, up_out, down_out, buf, gbuf):
        @pl.when((pl.program_id(0) == 0) & (pl.program_id(1) == 0))
        def _():
            def col_of(s, p):
                z, i = at[s]
                row = slice(2 * layer + p, 2 * layer + p + 1)
                return cn[i, row, :] if z is None else cf[z, i, row, :]

            def token_of(s, p):
                z, i = at[s]
                if layer == 0:
                    return tn_[i] if z is None else tf[z, i]
                return tn_[p, i] if z is None else tf[z, i, p]

            def grad_of(s, p):
                z, i = at[s]
                if z is None:
                    return gn[p, i] if layer == 0 else gn[i, p]
                return gf[z, i, p]

            fill_buffers(cap, col_of, token_of, sources, buf)
            fill_buffers(cap, col_of, grad_of, sources, gbuf)

        j = pl.program_id(0)
        x, g = buf[j], gbuf[j]
        value, slope = gelu_both(nt(up[0], x))
        hidden_grad = (slope * nt(down[0], g)).astype(BF16)
        up_out[0, 0] = nn(hidden_grad, x).astype(BF16)
        down_out[0, 0] = nn(value.astype(BF16), g).astype(BF16)

    ins = [*tokens, *grads, *cols, weight_up, weight_down]
    weight = pl.BlockSpec((1, span, feature), lambda j, r, place_ref: (j, place_ref[0] * ny + (place_ref[1] ^ r), 0))
    out = pl.BlockSpec((1, 1, span, feature), lambda j, r, *_: (r, j, 0, 0))
    return pl.pallas_call(
        body,
        out_shape=[jax.ShapeDtypeStruct((ny, experts, span, feature), BF16)] * 2,
        grid_spec=pltpu.PrefetchScalarGridSpec(
            num_scalar_prefetch=1,
            grid=(experts, ny),
            in_specs=[vmem(a.shape) for a in ins[:6]] + [weight, weight],
            out_specs=[out, out],
            scratch_shapes=[pltpu.VMEM((experts, length, feature), BF16)] * 2,
        ),
        name="expert_weights",
        compiler_params=pltpu.CompilerParams(vmem_limit_bytes=VMEM_LIMIT),
        cost_estimate=pl.CostEstimate(flops=int(21 * 1.15e9), bytes_accessed=0, transcendentals=0),
    )(place, *ins)


AXES = ("dp", "expert")


def local(
    plan,
    source,
    target,
    attention_in,
    attention_out,
    gains,
    encoder_up,
    encoder_down,
    decoder_up,
    decoder_down,
    encoder_route,
    encoder_slot,
    decoder_route,
    decoder_slot,
    output_grad,
):
    _, rows, feature = source.shape
    cap = 2 * rows // EXPERTS
    n_dp, n_expert, ny = plan.n_dp, plan.n_expert, plan.ny
    dp = lax.axis_index("dp").astype(jnp.int32)
    place = jnp.stack([dp // ny, dp % ny])
    zr = plan.zr
    za, zb, zc = zr[0::3], zr[1::3], zr[2::3]
    weights = (attention_in, attention_out)

    cols = jnp.stack([encoder_route * cap + encoder_slot, decoder_route * cap + decoder_slot]).reshape(4, rows)
    own_cols = cols.reshape(2, 2, rows, 1)
    out_grad = output_grad.reshape(2, rows, feature)
    og = out_grad.astype(BF16)

    enc, dec, (u_near, og_near, col_near), (col_far, og_far) = self_forward(
        plan, source, target, cols, og, gains, *weights, [Job(cols, None, z=zr), Job(og, None, z=za + zb)]
    )
    e1, u, *enc_saved = enc
    t1, hc, *dec_saved = dec
    (e2, memory), (col_far, og_far) = expert_forward(
        plan,
        u_near,
        col_near,
        own_cols[0],
        e1,
        gains,
        encoder_up,
        encoder_down,
        [Job(None, col_far, x=zr), Job(og, og_far, z=zc, x=za)],
    )
    (t2, w, w_near, *cross_saved), (col_far, og_far, u_far) = cross_forward(
        plan, hc, t1, memory, gains, *weights, [Job(None, col_far, c=zr), Job(None, og_far, x=zb, c=za), Job(u, None, z=zr)]
    )
    (upstream, dg5, result), (og_far, w_far) = decoder_experts(
        plan,
        w_near,
        og_near,
        col_near,
        own_cols[1],
        t2,
        out_grad,
        gains,
        decoder_up,
        decoder_down,
        [Job(None, og_far, x=zc, c=zb), Job(w, None, z=zb + za)],
    )
    (decoder_output, fg, fg_low, fg_near, dt1, cross_dw, dg2, dg4), (og_far, w_far, u_far) = cross_backward(
        plan,
        upstream,
        result,
        own_cols[1],
        t2,
        e2,
        hc,
        t1,
        gains,
        cross_saved,
        *weights,
        [Job(None, og_far, c=zc), Job(w, w_far, z=zc), Job(None, u_far, x=zr)],
    )
    (de1, dg1), (w_far, u_far, fg_far) = encoder_experts(
        plan,
        u_near,
        fg_near,
        col_near,
        own_cols[0],
        e1,
        fg,
        gains,
        encoder_up,
        encoder_down,
        [Job(None, w_far, x=za), Job(None, u_far, c=zr), Job(fg_low, None, z=zr)],
    )
    (source_grad, target_grad, enc_dw, dec_dw, dg0, dg3), (w_far,) = self_backward(
        plan,
        de1,
        dt1,
        source,
        target,
        gains,
        enc_saved,
        dec_saved,
        *weights,
        [Job(None, w_far, x=zb + zc, c=za)],
    )
    w_far, fg_far = transfers(plan, "far_a", 8, [Job(None, w_far, c=zb + zc), Job(None, fg_far, x=zr)])
    dec_g = expert_weights(
        plan, place, 1, (w_near, w_far), (og_near, og_far), (col_near, col_far), decoder_up, decoder_down
    )
    (fg_far,) = transfers(plan, "far_b", 9, [Job(None, fg_far, c=zr)])
    enc_g = expert_weights(
        plan, place, 0, (u_near, u_far), (fg_near, fg_far), (col_near, col_far), encoder_up, encoder_down
    )

    def swap(value, d, e):
        pairs = []
        for i in range(n_dp):
            for k in range(n_expert):
                pairs.append((i * n_expert + k, (i ^ d) * n_expert + (k ^ e)))
        return lax.ppermute(value, AXES, pairs)

    def finish_weights(grads):
        blocks = [grads[i] for i in range(ny)]
        half = ny // 2
        while half >= 1:
            got = swap(jnp.concatenate([b[None] for b in blocks[half:]], axis=0), half, 0)
            if half == 1:
                return blocks[0].astype(F32) + got[0].astype(F32)
            blocks = [(blocks[i].astype(F32) + got[i].astype(F32)).astype(BF16) for i in range(half)]
            half //= 2

    counts = jnp.sum(
        (
            jnp.stack([encoder_route, decoder_route]).reshape(2, 2, rows, 1)
            == jnp.arange(EXPERTS, dtype=jnp.int32)
        ).astype(F32),
        axis=2,
    )
    gain_grads = jnp.concatenate([dg0, dg1, dg2, dg3, dg4, dg5], axis=0)
    dw = lax.psum(jnp.stack([enc_dw, dec_dw, cross_dw]), AXES).astype(F32)
    gain_grads, counts = lax.psum((gain_grads, counts), AXES)
    return (
        decoder_output.reshape(2, 1, rows, feature),
        source_grad[None],
        target_grad[None],
        dw[..., : 3 * feature],
        dw[..., 3 * feature :],
        gain_grads,
        finish_weights(enc_g[0]),
        finish_weights(enc_g[1]),
        finish_weights(dec_g[0]),
        finish_weights(dec_g[1]),
        counts.astype(jnp.int32),
    )


def solution(mesh):
    plan = Plan(mesh.shape["dp"], mesh.shape["expert"])
    in_specs = (
        P("dp", "expert", None),
        P("dp", "expert", None),
        P(),
        P(),
        P(),
        P("expert", None, None),
        P("expert", None, None),
        P("expert", None, None),
        P("expert", None, None),
        P(None, "dp", "expert"),
        P(None, "dp", "expert"),
        P(None, "dp", "expert"),
        P(None, "dp", "expert"),
        P(None, "dp", "expert", None),
    )
    out_specs = (
        P(None, "dp", "expert", None),
        P("dp", "expert", None),
        P("dp", "expert", None),
        P(),
        P(),
        P(),
        P("expert", "dp", None),
        P("expert", "dp", None),
        P("expert", "dp", None),
        P("expert", "dp", None),
        P(),
    )
    return jax.shard_map(
        functools.partial(local, plan),
        mesh=mesh,
        in_specs=in_specs,
        out_specs=out_specs,
        check_vma=False,
    )
```

time: 1360 us -> 606 us (0.45)
  waiting for transfers between devices: 872 us -> 14.8 us
  Pallas kernels: 0 us -> 407 us
  matrix products: 243 us -> 0 us
  blocking collectives: 41.9 us -> 115 us
  local copies, waits for them, and re-layouts: 83.6 us -> 20.3 us
  other arithmetic: 62.6 us -> 21.7 us
  starting transfers between devices: 31.7 us -> 4.15 us
    reduce_scatter x10 -> x0, waiting for transfers between devices: 531 us -> none  [the longest x1 150 us: local(): lax.psum_scatter(decoder_up_grad.astype(jnp.bfloat16), 'dp', scatter_dime...]
    pallas_call x0 -> x11, Pallas kernels: none -> 407 us  [the longest x9 365 us: fused(): pl.pallas_call(run, out_shape=[jax.ShapeDtypeStruct(s, d) for s, d in out...]
    dot_general x59 -> x0, matrix products: 243 us -> none  [the longest x3 21.8 us: core_backward(): jnp.einsum('bqhd,bkhd->bhqk', blended_grad, value_rows, preferred_element...]
    psum x1, waiting for transfers between devices: 234 us -> 14.8 us  [local(): dw = lax.psum(jnp.stack([enc_dw, dec_dw, cross_dw]), AXES).astype(F32)]
    psum x1, blocking collectives: 41.9 us -> 115 us  [local(): gain_grads, counts = lax.psum((gain_grads, counts), AXES)]
    all_to_all x8 -> x0, waiting for transfers between devices: 59.1 us -> none  [the longest x2 26 us: moe_forward(): lax.all_to_all(result, 'expert', split_axis=1, concat_axis=0, tiled=True)]
    all_gather x6 -> x0, waiting for transfers between devices: 47.6 us -> none  [the longest x3 25.4 us: attend(): lax.all_gather(key_rows, 'expert', axis=1, tiled=True)]
    unnamed x232 -> x38, local copies, waits for them, and re-layouts: 39.6 us -> 2.45 us
  transfers between devices with their start and end apart: 25 -> 5, of which waited for: 17 -> 1; matrix products, arithmetic and copies ran while one was open for 21% -> 4% of each run, Pallas kernels for 0% -> 4%
where the time goes in v3:
time: 606 us; the launch traced here: 597 us
  Pallas kernels  407 us (67%)
  blocking collectives  115 us (19%)
  other arithmetic  21.7 us (4%)
  local copies, waits for them, and re-layouts  20.3 us (3%)
  waiting for transfers between devices  14.8 us (2%)
  between operations  14.7 us (2%)
    pallas_call x9, Pallas kernels, fused(): pl.pallas_call(run, out_shape=[jax.ShapeDtypeStruct(s, d) for s, d in out...  365 us
    psum x1, blocking collectives, local(): gain_grads, counts = lax.psum((gain_grads, counts), AXES)  115 us
    pallas_call x2, Pallas kernels, expert_weights(): pl.pallas_call(body, out_shape=[jax.ShapeDtypeStruct((ny, experts, span,...  41.7 us
    psum x1, waiting for transfers between devices, local(): dw = lax.psum(jnp.stack([enc_dw, dec_dw, cross_dw]), AXES).astype(F32)  14.8 us
    add x4, other arithmetic, finish_weights(): return blocks[0].astype(F32) + got[0].astype(F32)  12.2 us
  transfers between devices with their start and end apart: 5, of which 1 were waited for; matrix products, arithmetic and copies ran while one was open for 4% of the time, Pallas kernels for 4%

profile of v3, /device:TPU:0, one launch (start us, length us, event | category | flops | bytes accessed | tf_op | source)
XLA Modules:
  0.0 597.1 jit_solution(9237896245370815327)
XLA Ops:
  7.2 0.8 fusion
  8.6 2.1 bitcast_convert_fusion.refs_3_.refs_8_
  10.7 0.8 squeeze.6.refs_2_.refs_3_
  11.5 0.8 squeeze.7.refs_3_.refs_2_
  12.4 45.3 %self_forward.1 = (f32[256,512]{1,0:T(8,128)}, bf16[256,512]{1,0:T(8,128)(2,1)}, bf16[1024,512]{1,0:T(8,128)(2,1)}, bf16[1024,512]{1,0:T(8,128)(2,1)}, bf16[512,...) custom-call(bf16[1,256,512]{2,1,0:T(8,128)(2,1)} %refs_2_.1, ...), custom_call_target="tpu_custom_call" | custom-call | flops 40249999360 | bytes 7356416 | tf_op jit(solution)/shard_map/self_forward/pallas_call | solution.py:281
  57.7 30.9 %expert_forward.1 = (f32[2,256,512]{2,1,0:T(8,128)}, bf16[2,256,512]{2,1,0:T(8,128)(2,1)}, s32[3,4,4,256]{3,2,1,0:T(4,128)}, bf16[3,4,2,256,512]{4,3,2,1,0:T(8,128)(2,1)}) custom-call(bf16[4,256,512]{2,1,0:T(8,128)(2,1)} %get-tuple-element.87.refs_0_.tn_, ...), custom_call_target="tpu_custom_call", output_to_operand_aliasing={{2}: (7, {}), {3}: (9, {})} | custom-call | flops 25300000768 | bytes 18380800 | tf_op jit(solution)/shard_map/expert_forward/pallas_call | solution.py:281
  88.7 50.1 %cross_forward.1 = (f32[2,256,512]{2,1,0:T(8,128)}, bf16[2,256,512]{2,1,0:T(8,128)(2,1)}, bf16[2,4,256,512]{3,2,1,0:T(8,128)(2,1)}, bf16[2,4,256,512]{3,2,1,0:T(...) custom-call(bf16[256,512]{1,0:T(8,128)(2,1)} %get-tuple-element.85.r, ...), custom_call_target="tpu_custom_call", output_to_operand_aliasing={{10}: (6, {}), {11}: (7, {})} | custom-call | flops 40249999360 | bytes 7614464 | tf_op jit(solution)/shard_map/cross_forward/pallas_call | solution.py:281
  138.7 32.2 %decoder_experts.1 = (f32[2,256,512]{2,1,0:T(8,128)}, f32[1,512]{1,0:T(1,128)}, bf16[4,4,2,32,512]{4,3,2,1,0:T(8,128)(2,1)}, bf16[3,4,2,256,512]{4,3,2,1,0:T(8,128)(2,1)}, bf16[3,4,2,256,512]{4,3,2,1,0:T(8,128)(2,1)}) custom-call(bf16[2,4,256,512]{3,2,1,0:T(8,128)(2,1)} %get-tuple-element.96.refs_0_.tn_, ...), custom_call_target="tpu_custom_call", output_to_operand_aliasing={{3}: (9, {})} | custom-call | flops 34500001792 | bytes 23099392 | tf_op jit(solution)/shard_map/decoder_experts/pallas_call | solution.py:281
  171.0 68.2 %cross_backward.1 = (bf16[2,256,512]{2,1,0:T(8,128)(2,1)}, f32[2,256,512]{2,1,0:T(8,128)}, bf16[2,256,512]{2,1,0:T(8,128)(2,1)}, bf16[2,4,256,512]{3,2,1,0:T(8,1...) custom-call(f32[2,256,512]{2,1,0:T(8,128)} %get-tuple-element.101.re, ...), custom_call_target="tpu_custom_call", output_to_operand_aliasing={{8}: (17, {}), {9}: (19, {}), {10}: (20, {})} | custom-call | flops 51749998592 | bytes 20477952 | tf_op jit(solution)/shard_map/cross_backward/pallas_call | solution.py:281
  239.2 44.0 %encoder_experts.1 = (f32[256,512]{1,0:T(8,128)}, f32[1,512]{1,0:T(1,128)}, bf16[3,4,2,256,512]{4,3,2,1,0:T(8,128)(2,1)}, bf16[3,4,256,512]{3,2,1,0:T(8,128)(2,1)}, bf16[3,4,2,256,512]{4,3,2,1,0:T(8,128)(2,1)}) custom-call(bf16[4,256,512]{2,1,0:T(8,128)(2,1)} %get-tuple-element.87.refs_0_.tn_, ...), custom_call_target="tpu_custom_call", output_to_operand_aliasing={{2}: (9, {}), {3}: (10, {})} | custom-call | flops 34500001792 | bytes 21526528 | tf_op jit(solution)/shard_map/encoder_experts/pallas_call | solution.py:281
  283.2 51.4 %self_backward.1 = (f32[256,512]{1,0:T(8,128)}, f32[256,512]{1,0:T(8,128)}, bf16[512,2048]{1,0:T(8,128)(2,1)}, bf16[512,2048]{1,0:T(8,128)(2,1)}, f32[1,512]{1,0...) custom-call(f32[256,512]{1,0:T(8,128)} %get-tuple-element.120.refs_0_, ...), custom_call_target="tpu_custom_call", output_to_operand_aliasing={{6}: (21, {})} | custom-call | flops 46000001024 | bytes 17330176 | tf_op jit(solution)/shard_map/self_backward/pallas_call | solution.py:281
  334.6 36.9 %far_a.1 = (bf16[3,4,2,256,512]{4,3,2,1,0:T(8,128)(2,1)}, bf16[3,4,2,256,512]{4,3,2,1,0:T(8,128)(2,1)}) custom-call(bf16[3,4,2,256,512]{4,3,2,1,0:T(8,128)(2,1)} %get-tuple-element.149.refs_0_, bf16[3,4,2,256,512]{4,3,2,1,0:T(8,128)(2,1)} %get-tuple-element.150.refs_1_), custom_call_target="tpu_custom_call", output_to_operand_aliasing={{0}: (0, {}), {1}: (1, {})} | custom-call | flops 34500001792 | tf_op jit(solution)/shard_map/far_a/pallas_call | solution.py:281
  372.1 21.3 %expert_weights.3 = (bf16[2,4,256,512]{3,2,1,0:T(8,128)(2,1)}, bf16[2,4,256,512]{3,2,1,0:T(8,128)(2,1)}) custom-call(s32[2]{0:T(128)} %pad_add_fusion.1.place_ref, bf16[2,4,256,512]{3,2,1,0:T(8,128)(2,1)} %get-tuple-element.96.refs_0_.tn_, bf16[3,4,2,256,512]{4,3,2,1,0:T(8,128)(2,1)} %get-tuple-element.155.tf, ...), custom_call_target="tpu_custom_call" | custom-call | flops 24149999616 | tf_op jit(solution)/shard_map/expert_weights/pallas_call | solution.py:1041
  393.3 2.4 slice.45
  395.8 1.5 collective-permute-start.3
  397.9 5.4 pad_maximum_fusion
  403.4 6.1 %far_b.1.gf = bf16[3,4,2,256,512]{4,3,2,1,0:T(8,128)(2,1)} custom-call(bf16[3,4,2,256,512]{4,3,2,1,0:T(8,128)(2,1)} %get-tuple-element.151.refs_0_), custom_call_target="tpu_custom_call", output_to_operand_aliasing={{}: (0, {})} | custom-call | flops 34500001792 | tf_op jit(solution)/shard_map/far_b/pallas_call | solution.py:281
  409.5 20.4 %expert_weights.2 = (bf16[2,4,256,512]{3,2,1,0:T(8,128)(2,1)}, bf16[2,4,256,512]{3,2,1,0:T(8,128)(2,1)}) custom-call(s32[2]{0:T(128)} %pad_add_fusion.1.place_ref, bf16[4,256,512]{2,1,0:T(8,128)(2,1)} %get-tuple-element.87.refs_0_.tn_, bf16[3,4,256,512]{3,2,1,0:T(8,128)(2,1)} %get-tuple-element.148.tf, ...), custom_call_target="tpu_custom_call" | custom-call | flops 24149999616 | tf_op jit(solution)/shard_map/expert_weights/pallas_call | solution.py:1041
  430.0 2.5 slice.41
  432.5 1.5 collective-permute-start.1
  434.0 1.0 slice.39
  435.8 114.5 %all-reduce = (f32[6,512]{1,0:T(8,128)}, f32[2,2,16]{2,1,0:T(2,128)S(1)}) all-reduce(f32[6,512]{1,0:T(8,128)S(1)} %concatenate.3, f32[2,2,16]{2,1,0:T(2,128)S(1)} %convert_reduce_fusion), channel_id=1, replica_groups=mesh['dp'=8,'expert'=4] {'dp','expert'}, use_global_device_ids=true, to_apply=%region_1.2 | all-reduce | flops 3136 | bytes 25088 | tf_op jit(solution)/shard_map/psum | solution.py:1197
  550.9 3.3 add_bitcast_fusion
  554.2 3.0 add_bitcast_fusion.1
  557.2 3.1 add_bitcast_fusion.2
  560.2 2.9 add_bitcast_fusion.3
  563.1 14.8 %all-reduce.3.cloned.1.call-done = bf16[3,512,2048]{2,1,0:T(8,128)(2,1)} async-done(((bf16[3,512,2048]{2,1,0:T(8,128)(2,1)}), bf16[3,512,2048]{2,1,0:T(8,128)(2,1)}) %all-reduce.3.cloned.1.call-update) | async-done | bytes 6291472 | tf_op jit(solution)/shard_map/psum | solution.py:1196
  577.9 7.6 %slice.46 = f32[3,512,1536]{2,1,0:T(8,128)} slice(bf16[3,512,2048]{2,1,0:T(8,128)(2,1)} %all-reduce.3.cloned.1.call-done), slice={[0:3], [0:512], [0:1536]} | slice | bytes 18874368 | tf_op jit(solution)/shard_map/slice | solution.py:1202
  585.4 2.0 slice.47
  587.4 0.8 copy.85
  588.2 0.8 copy.86
  589.0 0.8 copy.87
  (51 shorter events, 3.3 us)
Async XLA Ops:
  7.2 570.7 %all-reduce.3.cloned.1.call-start = ((), (), s32[]{:S(2)}) async-start(), calls=%async_computation | async-start | bytes 12582912 | tf_op jit(solution)/shard_map/psum | solution.py:1196
  393.3 4.0 copy-start.1
  393.3 4.6 copy-start.5
  395.8 155.1 %collective-permute-start.3 = (bf16[1,4,256,512]{3,2,1,0:T(8,128)(2,1)}, bf16[1,4,256,512]{3,2,1,0:T(8,128)(2,1)}, u32[]{:S(2)}, u32[]{:S(2)}) collective-permute-start(bf16[1,4,256,512]{3,2,1,0:T(8,128)(2,1)} %slice.45), channel_id=1, source_target_pairs={{0,4},{1,5},{2,6},{3,7},{4,0},{5,1},{6,2},{7,3},{8,12},{9,13},{10,... | collective-permute-start | bytes 3145736 | tf_op jit(solution)/shard_map/ppermute | solution.py:1176
  397.4 156.8 %collective-permute-start.2 = (bf16[1,4,256,512]{3,2,1,0:T(8,128)(2,1)S(1)}, bf16[1,4,256,512]{3,2,1,0:T(8,128)(2,1)}, u32[]{:S(2)}, u32[]{:S(2)}) collective-permute-start(bf16[1,4,256,512]{3,2,1,0:T(8,128)(2,1)S(1)} %slice.43), channel_id=1, source_target_pairs={{0,4},{1,5},{2,6},{3,7},{4,0},{5,1},{6,2},{7,3},{8,12},{9,13},{10,... | collective-permute-start | bytes 3145736 | tf_op jit(solution)/shard_map/ppermute | solution.py:1176
  430.0 4.0 copy-start.2
  430.0 5.6 copy-start.9
  430.0 5.6 copy-start.10
  430.0 5.7 copy-start.11
  430.0 5.7 copy-start.12
  430.0 5.7 copy-start.13
  430.0 5.7 copy-start.14
  430.0 5.7 copy-start.15
  430.0 5.7 copy-start.16
  432.5 124.7 %collective-permute-start.1 = (bf16[1,4,256,512]{3,2,1,0:T(8,128)(2,1)}, bf16[1,4,256,512]{3,2,1,0:T(8,128)(2,1)}, u32[]{:S(2)}, u32[]{:S(2)}) collective-permute-start(bf16[1,4,256,512]{3,2,1,0:T(8,128)(2,1)} %slice.41), channel_id=1, source_target_pairs={{0,4},{1,5},{2,6},{3,7},{4,0},{5,1},{6,2},{7,3},{8,12},{9,13},{10,... | collective-permute-start | bytes 3145736 | tf_op jit(solution)/shard_map/ppermute | solution.py:1176
  435.0 125.2 %collective-permute-start = (bf16[1,4,256,512]{3,2,1,0:T(8,128)(2,1)}, bf16[1,4,256,512]{3,2,1,0:T(8,128)(2,1)}, u32[]{:S(2)}, u32[]{:S(2)}) collective-permute-start(bf16[1,4,256,512]{3,2,1,0:T(8,128)(2,1)} %slice.39), channel_id=1, source_target_pairs={{0,4},{1,5},{2,6},{3,7},{4,0},{5,1},{6,2},{7,3},{8,12},{9,13},{10,... | collective-permute-start | bytes 3145736 | tf_op jit(solution)/shard_map/ppermute | solution.py:1176
  554.2 3.0 copy-start.4
  557.2 3.1 copy-start.3
  577.9 7.6 %copy-start = (bf16[3,512,2048]{2,1,0:T(8,128)(2,1)S(1)}, bf16[3,512,2048]{2,1,0:T(8,128)(2,1)}, u32[]{:S(2)}) copy-start(bf16[3,512,2048]{2,1,0:T(8,128)(2,1)} %all-reduce.3.cloned.1.call-done) | copy-start | bytes 18874372
  585.4 2.0 copy-start.6
  585.4 2.8 copy-start.8
  587.4 1.6 copy-start.7
Sparse Core Ops, SparseCore 0:
  403.5 174.3 all-reduce.2

commit v4 on v3

v4 whole, which is shorter than its diff:
```python
import functools

import jax
import jax.numpy as jnp
from jax import lax
from jax.experimental import pallas as pl
from jax.experimental.pallas import tpu as pltpu
from jax.sharding import PartitionSpec as P

HEAD_DIM = 64
EXPERTS = 16
NORM_EPSILON = 1e-05
MASKED = -1e30
F32 = jnp.float32
BF16 = jnp.bfloat16
VMEM_LIMIT = 60 << 20
MESH = pl.DeviceIdType.MESH
DMA = pltpu.SemaphoreType.DMA


def nn(a, b):
    return jnp.dot(a, b, preferred_element_type=F32)


def nt(a, b):
    return lax.dot_general(a, b, (((1,), (1,)), ((), ())), preferred_element_type=F32)


def tn(a, b):
    return lax.dot_general(a, b, (((0,), (0,)), ((), ())), preferred_element_type=F32)


def tt(a, b):
    return lax.dot_general(a, b, (((0,), (1,)), ((), ())), preferred_element_type=F32)


def norm_parts(x):
    mean = jnp.mean(x, axis=-1, keepdims=True)
    centered = x - mean
    spread = jnp.mean(centered * centered, axis=-1, keepdims=True)
    scale = lax.rsqrt(spread + NORM_EPSILON)
    return centered * scale, scale


def norm(x, gain):
    return norm_parts(x)[0] * gain


def norm_back(x, gain, grad):
    hat, scale = norm_parts(x)
    inner = grad * gain
    dx = scale * (
        inner
        - jnp.mean(inner, axis=-1, keepdims=True)
        - hat * jnp.mean(inner * hat, axis=-1, keepdims=True)
    )
    return dx, jnp.sum(grad * hat, axis=0, keepdims=True)


NORM_ROWS = 64


def norm_rows(src, dst, gain):
    for at in range(0, src.shape[0], NORM_ROWS):
        span = slice(at, at + NORM_ROWS)
        dst[span, :] = norm(src[span, :].astype(F32), gain).astype(dst.dtype)


def norm_back_rows(x, gain, grad, store):
    total = None
    for at in range(0, x.shape[0], NORM_ROWS):
        span = slice(at, at + NORM_ROWS)
        dx, part = norm_back(x[span, :].astype(F32), gain, grad[span, :].astype(F32))
        store(span, dx)
        total = part if total is None else total + part
    return total


GELU_A = 0.7978845608028654
GELU_B = 0.044715


def gelu(x):
    return 0.5 * x * (1.0 + jnp.tanh(x * (GELU_A + (GELU_A * GELU_B) * (x * x))))


def gelu_both(x):
    sq = x * x
    th = jnp.tanh(x * (GELU_A + (GELU_A * GELU_B) * sq))
    half = 0.5 * (1.0 + th)
    slope = half + (0.5 * x) * (1.0 - th * th) * (GELU_A + (3.0 * GELU_A * GELU_B) * sq)
    return x * half, slope


WIDE = 256
TALL = 64


def gelu_pair(raw, grad, act, slopes):
    for at in range(0, raw.shape[0], TALL):
        span = slice(at, at + TALL)
        value, slope = gelu_both(raw[span])
        if act is not None:
            act[span, :] = value.astype(BF16)
        slopes[span, :] = (slope * grad[span]).astype(BF16)


def xor(value, bits):
    b = 1
    while b <= bits:
        if bits & b:
            value = value + b * (1 - 2 * lax.rem(lax.div(value, b), 2))
        b *= 2
    return value


def peer(to):
    return (xor(lax.axis_index("dp"), to[0]), xor(lax.axis_index("expert"), to[1]))


def send(src, dst, send_sem, recv_sem, to):
    return pltpu.make_async_remote_copy(
        src_ref=src, dst_ref=dst, send_sem=send_sem, recv_sem=recv_sem, device_id=peer(to), device_id_type=MESH
    )


def expert_peers(ids):
    return [(0, r) for r in ids[1:]]


class Gather:
    def __init__(self, ids, near, send_sems, recv_sems):
        self.pos = {r: i for i, r in enumerate(ids)}
        self.far = [r for r in ids if r % 2 == 0 and r > 0]
        self.near, self.sems = near, (send_sems, recv_sems)

    def copy(self, r, src, to):
        at = self.pos[r]
        return send(src, self.near.at[at], self.sems[0].at[at], self.sems[1].at[at], (0, to))

    def first(self, r):
        return self.copy(r, self.near.at[0], r)

    def second(self, r):
        return self.copy(r ^ 1, self.near.at[self.pos[r]], 1)

    def start(self):
        for r in self.far:
            self.first(r).start()
        self.first(1).start()

    def forward(self):
        for r in self.far:
            self.first(r).wait_recv()
            self.second(r).start()

    def finish(self):
        for r in self.far:
            self.second(r).wait_recv()
        self.first(1).wait_recv()
        for r in self.far:
            self.first(r).wait_send()
            self.second(r).wait_send()
        self.first(1).wait_send()


class Scatter:
    def __init__(self, ids, parts, got, send_sems, recv_sems):
        self.pos = {r: i for i, r in enumerate(ids)}
        self.odd = [r for r in ids if r % 2]
        self.even = [r for r in ids if r % 2 == 0]
        self.parts, self.got, self.sems = parts, got, (send_sems, recv_sems)

    def copy(self, r, to):
        at = self.pos[r]
        return send(
            self.parts.at[at], self.got.at[self.pos[r ^ 1]], self.sems[0].at[at], self.sems[1].at[at], (0, to)
        )

    def start(self):
        for r in self.odd:
            self.copy(r, 1).start()

    def middle(self):
        for r in self.odd:
            self.copy(r, 1).wait_recv()
        for r in self.even[1:]:
            at = self.pos[r]
            self.parts[at] = (self.parts[at].astype(F32) + self.got[at].astype(F32)).astype(BF16)
            self.copy(r, r).start()

    def finish(self):
        total = self.parts[0].astype(F32) + self.got[0].astype(F32)
        for r in self.even[1:]:
            self.copy(r, r).wait_recv()
            total = total + self.got[self.pos[r ^ 1]].astype(F32)
        for r in self.odd:
            self.copy(r, 1).wait_send()
        for r in self.even[1:]:
            self.copy(r, r).wait_send()
        return total


class Job:
    def __init__(self, own, far, z=(), x=(), c=(), s=(), then_x=(), then_c=(), near=None, by_pass=False):
        self.own, self.far, self.z, self.x, self.c, self.s = own, far, list(z), list(x), list(c), list(s)
        self.then_x, self.then_c, self.near, self.by_pass = list(then_x), list(then_c), near, by_pass

    def inputs(self):
        return ([self.own] if self.z else []) + ([self.near] if self.s else [])

    def shape(self, plan):
        return (plan.nz - 1, plan.n_expert) + self.own.shape

    def moves(self, plan, refs, far):
        for zr in self.z:
            yield "z", zr, refs[0], far.at[zr - 1, 0], (zr * plan.ny, 0)
        for zr in self.s:
            for r in plan.across:
                at = plan.pos[r]
                if self.by_pass:
                    for p in range(2):
                        yield "s", zr, refs[-1].at[p, at], far.at[zr - 1, at, p], (zr * plan.ny, 0)
                else:
                    yield "s", zr, refs[-1].at[at], far.at[zr - 1, at], (zr * plan.ny, 0)
        yield from self.steps("x", plan, far, self.x)
        yield from self.steps("c", plan, far, self.c)

    def steps(self, kind, plan, far, zrs):
        for zr in zrs:
            if kind == "x":
                for r in plan.across:
                    yield "x", zr, far.at[zr - 1, 0], far.at[zr - 1, plan.pos[r]], (0, r)
            else:
                for r in [0] + plan.across:
                    yield "c", zr, far.at[zr - 1, plan.pos[r]], far.at[zr - 1, plan.pos[r ^ 1]], (0, 1)

    def second(self, plan, refs, far):
        yield from self.steps("x", plan, far, self.then_x)
        yield from self.steps("c", plan, far, self.then_c)

    def targets(self, plan):
        return (
            [(zr * plan.ny, 0) for zr in self.z + self.s]
            + ([(0, r) for r in plan.across] if self.x or self.then_x else [])
            + ([(0, 1)] if self.c or self.then_c else [])
        )


class Swap:
    def __init__(self, own, paced=False):
        self.own, self.far, self.paced = own, None, paced

    def inputs(self):
        return [self.own]

    def shape(self, plan):
        return (plan.ny - 1,) + self.own.shape[1:]

    def moves(self, plan, refs, far):
        for r in range(1, plan.ny):
            for j in range(self.own.shape[1]):
                yield "p" if self.paced else "y", r, refs[0].at[r, j], far.at[r - 1, j], (r, 0)

    def second(self, plan, refs, far):
        return ()

    def targets(self, plan):
        return [(r, 0) for r in range(1, plan.ny)]


class Plan:
    def __init__(self, n_dp, n_expert):
        self.n_dp, self.n_expert = n_dp, n_expert
        self.ny = 2 if n_dp <= 8 else 4
        self.nz = n_dp // self.ny
        ids, bit = [0], n_expert // 2
        while bit >= 1:
            ids = ids + [i ^ bit for i in ids]
            bit //= 2
        self.ids = ids
        self.pos = {r: i for i, r in enumerate(ids)}
        self.across = [r for r in ids if r % 2 == 0 and r > 0]
        self.zr = list(range(1, self.nz))


class Background:
    def __init__(self, plan, jobs, owns, fars, send_sems, recv_sems, peers):
        self.plan, self.jobs, self.peers = plan, jobs, peers
        self.owns, self.fars, self.sems, self.began = owns, fars, (send_sems, recv_sems), False
        self.released = 0

    def copies(self):
        n = 0
        for job, own, far in zip(self.jobs, self.owns, self.fars):
            moves = [(False, m) for m in job.moves(self.plan, own, far)]
            moves += [(True, m) for m in job.second(self.plan, own, far)]
            for late, (kind, zr, src, dst, to) in moves:
                yield job, late, kind, zr, send(src, dst, self.sems[0].at[n], self.sems[1].at[n], to)
                n += 1

    def greet(self):
        barrier = pltpu.get_barrier_semaphore()
        for p in self.peers:
            pl.semaphore_signal(barrier, inc=1, device_id=peer(p), device_id_type=MESH)
        pl.semaphore_wait(barrier, len(self.peers))

    def start(self):
        for _, late, kind, _, copy in self.copies():
            if not late and kind != "p":
                copy.start()

    def release(self, n):
        paced = [copy for _, _, kind, _, copy in self.copies() if kind == "p"]
        for copy in paced[self.released : self.released + n]:
            copy.start()
        self.released += n

    def second(self):
        needs = [(job, zr) for job, late, _, zr, _ in self.copies() if late]
        for job, late, kind, zr, copy in self.copies():
            if not late and kind in "zx" and (job, zr) in needs:
                copy.wait_recv()
        for _, late, _, _, copy in self.copies():
            if late:
                copy.start()
        self.began = True

    def finish(self):
        if not self.began:
            self.second()
        self.release(sum(kind == "p" for _, _, kind, _, _ in self.copies()) - self.released)
        needs = [(job, zr) for job, late, _, zr, _ in self.copies() if late]
        for job, late, kind, zr, copy in self.copies():
            if not late and kind in "zx" and (job, zr) in needs:
                copy.wait_send()
            else:
                copy.wait()


class Blank:
    def __init__(self):
        self.at = self

    def __getitem__(self, at):
        return self


class AllReduce:
    LEAST = 16

    def __init__(self, plan, acc, groups, tmp, small, small_tmp, sems, small_sems, credits=None):
        self.acc, self.groups, self.tmp, self.small, self.small_tmp = acc, groups, tmp, small, small_tmp
        self.sems, self.small_sems, self.credits = sems, small_sems, credits
        self.orders = [[(0, 1)] + o for o in self.rotations(plan)]
        self.steps = len(self.orders[0])
        self.spans = [[(0, acc.shape[1])] for _ in groups]

    @staticmethod
    def rotations(plan):
        def powers(n):
            return [1 << i for i in range(n.bit_length() - 1)]

        x = [(0, 2 * b) for b in powers(plan.n_expert // 2)]
        y = [(b, 0) for b in powers(plan.ny)]
        z = [(plan.ny * b, 0) for b in powers(plan.nz)]
        return [x + y + z, y + z + x, z + x + y]

    @classmethod
    def tmp_rows(cls, plan, rows):
        total = 0
        for _ in range(1 + len(cls.rotations(plan)[0])):
            rows = max(rows // 2, cls.LEAST)
            total += rows
        return total

    @classmethod
    def peers(cls, plan):
        return [(0, 1)] + cls.rotations(plan)[0]

    @staticmethod
    def side(to):
        axis, bits = ("dp", to[0]) if to[0] else ("expert", to[1])
        return lax.rem(lax.div(lax.axis_index(axis), bits), 2)

    def halves(self, g, step):
        return self.spans[g][step][1] > self.LEAST

    def place(self, g, step):
        to = self.orders[g % 3][step]
        low, length = self.spans[g][step]
        if length <= self.LEAST:
            return to, low, low, length
        half = length // 2
        side = self.side(to)
        return to, low + (1 - side) * half, low + side * half, half

    def view(self, ref, g, low, length):
        index, first, width = self.groups[g]
        if not isinstance(low, int):
            low = pl.multiple_of(low, self.LEAST)
        return ref.at[index, pl.ds(low, length), pl.ds(first, width)]

    def offset(self, g, step):
        return sum(self.place(g, n)[3] for n in range(step))

    def reduce_copy(self, g, step):
        to, sent, _, length = self.place(g, step)
        dst = self.view(self.tmp, g, self.offset(g, step), length)
        return send(self.view(self.acc, g, sent, length), dst, self.sems.at[0, g, step], self.sems.at[1, g, step], to)

    def small_copy(self, step):
        to = self.orders[0][step]
        return send(
            self.small, self.small_tmp.at[step], self.small_sems.at[0, step], self.small_sems.at[1, step], to
        )

    def reduce_start(self, step):
        for g in range(len(self.groups)):
            self.reduce_copy(g, step).start()
        if self.small is not None:
            self.small_copy(step).start()

    def reduce_finish(self, step):
        for g in range(len(self.groups)):
            self.reduce_copy(g, step).wait()
            _, _, kept, length = self.place(g, step)
            mine = self.view(self.acc, g, kept, length)
            got = self.view(self.tmp, g, self.offset(g, step), length)
            mine[...] = (mine[...].astype(F32) + got[...].astype(F32)).astype(BF16)
            if self.halves(g, step):
                pl.semaphore_signal(
                    self.credits.at[g, step],
                    inc=1,
                    device_id=peer(self.orders[g % 3][step]),
                    device_id_type=MESH,
                )
            self.spans[g].append((kept, length))
        if self.small is not None:
            self.small_copy(step).wait()
            self.small[...] = self.small[...] + self.small_tmp[step]

    def spread_copy(self, g, step):
        to = self.orders[g % 3][step]
        low, length = self.spans[g][step + 1]
        mine = self.view(self.acc, g, low, length)
        return send(mine, mine, self.sems.at[2, g, step], self.sems.at[3, g, step], to)

    def spread(self, step, action):
        for g in range(len(self.groups)):
            if self.halves(g, step):
                copy = self.spread_copy(g, step)
                if action == "start":
                    pl.semaphore_wait(self.credits.at[g, step], 1)
                    copy.start()
                else:
                    copy.wait()

    def run(self):
        for step in range(self.steps):
            self.reduce_start(step)
            yield
            self.reduce_finish(step)
        for step in reversed(range(self.steps)):
            self.spread(step, "start")
            yield
            self.spread(step, "wait")


def vmem(shape):
    return pl.BlockSpec(shape, lambda *_: (0,) * len(shape))


ANYWHERE = pl.BlockSpec(memory_space=pl.ANY)


def fused(
    plan, body, ins, outs, name, cid=None, peers=(), jobs=(), grid=None, in_specs=None, out_specs=None, scratch=(), us=10
):
    whole = (lambda shape: pl.BlockSpec(memory_space=pltpu.VMEM)) if grid is None else vmem
    in_specs = [None] * len(ins) if in_specs is None else in_specs
    out_specs = [None] * len(outs) if out_specs is None else out_specs
    in_specs = [whole(a.shape) if s is None else s for a, s in zip(ins, in_specs)]
    out_specs = [whole(o[0]) if s is None else s for o, s in zip(outs, out_specs)]
    ins, outs, scratch = list(ins), list(outs), list(scratch)
    n_in, n_out, n_scratch = len(ins), len(outs), len(scratch)
    aliases, places, count, peers = {}, [], 0, list(peers)
    for k, job in enumerate(jobs):
        place = range(len(ins), len(ins) + len(job.inputs()))
        ins += job.inputs()
        in_specs += [ANYWHERE] * len(job.inputs())
        if job.far is not None:
            aliases[len(ins)] = n_out + k
            ins.append(job.far)
            in_specs.append(ANYWHERE)
            outs.append((job.far.shape, job.far.dtype))
        else:
            outs.append((job.shape(plan), job.own.dtype))
        out_specs.append(ANYWHERE)
        places.append(place)
        blank = [Blank(), Blank()]
        count += len(list(job.moves(plan, blank, Blank()))) + len(list(job.second(plan, blank, Blank())))
        peers += [p for p in dict.fromkeys(job.targets(plan)) if p not in peers]
    if jobs:
        scratch += [DMA((count,)), DMA((count,))]

    def run(*refs):
        i, o, s = refs[: len(ins)], refs[len(ins) : len(ins) + len(outs)], refs[len(ins) + len(outs) :]
        if cid is None:
            return body(*i, *o, *s)
        sems = s[n_scratch:] if jobs else (None, None)
        bg = Background(plan, jobs, [[i[n] for n in p] for p in places], o[n_out:], *sems, peers)
        body(bg, *i[:n_in], *o[:n_out], *s[:n_scratch])

    moved = sum(a.size * a.dtype.itemsize for a in ins[:n_in])
    extra = {} if grid is None else {"grid": grid}
    got = pl.pallas_call(
        run,
        out_shape=[jax.ShapeDtypeStruct(s, d) for s, d in outs],
        in_specs=in_specs,
        out_specs=out_specs,
        scratch_shapes=scratch,
        input_output_aliases=aliases,
        name=name,
        compiler_params=pltpu.CompilerParams(
            vmem_limit_bytes=VMEM_LIMIT, collective_id=cid, has_side_effects=cid is not None
        ),
        cost_estimate=pl.CostEstimate(flops=int(us * 1.15e9), bytes_accessed=moved, transcendentals=0),
        **extra,
    )(*ins)
    return got[:n_out], got[n_out:]


CHUNK = 128


def zero_half(rows, half):
    zero = jnp.zeros_like(rows)
    return jnp.concatenate([rows, zero] if half == 0 else [zero, rows], axis=0)


def half_lanes(pair, half):
    lane = lax.broadcasted_iota(jnp.int32, pair.shape, 1)
    keep = lane < HEAD_DIM if half == 0 else lane >= HEAD_DIM
    return jnp.where(keep, pair, jnp.zeros_like(pair))


def fold(values, op):
    return op(values.reshape(values.shape[0] // 8, 8, values.shape[1]), axis=0)


def masked(scores, at, ids, rows):
    me = lax.axis_index("expert")
    first = xor(me, ids[at // rows]) * rows + at % rows
    key = first + lax.broadcasted_iota(jnp.int32, scores.shape, 0)
    query = me * rows + lax.broadcasted_iota(jnp.int32, scores.shape, 1)
    return jnp.where(key <= query, scores, MASKED)


def head_pairs(pairs, body, between):
    at = 0
    for stop, act in [*between, (pairs, None)]:
        if stop > at:
            lax.fori_loop(at, stop, lambda h2, _: (body(h2), 0)[1], 0)
            at = stop
        if act is not None:
            act()


def attend_forward(q_t, k, v_t, causal, o_t, lse, scratch, between=()):
    raw, low = scratch
    length = k.shape[0]

    def body(h2):
        first = pl.multiple_of(h2 * 128, 128)
        for half in range(2):
            rows = pl.ds(pl.multiple_of(h2 * 128 + half * HEAD_DIM, HEAD_DIM), HEAD_DIM)
            query = zero_half(q_t[rows, :], half)
            top = None
            for at in range(0, length, CHUNK):
                scores = nn(k[at : at + CHUNK, pl.ds(first, 128)], query)
                if causal is not None:
                    scores = masked(scores, at, *causal)
                raw[half, at : at + CHUNK, :] = scores
                part = fold(scores, jnp.max)
                top = part if top is None else jnp.maximum(top, part)
            top = jnp.max(top, axis=0, keepdims=True)
            total = None
            for at in range(0, length, CHUNK):
                lifted = jnp.exp(raw[half, at : at + CHUNK, :] - top)
                low[half, at : at + CHUNK, :] = lifted.astype(BF16)
                part = fold(lifted, jnp.sum)
                total = part if total is None else total + part
            total = jnp.sum(total, axis=0, keepdims=True)
            o_t[rows, :] = nn(v_t[rows, :], low[half]) * (1.0 / total)
            lse[pl.ds(2 * h2 + half, 1), :] = top + jnp.log(total)

    head_pairs(k.shape[1] // 128, body, between)


def attend_backward(q, k, v, k_t, do, o_t, lse, causal, dk, dv, dq_t, scratch, between=()):
    q_t, do_t, low = scratch
    length = k.shape[0]
    q_t[...] = q[...].astype(F32).T.astype(BF16)
    do_t[...] = do[...].astype(F32).T.astype(BF16)

    def body(h2):
        first = pl.multiple_of(h2 * 128, 128)
        pair = pl.ds(first, 128)
        q_pair, do_pair = q[:, pair], do[:, pair]
        parts = []
        for half in range(2):
            rows = pl.ds(pl.multiple_of(h2 * 128 + half * HEAD_DIM, HEAD_DIM), HEAD_DIM)
            do_rows = do_t[rows, :]
            centre = jnp.sum(do_rows.astype(F32) * o_t[rows, :], axis=0, keepdims=True)
            parts.append(
                (
                    rows,
                    zero_half(q_t[rows, :], half),
                    zero_half(do_rows, half),
                    half_lanes(q_pair, half),
                    half_lanes(do_pair, half),
                    lse[pl.ds(2 * h2 + half, 1), :],
                    centre,
                )
            )
        for at in range(0, length, CHUNK):
            span = slice(at, at + CHUNK)
            dk_pair = dv_pair = None
            for half, (_, q_row, do_row, q_lane, do_lane, total, centre) in enumerate(parts):
                scores = nn(k[span, pair], q_row)
                if causal is not None:
                    scores = masked(scores, at, *causal)
                weights = jnp.exp(scores - total)
                weights_grad = nn(v[span, pair], do_row)
                scores_grad = (weights * (weights_grad - centre)).astype(BF16)
                low[half, span, :] = scores_grad
                dv_part = nn(weights.astype(BF16), do_lane)
                dk_part = nn(scores_grad, q_lane)
                dv_pair = dv_part if dv_pair is None else dv_pair + dv_part
                dk_pair = dk_part if dk_pair is None else dk_pair + dk_part
            dk[span, pair] = dk_pair.astype(BF16)
            dv[span, pair] = dv_pair.astype(BF16)
        for half in range(2):
            rows = parts[half][0]
            dq_t[rows, :] = (nn(k_t[rows, :], low[half]) * HEAD_DIM ** (-0.5)).astype(BF16)

    head_pairs(k.shape[1] // 128, body, between)


def forward_scratch(plan, rows, feature):
    length = plan.n_expert * rows
    return [
        pltpu.VMEM((feature, rows), BF16),
        pltpu.VMEM((feature, length), BF16),
        pltpu.VMEM((2, length, rows), F32),
        pltpu.VMEM((2, length, rows), BF16),
    ]


def backward_scratch(plan, rows, feature):
    length = plan.n_expert * rows
    return [
        pltpu.VMEM((length, feature), BF16),
        pltpu.VMEM((length, feature), BF16),
        pltpu.VMEM((feature, rows), BF16),
        pltpu.VMEM((rows, feature), BF16),
        pltpu.VMEM((feature, rows), BF16),
        pltpu.VMEM((feature, rows), BF16),
        pltpu.VMEM((2, length, rows), BF16),
    ]


def project_rows(hm, win, k, k_t, v, v_t):
    feature = hm.shape[1]
    w_k, w_v = win[:, feature : 2 * feature], win[:, 2 * feature :]
    k[...] = nn(hm, w_k).astype(BF16)
    v[...] = nn(hm, w_v).astype(BF16)
    k_t[...] = tt(w_k, hm).astype(BF16)
    v_t[...] = tt(w_v, hm).astype(BF16)


def project_query(rows, win):
    return nn(rows, win[:, : rows.shape[1]]).astype(BF16).astype(F32) * HEAD_DIM ** (-0.5)


def attention_shapes(plan, rows, feature):
    length = plan.n_expert * rows
    return [
        ((length, feature), BF16),
        ((feature, length), BF16),
        ((length, feature), BF16),
        ((rows, feature), BF16),
        ((feature, rows), F32),
        ((feature // HEAD_DIM, rows), F32),
    ]


def gather_rows(ids, col, returned):
    me = lax.axis_index("expert")
    total = None
    for r, rows in zip(ids, returned):
        slots = rows.shape[0] * rows.shape[1]
        local = col - xor(me, r) * slots
        hot = (local == lax.broadcasted_iota(jnp.int32, (col.shape[0], slots), 1)).astype(BF16)
        part = nn(hot, rows.reshape(slots, rows.shape[-1]))
        total = part if total is None else total + part
    return total


def fill_buffers(cap, col_of, token_of, sources, dest):
    experts = dest.shape[0]
    slots = experts * cap
    me = lax.axis_index("expert")
    for s in sources:
        for p in range(2):
            local = col_of(s, p) - me * slots
            hot = (local == lax.broadcasted_iota(jnp.int32, (slots, local.shape[1]), 0)).astype(BF16)
            rows = nn(hot, token_of(s, p)).astype(BF16)
            at = (2 * s + p) * cap
            for j in range(experts):
                dest[j, at : at + cap, :] = rows[j * cap : (j + 1) * cap]


def column(ref, s, layer, p):
    return ref[s, pl.ds(2 * layer + p, 1), :]


class Return:
    def __init__(self, ids, stage, ret, send_sems, recv_sems):
        self.ids, self.stage, self.ret, self.sems = ids, stage, ret, (send_sems, recv_sems)

    def copy(self, s, n):
        return send(
            self.stage.at[s, n], self.ret.at[s, n], self.sems[0].at[s, n], self.sems[1].at[s, n], (0, self.ids[s])
        )

    def put(self, j, rows, cap):
        for s in range(len(self.ids)):
            for p in range(2):
                at = (2 * s + p) * cap
                (self.ret if s == 0 else self.stage)[s, j, p] = rows[at : at + cap]

    def start(self, j):
        for s in range(1, len(self.ids)):
            self.copy(s, j).start()

    def finish(self, experts):
        for n in range(experts):
            for s in range(1, len(self.ids)):
                self.copy(s, n).wait()

    def rows(self, p):
        return [self.ret[s, :, p] for s in range(len(self.ids))]


def load(src, dst, sem):
    return pltpu.make_async_copy(src, dst, sem)


def self_forward(plan, source, target, cols, out_grad, gains, inward, outward, jobs):
    ids, count = plan.ids, plan.n_expert
    _, rows, feature = source.shape
    length = count * rows

    def body(bg, *refs):
        src, tgt, col, og, g, win_any, wout_any = refs[:7]
        enc, dec = refs[7:16], refs[16:25]
        u_near, og_near, col_near = refs[25:28]
        near_s, near_t, win, wout, q_t, v_t, raw, low, lsem, *sems = refs[28:]
        weights = [load(win_any.at[n], win.at[n], lsem.at[n]) for n in range(2)]
        weights += [load(wout_any.at[n], wout.at[n], lsem.at[2 + n]) for n in range(2)]
        for w in weights:
            w.start()
        g_s, g_t, g_u, g_og, g_col = [
            Gather(ids, ref, sems[2 * n], sems[2 * n + 1])
            for n, ref in enumerate((near_s, near_t, u_near, og_near, col_near))
        ]
        near_s[0] = src[0]
        near_t[0] = tgt[0]
        col_near[0] = col[...]
        og_near[0] = og[...]
        bg.greet()
        g_s.start()
        g_t.start()
        g_col.start()
        bg.start()

        def attend(near, outs, n, gain, gain_next, causal, first, between):
            after, nxt, hm, k, k_t, v, q, o_t, lse = outs
            norm_rows(near.at[0], hm.at[0:rows], g[gain : gain + 1])
            if n == 0:
                for w in weights:
                    w.wait()
            q_scaled = project_query(hm[0:rows, :], win[n])
            q[...] = q_scaled.astype(BF16)
            first()
            for b in range(1, count):
                norm_rows(near.at[b], hm.at[b * rows : (b + 1) * rows], g[gain : gain + 1])
            project_rows(hm[...], win[n], k, k_t, v, v_t)
            q_t[...] = q_scaled.T.astype(BF16)
            attend_forward(q_t, k, v_t, causal, o_t, lse, (raw, low), [(2, between)])
            merged = o_t[...].T.astype(BF16)
            after[...] = near[0].astype(F32) + nn(merged, wout[n])
            norm_rows(after, nxt, g[gain_next : gain_next + 1])

        def first_enc():
            g_s.forward()
            g_s.finish()
            g_og.start()

        def mid_enc():
            g_t.forward()
            g_col.forward()

        attend(near_s, enc, 0, 0, 1, None, first_enc, mid_enc)
        u_near[0] = enc[1][...]
        g_u.start()

        def mid_dec():
            g_u.forward()
            g_og.forward()

        attend(near_t, dec, 1, 3, 4, (ids, rows), g_t.finish, mid_dec)
        g_u.finish()
        g_og.finish()
        g_col.finish()
        bg.finish()

    shapes = [((rows, feature), F32), ((rows, feature), BF16), ((length, feature), BF16)]
    shapes += attention_shapes(plan, rows, feature)
    outs, fars = fused(
        plan,
        body,
        [source, target, cols, out_grad, gains, inward, outward],
        shapes
        + shapes
        + [
            ((count, rows, feature), BF16),
            ((count, 2, rows, feature), BF16),
            ((count,) + cols.shape, jnp.int32),
        ],
        "self_forward",
        cid=1,
        peers=expert_peers(ids),
        jobs=jobs,
        in_specs=[None] * 5 + [ANYWHERE] * 2,
        scratch=[
            pltpu.VMEM((count, rows, feature), BF16),
            pltpu.VMEM((count, rows, feature), BF16),
            pltpu.VMEM((2, feature, 3 * feature), BF16),
            pltpu.VMEM((2, feature, feature), BF16),
            *forward_scratch(plan, rows, feature),
            DMA((4,)),
        ]
        + [DMA((count,))] * 10,
        us=35,
    )
    return outs[:9], outs[9:18], outs[18:], fars


def return_scratch(plan, experts, cap, feature):
    shape = (plan.n_expert, experts, 2, cap, feature)
    return [pltpu.VMEM(shape, BF16), pltpu.VMEM(shape, BF16), DMA(shape[:2]), DMA(shape[:2])]


def expert_forward(plan, near, col_near, own_col, residual, gains, weight_up, weight_down, jobs):
    ids, count = plan.ids, plan.n_expert
    experts, hidden, feature = weight_up.shape
    rows = near.shape[1]
    cap = 2 * rows // EXPERTS
    length = count * 2 * cap

    def body(bg, u, col, mine, res, g, up, down, out, nxt, buf, act, *scratch):
        j = pl.program_id(0)
        back = Return(ids, *scratch)

        @pl.when(j == 0)
        def _():
            bg.greet()
            bg.start()
            fill_buffers(cap, lambda s, p: col[s, p : p + 1, :], lambda s, p: u[s], range(count), buf)

        for at in range(0, hidden, WIDE):
            raw = nt(buf[j], up[0, at : at + WIDE])
            for n in range(0, length, TALL):
                act[n : n + TALL, at : at + WIDE] = gelu(raw[n : n + TALL]).astype(BF16)
        back.put(j, nn(act[...], down[0]).astype(BF16), cap)
        back.start(j)

        @pl.when(j == experts - 1)
        def _():
            back.finish(experts)
            for p in range(2):
                out[p] = res[...] + gather_rows(ids, mine[p], back.rows(p))
                norm_rows(out.at[p], nxt.at[p], g[2:3])
            bg.finish()

    weight = pl.BlockSpec((1, hidden, feature), lambda j: (j, 0, 0))
    return fused(
        plan,
        body,
        [near, col_near, own_col, residual, gains, weight_up, weight_down],
        [((2, rows, feature), F32), ((2, rows, feature), BF16)],
        "expert_forward",
        cid=2,
        peers=expert_peers(ids),
        jobs=jobs,
        grid=(experts,),
        in_specs=[None] * 5 + [weight, weight],
        scratch=[pltpu.VMEM((experts, length, feature), BF16), pltpu.VMEM((length, hidden), BF16)]
        + return_scratch(plan, experts, cap, feature),
        us=22,
    )


def cross_forward(plan, hc, mid, memory, gains, inward, outward, jobs):
    ids, count = plan.ids, plan.n_expert
    rows, feature = hc.shape
    length = count * rows

    def body(bg, h, res, mem, g, win_any, wout_any, t2, w, w_near, hm, k, k_t, v, q, o_t, lse, win, wout, q_t, v_t, raw, low, lsem, *sems):
        weights = [load(win_any.at[2], win, lsem.at[0]), load(wout_any.at[2], wout, lsem.at[1])]
        for x in weights:
            x.start()
        gather_m = [Gather(ids, hm.at[p], sems[p].at[0], sems[p].at[1]) for p in range(2)]
        gather_w = [Gather(ids, w_near.at[p], sems[2 + p].at[0], sems[2 + p].at[1]) for p in range(2)]
        for p in range(2):
            hm[p, 0] = mem[p]
        bg.greet()
        gather_m[0].start()
        gather_m[1].start()
        bg.start()
        for x in weights:
            x.wait()
        q_scaled = project_query(h[...], win[...])
        q[...] = q_scaled.astype(BF16)
        q_t[...] = q_scaled.T.astype(BF16)
        gather_m[0].forward()
        gather_m[0].finish()
        for p in range(2):
            project_rows(hm[p].reshape(length, feature), win[...], k.at[p], k_t.at[p], v.at[p], v_t)
            between = gather_m[1].forward if p == 0 else gather_w[0].forward
            attend_forward(q_t, k.at[p], v_t, None, o_t.at[p], lse.at[p], (raw, low), [(2, between)])
            t2[p] = res[...] + nn(o_t[p].T.astype(BF16), wout[...])
            norm_rows(t2.at[p], w_near.at[p, 0], g[5:6])
            w[p] = w_near[p, 0]
            gather_w[p].start()
            if p == 0:
                gather_m[1].finish()
        gather_w[1].forward()
        gather_w[0].finish()
        gather_w[1].finish()
        bg.finish()

    saved = attention_shapes(plan, rows, feature)
    saved = [((2,) + s, d) if n != 3 else (s, d) for n, (s, d) in enumerate(saved)]
    return fused(
        plan,
        body,
        [hc, mid, memory, gains, inward, outward],
        [
            ((2, rows, feature), F32),
            ((2, rows, feature), BF16),
            ((2, count, rows, feature), BF16),
            ((2, count, rows, feature), BF16),
        ]
        + saved,
        "cross_forward",
        cid=3,
        peers=expert_peers(ids),
        jobs=jobs,
        in_specs=[None] * 4 + [ANYWHERE] * 2,
        scratch=[
            pltpu.VMEM((feature, 3 * feature), BF16),
            pltpu.VMEM((feature, feature), BF16),
            *forward_scratch(plan, rows, feature),
            DMA((2,)),
        ]
        + [DMA((2, count))] * 4,
        us=35,
    )


def decoder_experts(plan, w_near, og_near, col_near, own_col, crossed, out_grad, gains, weight_up, weight_down, jobs):
    ids, count = plan.ids, plan.n_expert
    experts, hidden, feature = weight_up.shape
    rows = crossed.shape[1]
    cap = 2 * rows // EXPERTS
    length = count * 2 * cap

    def body(bg, w, og, col, mine, t2, og_own, g, up, down, upstream, dg, result, buf, gbuf, act, slopes, *scratch):
        j = pl.program_id(0)
        back = Return(ids, *scratch)

        @pl.when(j == 0)
        def _():
            bg.greet()
            bg.start()
            fill_buffers(cap, lambda s, p: col[s, 2 + p : 3 + p, :], lambda s, p: w[p, s], range(count), buf)
            fill_buffers(cap, lambda s, p: col[s, 2 + p : 3 + p, :], lambda s, p: og[s, p], range(count), gbuf)

        for at in range(0, hidden, WIDE):
            span = slice(at, at + WIDE)
            gelu_pair(nt(buf[j], up[0, span]), nt(gbuf[j], down[0, span]), act.at[:, span], slopes.at[:, span])
        back.put(j, nn(slopes[...], up[0]).astype(BF16), cap)
        back.start(j)
        res = nn(act[...], down[0]).astype(BF16)
        for s in range(count):
            for p in range(2):
                at = (2 * s + p) * cap
                result[s, 0, p] = res[at : at + cap]

        @pl.when(j == experts - 1)
        def _():
            bg.second()
            back.finish(experts)
            total = None
            for p in range(2):
                upstream[p] = gather_rows(ids, mine[p], back.rows(p))

                def store(span, dx):
                    upstream[p, span, :] = og_own[p, span, :] + dx

                gain = norm_back_rows(t2.at[p], g[5:6], upstream.at[p], store)
                total = gain if total is None else total + gain
            dg[...] = total
            bg.finish()

    weight = pl.BlockSpec((1, hidden, feature), lambda j: (j, 0, 0))
    return fused(
        plan,
        body,
        [w_near, og_near, col_near, own_col, crossed, out_grad, gains, weight_up, weight_down],
        [((2, rows, feature), F32), ((1, feature), F32), ((count, experts, 2, cap, feature), BF16)],
        "decoder_experts",
        cid=4,
        peers=expert_peers(ids),
        jobs=jobs,
        grid=(experts,),
        in_specs=[None] * 7 + [weight, weight],
        out_specs=[None, None, pl.BlockSpec((count, 1, 2, cap, feature), lambda j: (0, j, 0, 0, 0))],
        scratch=[pltpu.VMEM((experts, length, feature), BF16)] * 2
        + [pltpu.VMEM((length, hidden), BF16)] * 2
        + return_scratch(plan, experts, cap, feature),
        us=30,
    )


def weight_grads(hq, hm, dq, dk, dv, o_t, d_branch):
    return [tn(hq, dq), tn(hm, dk), tn(hm, dv), nn(o_t.astype(BF16), d_branch)]


def cross_backward(
    plan, upstream, final, hc, mid, gains, saved, inward, outward, jobs
):
    ids, count = plan.ids, plan.n_expert
    rows, feature = mid.shape
    length = count * rows

    def body(bg, *refs):
        up, e2, h, t1, g = refs[:5]
        hm, k, k_t, v, q, o_t, lse, win_any, wout_any = refs[5:14]
        fg, fg_low, fg_near, dt1, dw, dg2, dg4 = refs[14:21]
        dk, dv, dq_t, do, *work, dw_acc, parts, got, win, wout, lsem = refs[21:-4]
        sems = refs[-4:]
        weights = [load(win_any.at[2], win, lsem.at[0]), load(wout_any.at[2], wout, lsem.at[1])]
        for x in weights:
            x.start()
        scatter = [Scatter(ids, parts.at[p], got.at[p], sems[p].at[0], sems[p].at[1]) for p in range(2)]
        gather = [Gather(ids, fg_near.at[p], sems[2 + p].at[0], sems[2 + p].at[1]) for p in range(2)]

        def memory_back(p):
            fg[p] = scatter[p].finish()

            def store(span, dx):
                fg[p, span, :] = dx
                fg_low[p, span, :] = dx.astype(BF16)
                fg_near[p, 0, span, :] = dx.astype(BF16)

            gain = norm_back_rows(e2.at[p], g[2:3], fg.at[p], store)
            gather[p].start()
            if p == 0:
                dg2[...] = gain
            else:
                dg2[...] = dg2[...] + gain

        bg.greet()
        bg.start()
        for x in weights:
            x.wait()
        dh = None
        for p in range(2):
            d_branch = up[p].astype(BF16)
            do[...] = nt(d_branch, wout[...]).astype(BF16)
            between = () if p == 0 else ((1, scatter[0].middle), (2, lambda: memory_back(0)), (3, bg.second))
            attend_backward(
                q, k.at[p], v.at[p], k_t.at[p], do, o_t.at[p], lse.at[p], None, dk, dv, dq_t, work, between
            )
            for b in range(count):
                span = slice(b * rows, (b + 1) * rows)
                part = nt(dk[span, :], win[:, feature : 2 * feature]) + nt(dv[span, :], win[:, 2 * feature :])
                parts[p, b] = part.astype(BF16)
            scatter[p].start()
            dq = dq_t[...].astype(F32).T.astype(BF16)
            back = nt(dq, win[:, :feature])
            dh = back if dh is None else dh + back
            if p == 1:
                scatter[1].middle()
                gather[0].forward()
            grads = weight_grads(
                h[...], hm[p].reshape(length, feature), dq, dk[...], dv[...], o_t[p], d_branch
            )
            for n, value in enumerate(grads):
                at = slice(n * feature, (n + 1) * feature)
                if p == 0:
                    dw_acc[:, at] = value
                else:
                    dw[:, at] = (dw_acc[:, at] + value).astype(BF16)
        memory_back(1)
        dt1[...] = dh

        def store_mid(span, dx):
            dt1[span, :] = up[0, span, :] + up[1, span, :] + dx

        dg4[...] = norm_back_rows(t1, g[4:5], dt1, store_mid)
        gather[1].forward()
        gather[0].finish()
        gather[1].finish()
        bg.finish()

    block = (rows, feature)
    return fused(
        plan,
        body,
        [upstream, final, hc, mid, gains, *saved, inward, outward],
        [
            ((2,) + block, F32),
            ((2,) + block, BF16),
            ((2, count) + block, BF16),
            (block, F32),
            ((feature, 4 * feature), BF16),
            ((1, feature), F32),
            ((1, feature), F32),
        ],
        "cross_backward",
        cid=5,
        peers=expert_peers(ids),
        jobs=jobs,
        in_specs=[None] * 12 + [ANYWHERE] * 2,
        scratch=[
            *backward_scratch(plan, rows, feature),
            pltpu.VMEM((feature, 4 * feature), F32),
            pltpu.VMEM((2, count) + block, BF16),
            pltpu.VMEM((2, count) + block, BF16),
            pltpu.VMEM((feature, 3 * feature), BF16),
            pltpu.VMEM((feature, feature), BF16),
            DMA((2,)),
        ]
        + [DMA((2, count))] * 4,
        us=45,
    )


def encoder_experts(plan, u_near, fg_near, col_near, own_col, attended, final_grad, gains, weight_up, weight_down, jobs):
    ids, count = plan.ids, plan.n_expert
    experts, hidden, feature = weight_up.shape
    rows = attended.shape[0]
    cap = 2 * rows // EXPERTS
    length = count * 2 * cap

    def body(bg, u, fgn, col, mine, e1, fg, g, up, down, de1, dg, buf, gbuf, slopes, *scratch):
        j = pl.program_id(0)
        back = Return(ids, *scratch)

        @pl.when(j == 0)
        def _():
            bg.greet()
            bg.start()
            fill_buffers(cap, lambda s, p: col[s, p : p + 1, :], lambda s, p: u[s], range(count), buf)
            fill_buffers(cap, lambda s, p: col[s, p : p + 1, :], lambda s, p: fgn[p, s], range(count), gbuf)

        for at in range(0, hidden, WIDE):
            span = slice(at, at + WIDE)
            gelu_pair(nt(buf[j], up[0, span]), nt(gbuf[j], down[0, span]), None, slopes.at[:, span])
        back.put(j, nn(slopes[...], up[0]).astype(BF16), cap)
        back.start(j)

        @pl.when(j == experts - 1)
        def _():
            back.finish(experts)
            de1[...] = gather_rows(ids, mine[0], back.rows(0)) + gather_rows(ids, mine[1], back.rows(1))

            def store(span, dx):
                de1[span, :] = fg[0, span, :] + fg[1, span, :] + dx

            dg[...] = norm_back_rows(e1, g[1:2], de1, store)
            bg.finish()

    weight = pl.BlockSpec((1, hidden, feature), lambda j: (j, 0, 0))
    return fused(
        plan,
        body,
        [u_near, fg_near, col_near, own_col, attended, final_grad, gains, weight_up, weight_down],
        [((rows, feature), F32), ((1, feature), F32)],
        "encoder_experts",
        cid=6,
        peers=expert_peers(ids),
        jobs=jobs,
        grid=(experts,),
        in_specs=[None] * 7 + [weight, weight],
        scratch=[pltpu.VMEM((experts, length, feature), BF16)] * 2
        + [pltpu.VMEM((length, hidden), BF16)]
        + return_scratch(plan, experts, cap, feature),
        us=30,
    )


def column_groups(n_dw, width):
    if n_dw % 3 == 0:
        return [(n, 0, width) for n in range(n_dw)]
    cut = (width // 3) // 128 * 128
    groups = []
    for n in range(n_dw):
        groups += [(n, 0, cut), (n, cut, width - 2 * cut), (n, width - cut, cut)]
    return groups


def attention_back(plan, ids, n, up, saved, win, wout, work, parts, scatter, dw, causal, between, after):
    hm, k, k_t, v, q, o_t, lse = saved
    dk, dv, dq_t, do, *rest = work
    rows, feature = q.shape
    d_branch = up[...].astype(BF16)
    do[...] = nt(d_branch, wout[...]).astype(BF16)
    attend_backward(q, k, v, k_t, do, o_t, lse, causal, dk, dv, dq_t, rest, between)
    dq = dq_t[...].astype(F32).T.astype(BF16)
    for b in [i for i, r in enumerate(ids) if r % 2] + [i for i, r in enumerate(ids) if r % 2 == 0]:
        span = slice(b * rows, (b + 1) * rows)
        part = nt(dk[span, :], win[:, feature : 2 * feature]) + nt(dv[span, :], win[:, 2 * feature :])
        if b == 0:
            part = part + nt(dq, win[:, :feature])
        parts[b] = part.astype(BF16)
    scatter.start()
    after()
    for i, value in enumerate(
        weight_grads(hm[0:rows, :], hm[...], dq, dk[...], dv[...], o_t[...], d_branch)
    ):
        dw[:, i * feature : (i + 1) * feature] = value.astype(BF16)


def input_back(up, src, gain, scatter, grad):
    grad[...] = scatter.finish()

    def store(span, dx):
        grad[span, :] = up[span, :] + dx

    return norm_back_rows(src.at[0], gain, grad, store)


def attention_scratch(plan, rows, feature):
    count = plan.n_expert
    return [
        *backward_scratch(plan, rows, feature),
        pltpu.VMEM((count, rows, feature), BF16),
        pltpu.VMEM((count, rows, feature), BF16),
        pltpu.VMEM((feature, 3 * feature), BF16),
        pltpu.VMEM((feature, feature), BF16),
    ]


def decoder_backward(plan, dec_up, target, gains, saved, inward, outward, jobs):
    ids, count = plan.ids, plan.n_expert
    _, rows, feature = target.shape

    def body(bg, *refs):
        up, src, g = refs[:3]
        saved_refs, win_any, wout_any = refs[3:10], refs[10], refs[11]
        grad, dw, dg = refs[12:15]
        *work, parts, got, win, wout, lsem, sems = refs[15:]
        weights = [load(win_any.at[1], win, lsem.at[0]), load(wout_any.at[1], wout, lsem.at[1])]
        for x in weights:
            x.start()
        bg.greet()
        bg.start()
        for x in weights:
            x.wait()
        scatter = Scatter(ids, parts, got, sems.at[0], sems.at[1])
        attention_back(
            plan, ids, 1, up, saved_refs, win, wout, work, parts, scatter, dw, (ids, rows), (), lambda: None
        )
        scatter.middle()
        bg.second()
        dg[...] = input_back(up, src, g[3:4], scatter, grad)
        bg.finish()

    return fused(
        plan,
        body,
        [dec_up, target, gains, *saved, inward, outward],
        [((rows, feature), F32), ((feature, 4 * feature), BF16), ((1, feature), F32)],
        "decoder_backward",
        cid=7,
        peers=expert_peers(ids),
        jobs=jobs,
        in_specs=[None] * 10 + [ANYWHERE] * 2,
        scratch=attention_scratch(plan, rows, feature) + [DMA((2,)), DMA((2, count))],
        us=28,
    )


def encoder_backward(plan, enc_up, source, gains, saved, inward, outward, sums, small, jobs):
    ids, count = plan.ids, plan.n_expert
    _, rows, feature = source.shape
    width = 4 * feature
    groups = column_groups(1, width)
    steps = 1 + len(AllReduce.rotations(plan)[0])
    n_dw = len(sums) + 1

    def body(bg, *refs):
        up, src, g, sm = refs[:4]
        saved_refs, win_any, wout_any = refs[4:11], refs[11], refs[12]
        sums_any = refs[13 : 13 + n_dw - 1]
        grad, sum_out, small_out = refs[12 + n_dw : 15 + n_dw]
        *work, parts, got, win, wout, acc, tmp, small_tmp, lsem, asem, ssem, credits, sems = refs[15 + n_dw :]
        weights = [load(win_any.at[0], win, lsem.at[0]), load(wout_any.at[0], wout, lsem.at[1])]
        firsts = [load(ref, acc.at[n], lsem.at[2 + n]) for n, ref in enumerate(sums_any)]
        for x in weights + firsts:
            x.start()
        small_out[...] = sm[...]
        bg.greet()
        bg.start()

        def reduce(n):
            return AllReduce(
                plan, acc.at[n : n + 1], groups, tmp.at[n : n + 1], None, None, asem.at[n], None, credits.at[n]
            ).run()

        for x in firsts:
            x.wait()
        runs = [reduce(n) for n in range(n_dw - 1)]

        def step(release=1):
            for run in runs:
                next(run, None)
            bg.release(release)

        step(0)
        for x in weights:
            x.wait()
        scatter = Scatter(ids, parts, got, sems.at[0], sems.at[1])
        between = ((2, step),)
        attention_back(
            plan, ids, 0, up, saved_refs, win, wout, work, parts, scatter, acc.at[n_dw - 1], None, between, step
        )
        runs.append(reduce(n_dw - 1))
        step()
        scatter.middle()
        step(1)
        small_out[0:1, :] = input_back(up, src, g[0:1], scatter, grad)
        runs.append(AllReduce(plan, acc, [], None, small_out, small_tmp, None, ssem).run())
        for _ in range(2 * steps):
            step()
        last = load(acc, sum_out, lsem.at[0])
        last.start()
        last.wait()
        bg.finish()

    peers = expert_peers(ids)
    return fused(
        plan,
        body,
        [enc_up, source, gains, small, *saved, inward, outward, *sums],
        [((rows, feature), F32), ((n_dw, feature, width), BF16), (small.shape, F32)],
        "encoder_backward",
        cid=9,
        peers=peers + [p for p in AllReduce.peers(plan) if p not in peers],
        jobs=jobs,
        in_specs=[None] * 11 + [ANYWHERE] * (2 + len(sums)),
        out_specs=[None, ANYWHERE, None],
        scratch=attention_scratch(plan, rows, feature)
        + [
            pltpu.VMEM((n_dw, feature, width), BF16),
            pltpu.VMEM((n_dw, AllReduce.tmp_rows(plan, feature), width), BF16),
            pltpu.VMEM((steps,) + small.shape, F32),
            DMA((1 + n_dw,)),
            DMA((n_dw, 4, len(groups), steps)),
            DMA((2, steps)),
            pltpu.SemaphoreType.REGULAR((n_dw, len(groups), steps)),
            DMA((2, count)),
        ],
        us=90,
    )


def column_groups(n_dw, width):
    if n_dw % 3 == 0:
        return [(n, 0, width) for n in range(n_dw)]
    cut = (width // 3) // 128 * 128
    groups = []
    for n in range(n_dw):
        groups += [(n, 0, cut), (n, cut, width - 2 * cut), (n, width - cut, cut)]
    return groups


def self_backward(plan, enc_up, dec_up, source, target, gains, enc_saved, dec_saved, inward, outward, jobs):
    ids, count = plan.ids, plan.n_expert
    _, rows, feature = source.shape
    length = count * rows

    def body(bg, *refs):
        ups, srcs, g = refs[:2], refs[2:4], refs[4]
        saved = (refs[5:12], refs[12:19])
        win_any, wout_any = refs[19:21]
        grads, dws, dgs = refs[21:23], refs[23:25], refs[25:27]
        dk, dv, dq_t, do, *work, parts, got, win, wout, lsem = refs[27:-2]
        sems = refs[-2:]
        weights = [load(win_any.at[n], win.at[n], lsem.at[n]) for n in range(2)]
        weights += [load(wout_any.at[n], wout.at[n], lsem.at[2 + n]) for n in range(2)]
        for x in weights:
            x.start()
        scatter = [Scatter(ids, parts.at[n], got.at[n], sems[n].at[0], sems[n].at[1]) for n in range(2)]

        def finish(n):
            gain = 3 * n
            grads[n][...] = scatter[n].finish()

            def store(span, dx):
                grads[n][span, :] = ups[n][span, :] + dx

            dgs[n][...] = norm_back_rows(srcs[n].at[0], g[gain : gain + 1], grads[n], store)

        bg.greet()
        bg.start()
        for x in weights:
            x.wait()
        for n in range(2):
            hm, k, k_t, v, q, o_t, lse = saved[n]
            d_branch = ups[n][...].astype(BF16)
            do[...] = nt(d_branch, wout[n]).astype(BF16)
            causal = (ids, rows) if n == 1 else None
            between = () if n == 0 else ((0, bg.second), (1, scatter[0].middle), (3, lambda: finish(0)))
            attend_backward(q, k, v, k_t, do, o_t, lse, causal, dk, dv, dq_t, work, between)
            dq = dq_t[...].astype(F32).T.astype(BF16)
            for b in range(count):
                span = slice(b * rows, (b + 1) * rows)
                part = nt(dk[span, :], win[n, :, feature : 2 * feature])
                part = part + nt(dv[span, :], win[n, :, 2 * feature :])
                if b == 0:
                    part = part + nt(dq, win[n, :, :feature])
                parts[n, b] = part.astype(BF16)
            scatter[n].start()
            if n == 1:
                scatter[1].middle()
            for i, value in enumerate(
                weight_grads(hm[0:rows, :], hm[...], dq, dk[...], dv[...], o_t[...], d_branch)
            ):
                dws[n][:, i * feature : (i + 1) * feature] = value.astype(BF16)
        finish(1)
        bg.finish()

    block = (rows, feature)
    return fused(
        plan,
        body,
        [enc_up, dec_up, source, target, gains, *enc_saved, *dec_saved, inward, outward],
        [(block, F32)] * 2 + [((feature, 4 * feature), BF16)] * 2 + [((1, feature), F32)] * 2,
        "self_backward",
        cid=7,
        peers=expert_peers(ids),
        jobs=jobs,
        in_specs=[None] * 19 + [ANYWHERE] * 2,
        scratch=[
            *backward_scratch(plan, rows, feature),
            pltpu.VMEM((2, count) + block, BF16),
            pltpu.VMEM((2, count) + block, BF16),
            pltpu.VMEM((2, feature, 3 * feature), BF16),
            pltpu.VMEM((2, feature, feature), BF16),
            DMA((4,)),
        ]
        + [DMA((2, count))] * 2,
        us=40,
    )


def weight_sources(plan, layer, tokens, grads, cols):
    count = plan.n_expert

    def col_of(s, p):
        row = slice(2 * layer + p, 2 * layer + p + 1)
        return cols[0][s, row, :] if s < count else cols[1][s // count - 1, s % count, row, :]

    def token_of(s, p):
        if layer == 0:
            return tokens[0][s] if s < count else tokens[1][s // count - 1, s % count]
        return tokens[0][p, s] if s < count else tokens[1][s // count - 1, s % count, p]

    def grad_of(s, p):
        if s < count:
            return grads[0][p, s] if layer == 0 else grads[0][s, p]
        return grads[1][s // count - 1, s % count, p]

    return col_of, token_of, grad_of


def weight_products(up, down, buf, gbuf, act, slopes):
    for at in range(0, buf.shape[0], WIDE):
        span = slice(at, at + WIDE)
        gelu_pair(nt(up, buf[span, :]), nt(down, gbuf[span, :]), act.at[:, span], slopes.at[:, span])
    return nn(slopes[...], buf[...]).astype(BF16), nn(act[...], gbuf[...]).astype(BF16)


def expert_weights(plan, layer, cid, tokens, grads, cols, weight_up, weight_down, jobs, home=None):
    count, ny, nz, ids = plan.n_expert, plan.ny, plan.nz, plan.ids
    experts, hidden, feature = weight_up.shape
    rows = tokens[0].shape[-2]
    cap = 2 * rows // EXPERTS
    sources = count * nz
    length = sources * 2 * cap
    span = hidden // plan.n_dp
    block = ny * span

    def body(bg, *refs):
        cn, cf = refs[:2]
        if home is not None:
            mine, res = refs[2:4]
        big, up_any, down_any = refs[n_small : n_small + 4], refs[n_small + 4], refs[n_small + 5]
        outs = refs[n_in:]
        up_out, down_out = outs[:2]
        held, (up, down, buf, gbuf, act, slopes, lsem) = outs[n_out : n_out + 4], outs[n_out + 4 : n_out + 11]
        first = pl.multiple_of(lax.div(lax.axis_index("dp"), ny) * block, block)
        loads = [load(src, dst, lsem.at[n]) for n, (src, dst) in enumerate(zip(big, held))]
        loads.append(load(up_any.at[:, pl.ds(first, block)], up, lsem.at[4]))
        loads.append(load(down_any.at[:, pl.ds(first, block)], down, lsem.at[5]))
        for x in loads:
            x.start()
        bg.greet()
        if home is not None:
            ret, rs, rr = outs[n_out + 11 :]
            own = load(refs[n_in - 1].at[0], ret.at[0], lsem.at[6])
            own.start()
            bring = [
                send(refs[n_in - 1].at[s], ret.at[s], rs.at[s], rr.at[s], (0, ids[s])) for s in range(1, count)
            ]
            for x in bring:
                x.start()
        bg.start()
        col_of, token_of, grad_of = weight_sources(plan, layer, held[0:2], held[2:4], (cn, cf))
        for n, (reader, dest) in enumerate(((token_of, buf), (grad_of, gbuf))):
            loads[2 * n].wait()
            fill_buffers(cap, col_of, reader, range(count), dest)
            loads[2 * n + 1].wait()
            fill_buffers(cap, col_of, reader, range(count, sources), dest)
        loads[4].wait()
        loads[5].wait()
        y = lax.rem(lax.axis_index("dp"), ny)
        for r in reversed(range(ny)):
            at = pl.ds(pl.multiple_of(xor(y, r) * span, span), span)

            def product(j, _):
                up_out[r, j], down_out[r, j] = weight_products(
                    up[j, at, :], down[j, at, :], buf.at[j], gbuf.at[j], act, slopes
                )
                return 0

            lax.fori_loop(0, experts, product, 0)
        if home is not None:
            own.wait()
            for x in bring:
                x.wait()
            for p in range(2):
                mixed = gather_rows(ids, mine[p], [ret[s, :, p] for s in range(count)])
                outs[2][p] = (res[p] + mixed).astype(BF16)
        bg.finish()

    small = [*cols] + ([] if home is None else [home[1], home[2]])
    n_small = len(small)
    big = [tokens[0], tokens[1], grads[0], grads[1], weight_up, weight_down] + ([] if home is None else [home[0]])
    n_in = n_small + len(big)
    outs = [((ny, experts, span, feature), BF16)] * 2 + ([] if home is None else [((2, rows, feature), BF16)])
    n_out = len(outs)
    scratch = [pltpu.VMEM(a.shape, BF16) for a in big[:4]] + [
        pltpu.VMEM((experts, block, feature), BF16),
        pltpu.VMEM((experts, block, feature), BF16),
        pltpu.VMEM((experts, length, feature), BF16),
        pltpu.VMEM((experts, length, feature), BF16),
        pltpu.VMEM((span, length), BF16),
        pltpu.VMEM((span, length), BF16),
        DMA((7,)),
    ]
    if home is not None:
        scratch += [pltpu.VMEM(home[0].shape, BF16), DMA((count,)), DMA((count,))]
    return fused(
        plan,
        body,
        small + big,
        outs,
        ("encoder", "decoder")[layer] + "_weights",
        cid=cid,
        peers=[] if home is None else expert_peers(ids),
        jobs=jobs,
        in_specs=[None] * n_small + [ANYWHERE] * len(big),
        scratch=scratch,
        us=25,
    )


def finish(plan, sums, dec, dec_got, enc, enc_got):
    n_dw, feature, width = sums.shape
    _, experts, span, _ = enc[0].shape
    part = feature // experts
    ny = plan.ny

    def body(s, du, dd, dug, ddg, eu, ed, eug, edg, a_in, a_out, eu_out, ed_out, du_out, dd_out):
        for n in range(n_dw):
            a_in[n] = s[n_dw - 1 - n, :, : 3 * feature].astype(F32)
            a_out[n] = s[n_dw - 1 - n, :, 3 * feature :].astype(F32)
        for out, own, others in (
            (eu_out, eu[0, 0], [eug[r, 0] for r in range(ny - 1)]),
            (ed_out, ed[0, 0], [edg[r, 0] for r in range(ny - 1)]),
            (du_out, du[0, 0], [dug[r, 0] for r in range(ny - 1)]),
            (dd_out, dd[0, 0], [ddg[r, 0] for r in range(ny - 1)]),
        ):
            total = own.astype(F32)
            for other in others:
                total = total + other.astype(F32)
            out[0] = total

    block = (1, span, feature)
    first = pl.BlockSpec((1,) + block, lambda j: (0, j, 0, 0))
    others = pl.BlockSpec((ny - 1,) + block, lambda j: (0, j, 0, 0))
    own = pl.BlockSpec(block, lambda j: (j, 0, 0))
    return fused(
        plan,
        body,
        [sums, *dec, *dec_got, *enc, *enc_got],
        [((n_dw, feature, 3 * feature), F32), ((n_dw, feature, feature), F32)] + [((experts, span, feature), F32)] * 4,
        "finish",
        grid=(experts,),
        in_specs=[
            pl.BlockSpec((n_dw, part, width), lambda j: (0, j, 0)),
            first,
            first,
            others,
            others,
            first,
            first,
            others,
            others,
        ],
        out_specs=[
            pl.BlockSpec((n_dw, part, 3 * feature), lambda j: (0, j, 0)),
            pl.BlockSpec((n_dw, part, feature), lambda j: (0, j, 0)),
        ]
        + [own] * 4,
        us=10,
    )[0]


def local(
    plan,
    source,
    target,
    attention_in,
    attention_out,
    gains,
    encoder_up,
    encoder_down,
    decoder_up,
    decoder_down,
    encoder_route,
    encoder_slot,
    decoder_route,
    decoder_slot,
    output_grad,
):
    _, rows, feature = source.shape
    cap = 2 * rows // EXPERTS
    zr = plan.zr
    za, zb, zc = zr[0::3], zr[1::3], zr[2::3]
    weights = (attention_in, attention_out)

    cols = jnp.stack([encoder_route * cap + encoder_slot, decoder_route * cap + decoder_slot]).reshape(4, rows)
    own_cols = cols.reshape(2, 2, rows, 1)
    out_grad = output_grad.reshape(2, rows, feature)
    og = out_grad.astype(BF16)

    counts = jnp.sum(
        (
            jnp.stack([encoder_route, decoder_route]).reshape(4, rows, 1) == jnp.arange(EXPERTS, dtype=jnp.int32)
        ).astype(F32),
        axis=1,
    )

    enc, dec, (u_near, og_near, col_near), (col_far, og_far) = self_forward(
        plan, source, target, cols, og, gains, *weights, [Job(cols, None, z=zr), Job(og, None, z=za + zb)]
    )
    e1, u, *enc_saved = enc
    t1, hc, *dec_saved = dec
    (e2, memory), (col_far, og_far) = expert_forward(
        plan,
        u_near,
        col_near,
        own_cols[0],
        e1,
        gains,
        encoder_up,
        encoder_down,
        [Job(None, col_far, x=zr), Job(og, og_far, z=zc)],
    )
    (t2, w, w_near, *cross_saved), (col_far, og_far, u_far) = cross_forward(
        plan,
        hc,
        t1,
        memory,
        gains,
        *weights,
        [Job(None, col_far, c=zr), Job(None, og_far, s=za + zb, near=og_near), Job(u, None, z=zr)],
    )
    (upstream, dg5, result), (og_far, w_far) = decoder_experts(
        plan,
        w_near,
        og_near,
        col_near,
        own_cols[1],
        t2,
        out_grad,
        gains,
        decoder_up,
        decoder_down,
        [Job(None, og_far, c=za + zb, then_x=zc), Job(w, None, z=za + zb)],
    )
    (fg, fg_low, fg_near, dt1, cross_dw, dg2, dg4), (w_far, og_far, u_far) = cross_backward(
        plan,
        upstream,
        e2,
        hc,
        t1,
        gains,
        cross_saved,
        *weights,
        [
            Job(w, w_far, z=zc, s=za + zb, then_x=zc, near=w_near, by_pass=True),
            Job(None, og_far, c=zc),
            Job(None, u_far, x=zr),
        ],
    )
    (de1, dg1), (w_far, u_far, fg_far) = encoder_experts(
        plan,
        u_near,
        fg_near,
        col_near,
        own_cols[0],
        e1,
        fg,
        gains,
        encoder_up,
        encoder_down,
        [Job(None, w_far, c=zr), Job(None, u_far, c=zr), Job(fg_low, None, z=za + zb)],
    )
    dec_g, (fg_far,) = expert_weights(
        plan,
        1,
        8,
        (w_near, w_far),
        (og_near, og_far),
        (col_near, col_far),
        decoder_up,
        decoder_down,
        [Job(fg_low, fg_far, z=zc, x=za + zb)],
    )
    (target_grad, dec_dw, dg3), (fg_far, up_got) = decoder_backward(
        plan,
        dt1,
        target,
        gains,
        dec_saved,
        *weights,
        [Job(None, fg_far, x=zc, c=za + zb, then_c=zc), Swap(dec_g[0])],
    )
    (*enc_g, decoder_output), (down_got,) = expert_weights(
        plan,
        0,
        10,
        (u_near, u_far),
        (fg_near, fg_far),
        (col_near, col_far),
        encoder_up,
        encoder_down,
        [Swap(dec_g[1])],
        (result, own_cols[1], t2),
    )
    count_row = jnp.pad(counts.reshape(1, -1), ((0, 1), (0, feature - counts.size)))
    small = jnp.concatenate([jnp.zeros_like(dg1), dg1, dg2, dg3, dg4, dg5, count_row], axis=0)
    (source_grad, sums, small), enc_got = encoder_backward(
        plan,
        de1,
        source,
        gains,
        enc_saved,
        *weights,
        [cross_dw, dec_dw],
        small,
        [Swap(enc_g[0], paced=True), Swap(enc_g[1], paced=True)],
    )
    a_in, a_out, enc_up_g, enc_down_g, dec_up_g, dec_down_g = finish(
        plan, sums, dec_g, (up_got, down_got), enc_g, enc_got
    )
    return (
        decoder_output.reshape(2, 1, rows, feature),
        source_grad[None],
        target_grad[None],
        a_in,
        a_out,
        small[:6],
        enc_up_g,
        enc_down_g,
        dec_up_g,
        dec_down_g,
        small[6, : counts.size].reshape(2, 2, EXPERTS).astype(jnp.int32),
    )


def solution(mesh):
    plan = Plan(mesh.shape["dp"], mesh.shape["expert"])
    in_specs = (
        P("dp", "expert", None),
        P("dp", "expert", None),
        P(),
        P(),
        P(),
        P("expert", None, None),
        P("expert", None, None),
        P("expert", None, None),
        P("expert", None, None),
        P(None, "dp", "expert"),
        P(None, "dp", "expert"),
        P(None, "dp", "expert"),
        P(None, "dp", "expert"),
        P(None, "dp", "expert", None),
    )
    out_specs = (
        P(None, "dp", "expert", None),
        P("dp", "expert", None),
        P("dp", "expert", None),
        P(),
        P(),
        P(),
        P("expert", "dp", None),
        P("expert", "dp", None),
        P("expert", "dp", None),
        P("expert", "dp", None),
        P(),
    )
    return jax.shard_map(
        functools.partial(local, plan),
        mesh=mesh,
        in_specs=in_specs,
        out_specs=out_specs,
        check_vma=False,
    )
```

time: 606 us -> 485 us (0.80)
  blocking collectives: 115 us -> 0 us
  Pallas kernels: 407 us -> 471 us
  other arithmetic: 21.7 us -> 2.99 us
  waiting for transfers between devices: 14.8 us -> 0 us
  between operations: 14.7 us -> 1.08 us
  local copies, waits for them, and re-layouts: 20.3 us -> 6.72 us
    psum x1 -> x0, blocking collectives: 115 us -> none  [local(): gain_grads, counts = lax.psum((gain_grads, counts), AXES)]
    pallas_call x9 -> x11, Pallas kernels: 365 us -> 471 us  [fused(): pl.pallas_call(run, out_shape=[jax.ShapeDtypeStruct(s, d) for s, d in out...]
    pallas_call x2 -> x0, Pallas kernels: 41.7 us -> none  [expert_weights(): pl.pallas_call(body, out_shape=[jax.ShapeDtypeStruct((ny, experts, span,...]
    slice x6 -> x0, local copies, waits for them, and re-layouts: 15.5 us -> none  [the longest x1 7.56 us: local(): dw[..., :3 * feature]]
    psum x1 -> x0, waiting for transfers between devices: 14.8 us -> none  [local(): dw = lax.psum(jnp.stack([enc_dw, dec_dw, cross_dw]), AXES).astype(F32)]
    add x4 -> x0, other arithmetic: 12.2 us -> none  [finish_weights(): return blocks[0].astype(F32) + got[0].astype(F32)]
  transfers between devices with their start and end apart: 5 -> 0, of which waited for: 1 -> 0; matrix products, arithmetic and copies ran while one was open for 4% -> 0% of each run, Pallas kernels for 4% -> 0%
where the time goes in v4:
time: 485 us; the launch traced here: 482 us
  Pallas kernels  471 us (97%)
  local copies, waits for them, and re-layouts  6.72 us (1%)
    pallas_call x11, Pallas kernels, fused(): pl.pallas_call(run, out_shape=[jax.ShapeDtypeStruct(s, d) for s, d in out...  471 us

profile of v4, /device:TPU:0, one launch (start us, length us, event | category | flops | bytes accessed | tf_op | source)
XLA Modules:
  0.0 481.6 jit_solution(14087963619079114691)
XLA Ops:
  0.6 0.8 fusion
  1.4 0.6 reshape.43.refs_2_.refs_7_
  2.0 2.1 bitcast_convert_fusion.refs_3_.refs_8_
  4.1 45.2 %self_forward.1 = (f32[256,512]{1,0:T(8,128)}, bf16[256,512]{1,0:T(8,128)(2,1)}, bf16[1024,512]{1,0:T(8,128)(2,1)}, bf16[1024,512]{1,0:T(8,128)(2,1)}, bf16[512,...) custom-call(bf16[1,256,512]{2,1,0:T(8,128)(2,1)} %refs_1_.5, ...), custom_call_target="tpu_custom_call" | custom-call | flops 40249999360 | bytes 7356416 | tf_op jit(solution)/shard_map/self_forward/pallas_call | solution.py:517
  49.3 0.8 squeeze.10.refs_2_.refs_3_
  50.1 20.6 %expert_forward.1 = (f32[2,256,512]{2,1,0:T(8,128)}, bf16[2,256,512]{2,1,0:T(8,128)(2,1)}, s32[3,4,4,256]{3,2,1,0:T(4,128)}, bf16[3,4,2,256,512]{4,3,2,1,0:T(8,128)(2,1)}) custom-call(bf16[4,256,512]{2,1,0:T(8,128)(2,1)} %get-tuple-element.97.refs_0_.refs_4_, ...), custom_call_target="tpu_custom_call", output_to_operand_aliasing={{2}: (7, {}), {3}: (9, {})} | custom-call | flops 25300000768 | bytes 18380800 | tf_op jit(solution)/shard_map/expert_forward/pallas_call | solution.py:517
  70.7 59.4 %cross_forward.1 = (f32[2,256,512]{2,1,0:T(8,128)}, bf16[2,256,512]{2,1,0:T(8,128)(2,1)}, bf16[2,4,256,512]{3,2,1,0:T(8,128)(2,1)}, bf16[2,4,256,512]{3,2,1,0:T(...) custom-call(bf16[256,512]{1,0:T(8,128)(2,1)} %get-tuple-element.95.r, ...), custom_call_target="tpu_custom_call", output_to_operand_aliasing={{10}: (6, {}), {11}: (8, {})} | custom-call | flops 40249999360 | bytes 7614464 | tf_op jit(solution)/shard_map/cross_forward/pallas_call | solution.py:517
  130.2 0.8 squeeze.11.refs_3_.refs_2_
  131.0 38.0 %decoder_experts.1 = (f32[2,256,512]{2,1,0:T(8,128)}, f32[1,512]{1,0:T(1,128)}, bf16[4,4,2,32,512]{4,3,2,1,0:T(8,128)(2,1)}, bf16[3,4,2,256,512]{4,3,2,1,0:T(8,128)(2,1)}, bf16[3,4,2,256,512]{4,3,2,1,0:T(8,128)(2,1)}) custom-call(bf16[2,4,256,512]{3,2,1,0:T(8,128)(2,1)} %get-tuple-element.108.refs_0_.refs_15_.refs_2_, ...), custom_call_target="tpu_custom_call", output_to_operand_aliasing={{3}: (9, {})} | custom-call | flops 34500001792 | bytes 23099392 | tf_op jit(solution)/shard_map/decoder_experts/pallas_call | solution.py:517
  169.0 64.3 %cross_backward.1 = (f32[2,256,512]{2,1,0:T(8,128)}, bf16[2,256,512]{2,1,0:T(8,128)(2,1)}, bf16[2,4,256,512]{3,2,1,0:T(8,128)(2,1)}, f32[256,512]{1,0:T(8,128)},...) custom-call(f32[2,256,512]{2,1,0:T(8,128)} %get-tuple-element.111.re, ...), custom_call_target="tpu_custom_call", output_to_operand_aliasing={{7}: (16, {}), {8}: (17, {}), {9}: (18, {})} | custom-call | flops 51749998592 | bytes 18903040 | tf_op jit(solution)/shard_map/cross_backward/pallas_call | solution.py:517
  233.3 33.1 %encoder_experts.1 = (f32[256,512]{1,0:T(8,128)}, f32[1,512]{1,0:T(1,128)}, bf16[3,4,2,256,512]{4,3,2,1,0:T(8,128)(2,1)}, bf16[3,4,256,512]{3,2,1,0:T(8,128)(2,1)}, bf16[3,4,2,256,512]{4,3,2,1,0:T(8,128)(2,1)}) custom-call(bf16[4,256,512]{2,1,0:T(8,128)(2,1)} %get-tuple-element.97.refs_0_.refs_4_, ...), custom_call_target="tpu_custom_call", output_to_operand_aliasing={{2}: (9, {}), {3}: (10, {})} | custom-call | flops 34500001792 | bytes 21526528 | tf_op jit(solution)/shard_map/encoder_experts/pallas_call | solution.py:517
  266.4 29.1 %decoder_weights.1 = (bf16[2,4,256,512]{3,2,1,0:T(8,128)(2,1)}, bf16[2,4,256,512]{3,2,1,0:T(8,128)(2,1)}, bf16[3,4,2,256,512]{4,3,2,1,0:T(8,128)(2,1)}) custom-call(s32[4,4,256]{2,1,0:T(4,128)} %get-tuple-element.94.refs_1_.refs_2_.refs_0_, s32[3,4,4,256]{3,2,1,0:T(4,128)} %get-tuple-element.106.refs_1_, ...), custom_call_target="tpu_custom_call", output_to_operand_aliasing={{2}: (9, {})} | custom-call | flops 28750000128 | bytes 33619968 | tf_op jit(solution)/shard_map/decoder_weights/pallas_call | solution.py:517
  295.5 30.8 %decoder_backward.1 = (f32[256,512]{1,0:T(8,128)}, bf16[512,2048]{1,0:T(8,128)(2,1)}, f32[1,512]{1,0:T(1,128)}, bf16[3,4,2,256,512]{4,3,2,1,0:T(8,128)(2,1)}, bf16[1,4,256,512]{3,2,1,0:T(8,128)(2,1)}) custom-call(f32[256,512]{1,0:T(8,128)} %get-tuple-element.129.refs_0_, bf16[1,256,512]{2,1,0:T(8,128)(2,1)} %refs_1_.4, ...), custom_call_target="tpu_custom_call", output_to_operand_aliasing={{3}: (12, {})} | custom-call | flops 32199999488 | bytes 12079104 | tf_op jit(solution)/shard_map/decoder_backward/pallas_call | solution.py:517
  326.2 0.0 copy-start.4
  326.2 0.0 copy-start.5
  326.2 0.0 copy-start.6
  326.3 0.0 copy-start.7
  326.3 29.0 %encoder_weights.1 = (bf16[2,4,256,512]{3,2,1,0:T(8,128)(2,1)}, bf16[2,4,256,512]{3,2,1,0:T(8,128)(2,1)}, bf16[2,256,512]{2,1,0:T(8,128)(2,1)}, bf16[1,4,256,512]{3,2,1,0:T(8,128)(2,1)}) custom-call(s32[4,4,256]{2,1,0:T(4,128)} %get-tuple-element.94.refs_1_.refs_2_.refs_0_, s32[3,4,4,256]{3,2,1,0:T(4,128)} %get-tuple-element.106.refs_1_, ...), custom_call_target="tpu_custom_call" | custom-call | flops 28750000128 | bytes 31524864 | tf_op jit(solution)/shard_map/encoder_weights/pallas_call | solution.py:517
  355.3 0.0 copy-done.4
  355.3 0.0 copy-done.5
  355.4 0.1 convert_reduce_fusion
  355.5 0.1 reshape.46
  355.6 0.6 concatenate.3.refs_3_
  356.3 108.3 %encoder_backward.1 = (f32[256,512]{1,0:T(8,128)}, bf16[3,512,2048]{2,1,0:T(8,128)(2,1)}, f32[8,512]{1,0:T(8,128)}, bf16[1,4,256,512]{3,2,1,0:T(8,128)(2,1)}, bf16[1,4,256,512]{3,2,1,0:T(8,128)(2,1)}) custom-call(f32[256,512]{1,0:T(8,128)} %get-tuple-element.146.refs_0_, bf16[1,256,512]{2,1,0:T(8,128)(2,1)} %refs_1_.5, f32[6,512]{1,0:T(8,128)} %refs_2_.3, ...), custom_call_target="tpu_custom_call" | custom-call | flops 103499997184 | bytes 16289792 | tf_op jit(solution)/shard_map/encoder_backward/pallas_call | solution.py:517
  464.6 13.2 %finish.1 = (f32[3,512,1536]{2,1,0:T(8,128)}, f32[3,512,512]{2,1,0:T(8,128)}, f32[4,256,512]{2,1,0:T(8,128)}, f32[4,256,512]{2,1,0:T(8,128)}, f32[4,256,512]{2,1,0:T(8,128)}, /*index=5*/f32[4,256,512]{2,1,0:T(8,128)}) custom-call(bf16[3,512,2048]{2,1,0:T(8,128)(2,1)} %get-tuple-element.165.refs_0_, ...), custom_call_target="tpu_custom_call" | custom-call | flops 11500000256 | bytes 18874368 | tf_op jit(solution)/shard_map/finish/pallas_call | solution.py:517
  477.7 0.0 copy-done.3
  477.8 0.7 convert_element_type.17
  478.4 0.0 copy-done.1
  478.4 0.8 copy.79
  479.2 0.8 copy.80
  480.0 0.8 copy.81
  480.8 0.6 copy.82
  (20 shorter events, 0.1 us)
Async XLA Ops:
  326.2 29.1 %copy-start.4 = (s32[2,1,256]{2,1,0:T(1,128)S(1)}, s32[2,1,256]{2,1,0:T(1,128)}, u32[]{:S(2)}) copy-start(s32[2,1,256]{2,1,0:T(1,128)} %param.23) | copy-start | bytes 6148
  326.2 29.1 %copy-start.5 = (s32[2,1,256]{2,1,0:T(1,128)S(1)}, s32[2,1,256]{2,1,0:T(1,128)}, u32[]{:S(2)}) copy-start(s32[2,1,256]{2,1,0:T(1,128)} %param.25) | copy-start | bytes 6148
  326.2 29.3 %copy-start.6 = (f32[1,512]{1,0:T(1,128)S(1)}, f32[1,512]{1,0:T(1,128)}, u32[]{:S(2)}) copy-start(f32[1,512]{1,0:T(1,128)} %get-tuple-element.151) | copy-start | bytes 6148
  326.3 29.3 %copy-start.7 = (f32[1,512]{1,0:T(1,128)S(1)}, f32[1,512]{1,0:T(1,128)}, u32[]{:S(2)}) copy-start(f32[1,512]{1,0:T(1,128)} %get-tuple-element.148) | copy-start | bytes 6148
  326.3 29.3 %copy-start.8 = (f32[1,512]{1,0:T(1,128)S(1)}, f32[1,512]{1,0:T(1,128)}, u32[]{:S(2)}) copy-start(f32[1,512]{1,0:T(1,128)} %get-tuple-element.150) | copy-start | bytes 6148
  326.3 29.3 %copy-start.9 = (f32[1,512]{1,0:T(1,128)S(1)}, f32[1,512]{1,0:T(1,128)}, u32[]{:S(2)}) copy-start(f32[1,512]{1,0:T(1,128)} %get-tuple-element.147) | copy-start | bytes 6148
  326.3 29.3 %copy-start.10 = (f32[1,512]{1,0:T(1,128)S(1)}, f32[1,512]{1,0:T(1,128)}, u32[]{:S(2)}) copy-start(f32[1,512]{1,0:T(1,128)} %get-tuple-element.149) | copy-start | bytes 6148
  464.5 13.2 %copy-start.3 = (f32[8,512]{1,0:T(8,128)S(1)}, f32[8,512]{1,0:T(8,128)}, u32[]{:S(2)}) copy-start(f32[8,512]{1,0:T(8,128)} %get-tuple-element.172) | copy-start | bytes 49156
  464.6 13.9 %copy-start.1 = (bf16[2,256,512]{2,1,0:T(8,128)(2,1)S(1)}, bf16[2,256,512]{2,1,0:T(8,128)(2,1)}, u32[]{:S(2)}) copy-start(bf16[2,256,512]{2,1,0:T(8,128)(2,1)} %get-tuple-element.145) | copy-start | bytes 1572868
  464.6 14.7 %copy-start.2 = (f32[256,512]{1,0:T(8,128)S(1)}, f32[256,512]{1,0:T(8,128)}, u32[]{:S(2)}) copy-start(f32[256,512]{1,0:T(8,128)} %get-tuple-element.163) | copy-start | bytes 1572868
  464.6 15.5 %copy-start = (f32[256,512]{1,0:T(8,128)S(1)}, f32[256,512]{1,0:T(8,128)}, u32[]{:S(2)}) copy-start(f32[256,512]{1,0:T(8,128)} %get-tuple-element.164) | copy-start | bytes 1572868

commit v5 on v4

--- a/solution.py
+++ b/solution.py
@@ -202,48 +202,50 @@
 
 
 class Job:
-    def __init__(self, own, far, z=(), x=(), c=(), s=(), then_x=(), then_c=(), near=None, by_pass=False):
-        self.own, self.far, self.z, self.x, self.c, self.s = own, far, list(z), list(x), list(c), list(s)
-        self.then_x, self.then_c, self.near, self.by_pass = list(then_x), list(then_c), near, by_pass
+    def __init__(self, own, far, z=(), x=(), c=(), s=(), later=(), near=None, by_pass=False, local=False):
+        self.own, self.far, self.near, self.by_pass, self.local = own, far, near, by_pass, local
+        self.todo = [(0, "z", z), (0, "s", s), (0, "x", x), (0, "c", c), *later]
+
+    def has(self, kind):
+        return any(k == kind and len(zrs) > 0 for _, k, zrs in self.todo)
 
     def inputs(self):
-        return ([self.own] if self.z else []) + ([self.near] if self.s else [])
+        if self.local:
+            return []
+        return ([self.own] if self.has("z") else []) + ([self.near] if self.has("s") else [])
 
     def shape(self, plan):
         return (plan.nz - 1, plan.n_expert) + self.own.shape
 
     def moves(self, plan, refs, far):
-        for zr in self.z:
-            yield "z", zr, refs[0], far.at[zr - 1, 0], (zr * plan.ny, 0)
-        for zr in self.s:
-            for r in plan.across:
-                at = plan.pos[r]
-                if self.by_pass:
-                    for p in range(2):
-                        yield "s", zr, refs[-1].at[p, at], far.at[zr - 1, at, p], (zr * plan.ny, 0)
+        for stage, kind, zrs in self.todo:
+            for zr in zrs:
+                z = (zr * plan.ny, 0)
+                if kind == "z" and not self.local:
+                    yield stage, kind, zr, refs[0], far.at[zr - 1, 0], z
+                elif kind in "zs":
+                    for r in [0] if kind == "z" else plan.across:
+                        at = plan.pos[r]
+                        if self.by_pass:
+                            for p in range(2):
+                                yield stage, kind, zr, refs[-1].at[p, at], far.at[zr - 1, at, p], z
+                        else:
+                            yield stage, kind, zr, refs[-1].at[at], far.at[zr - 1, at], z
+                elif kind == "x":
+                    for r in plan.across:
+                        yield stage, kind, zr, far.at[zr - 1, 0], far.at[zr - 1, plan.pos[r]], (0, r)
                 else:
-                    yield "s", zr, refs[-1].at[at], far.at[zr - 1, at], (zr * plan.ny, 0)
-        yield from self.steps("x", plan, far, self.x)
-        yield from self.steps("c", plan, far, self.c)
-
-    def steps(self, kind, plan, far, zrs):
-        for zr in zrs:
-            if kind == "x":
-                for r in plan.across:
-                    yield "x", zr, far.at[zr - 1, 0], far.at[zr - 1, plan.pos[r]], (0, r)
-            else:
-                for r in [0] + plan.across:
-                    yield "c", zr, far.at[zr - 1, plan.pos[r]], far.at[zr - 1, plan.pos[r ^ 1]], (0, 1)
-
-    def second(self, plan, refs, far):
-        yield from self.steps("x", plan, far, self.then_x)
-        yield from self.steps("c", plan, far, self.then_c)
+                    for r in [0] + plan.across:
+                        yield stage, kind, zr, far.at[zr - 1, plan.pos[r]], far.at[zr - 1, plan.pos[r ^ 1]], (0, 1)
+
+    def before(self, kind):
+        return {"x": "z", "c": "zsx"}.get(kind, "")
 
     def targets(self, plan):
         return (
-            [(zr * plan.ny, 0) for zr in self.z + self.s]
-            + ([(0, r) for r in plan.across] if self.x or self.then_x else [])
-            + ([(0, 1)] if self.c or self.then_c else [])
+            [(zr * plan.ny, 0) for _, kind, zrs in self.todo if kind in "zs" for zr in zrs]
+            + ([(0, r) for r in plan.across] if self.has("x") else [])
+            + ([(0, 1)] if self.has("c") else [])
         )
 
 
@@ -260,10 +262,10 @@
     def moves(self, plan, refs, far):
         for r in range(1, plan.ny):
             for j in range(self.own.shape[1]):
-                yield "p" if self.paced else "y", r, refs[0].at[r, j], far.at[r - 1, j], (r, 0)
-
-    def second(self, plan, refs, far):
-        return ()
+                yield 0, "p" if self.paced else "y", r, refs[0].at[r, j], far.at[r - 1, j], (r, 0)
+
+    def before(self, kind):
+        return ""
 
     def targets(self, plan):
         return [(r, 0) for r in range(1, plan.ny)]
@@ -287,16 +289,17 @@
 class Background:
     def __init__(self, plan, jobs, owns, fars, send_sems, recv_sems, peers):
         self.plan, self.jobs, self.peers = plan, jobs, peers
-        self.owns, self.fars, self.sems, self.began = owns, fars, (send_sems, recv_sems), False
-        self.released = 0
+        self.owns, self.fars, self.sems = owns, fars, (send_sems, recv_sems)
+        self.released, self.begun, self.arrived = 0, set(), set()
+
+    def bind(self, n, ref):
+        self.owns[n] = [ref]
 
     def copies(self):
         n = 0
         for job, own, far in zip(self.jobs, self.owns, self.fars):
-            moves = [(False, m) for m in job.moves(self.plan, own, far)]
-            moves += [(True, m) for m in job.second(self.plan, own, far)]
-            for late, (kind, zr, src, dst, to) in moves:
-                yield job, late, kind, zr, send(src, dst, self.sems[0].at[n], self.sems[1].at[n], to)
+            for stage, kind, zr, src, dst, to in job.moves(self.plan, own, far):
+                yield n, job, stage, kind, zr, send(src, dst, self.sems[0].at[n], self.sems[1].at[n], to)
                 n += 1
 
     def greet(self):
@@ -305,34 +308,30 @@
             pl.semaphore_signal(barrier, inc=1, device_id=peer(p), device_id_type=MESH)
         pl.semaphore_wait(barrier, len(self.peers))
 
-    def start(self):
-        for _, late, kind, _, copy in self.copies():
-            if not late and kind != "p":
-                copy.start()
+    def start(self, stage=0):
+        self.begun.add(stage)
+        copies = list(self.copies())
+        mine = [c for c in copies if c[2] == stage and c[3] != "p"]
+        needs = [(job, k, zr) for _, job, _, kind, zr, _ in mine for k in job.before(kind)]
+        for n, job, at, kind, zr, copy in copies:
+            if (job, kind, zr) in needs and n not in self.arrived and at in self.begun:
+                copy.wait_recv()
+                self.arrived.add(n)
+        for c in mine:
+            c[-1].start()
 
     def release(self, n):
-        paced = [copy for _, _, kind, _, copy in self.copies() if kind == "p"]
+        paced = [c[-1] for c in self.copies() if c[3] == "p"]
         for copy in paced[self.released : self.released + n]:
             copy.start()
         self.released += n
 
-    def second(self):
-        needs = [(job, zr) for job, late, _, zr, _ in self.copies() if late]
-        for job, late, kind, zr, copy in self.copies():
-            if not late and kind in "zx" and (job, zr) in needs:
-                copy.wait_recv()
-        for _, late, _, _, copy in self.copies():
-            if late:
-                copy.start()
-        self.began = True
-
     def finish(self):
-        if not self.began:
-            self.second()
-        self.release(sum(kind == "p" for _, _, kind, _, _ in self.copies()) - self.released)
-        needs = [(job, zr) for job, late, _, zr, _ in self.copies() if late]
-        for job, late, kind, zr, copy in self.copies():
-            if not late and kind in "zx" and (job, zr) in needs:
+        for stage in sorted({c[2] for c in self.copies()} - self.begun):
+            self.start(stage)
+        self.release(sum(c[3] == "p" for c in self.copies()) - self.released)
+        for n, _, _, _, _, copy in self.copies():
+            if n in self.arrived:
                 copy.wait_send()
             else:
                 copy.wait()
@@ -499,7 +498,7 @@
         out_specs.append(ANYWHERE)
         places.append(place)
         blank = [Blank(), Blank()]
-        count += len(list(job.moves(plan, blank, Blank()))) + len(list(job.second(plan, blank, Blank())))
+        count += len(list(job.moves(plan, blank, Blank())))
         peers += [p for p in dict.fromkeys(job.targets(plan)) if p not in peers]
     if jobs:
         scratch += [DMA((count,)), DMA((count,))]
@@ -914,17 +913,45 @@
     )
 
 
-def cross_forward(plan, hc, mid, memory, gains, inward, outward, jobs):
+def weight_grads(hq, hm, dq, dk, dv, o_t, d_branch):
+    return [tn(hq, dq), tn(hm, dk), tn(hm, dv), nn(o_t.astype(BF16), d_branch)]
+
+
+def middle(plan, hc, mid, memory, final, cols, own_col, out_grad, og_near, gains, inward, outward, up, down, jobs):
     ids, count = plan.ids, plan.n_expert
     rows, feature = hc.shape
     length = count * rows
-
-    def body(bg, h, res, mem, g, win_any, wout_any, t2, w, w_near, hm, k, k_t, v, q, o_t, lse, win, wout, q_t, v_t, raw, low, lsem, *sems):
+    experts, hidden, _ = up.shape
+    cap = 2 * rows // EXPERTS
+    slots = count * 2 * cap
+    heads = feature // HEAD_DIM
+
+    def body(bg, *refs):
+        h, t1, mem, e2, g, col, mine, og_own = refs[:8]
+        og_any, win_any, wout_any, up_any, down_any = refs[8:13]
+        t2_out, w_out, res_out, fg, fg_low, fg_near, dt1, dw, dg2, dg4, dg5 = refs[13:24]
+        t2, w_near, result, og, hm, k, k_t, v, q, o_t, lse, q_t, v_t, raw, low, do_t = refs[24:40]
+        buf, gbuf, act, slopes, wup, wdown, stage, ret, rs, rr = refs[40:50]
+        dk, dv, dq, dq_t, do, parts, got, upstream, win, wout, lsem, wsem, osem = refs[50:63]
+        sems = refs[63:]
         weights = [load(win_any.at[2], win, lsem.at[0]), load(wout_any.at[2], wout, lsem.at[1])]
+        og_load = load(og_any, og, lsem.at[2])
+        gather_m = [Gather(ids, hm.at[p], sems[p].at[0], sems[p].at[1]) for p in range(2)]
+        gather_w = [Gather(ids, w_near.at[p], sems[2 + p].at[0], sems[2 + p].at[1]) for p in range(2)]
+        gather_f = [Gather(ids, fg_near.at[p], sems[4 + p].at[0], sems[4 + p].at[1]) for p in range(2)]
+        scatter = [Scatter(ids, parts.at[p], got.at[p], sems[6 + p].at[0], sems[6 + p].at[1]) for p in range(2)]
+        back = Return(ids, stage, ret, rs, rr)
+        flushes = [load(t2, t2_out, osem.at[0]), load(w_near, w_out, osem.at[1]), load(result, res_out, osem.at[2])]
+        bg.bind(0, w_near)
+
+        def fetch(j):
+            return [
+                load(up_any.at[j], wup.at[j % 2], wsem.at[0, j % 2]),
+                load(down_any.at[j], wdown.at[j % 2], wsem.at[1, j % 2]),
+            ]
+
         for x in weights:
             x.start()
-        gather_m = [Gather(ids, hm.at[p], sems[p].at[0], sems[p].at[1]) for p in range(2)]
-        gather_w = [Gather(ids, w_near.at[p], sems[2 + p].at[0], sems[2 + p].at[1]) for p in range(2)]
         for p in range(2):
             hm[p, 0] = mem[p]
         bg.greet()
@@ -933,6 +960,8 @@
         bg.start()
         for x in weights:
             x.wait()
+        for x in [og_load] + [x for j in range(min(2, experts)) for x in fetch(j)]:
+            x.start()
         q_scaled = project_query(h[...], win[...])
         q[...] = q_scaled.astype(BF16)
         q_t[...] = q_scaled.T.astype(BF16)
@@ -942,133 +971,52 @@
             project_rows(hm[p].reshape(length, feature), win[...], k.at[p], k_t.at[p], v.at[p], v_t)
             between = gather_m[1].forward if p == 0 else gather_w[0].forward
             attend_forward(q_t, k.at[p], v_t, None, o_t.at[p], lse.at[p], (raw, low), [(2, between)])
-            t2[p] = res[...] + nn(o_t[p].T.astype(BF16), wout[...])
+            t2[p] = t1[...] + nn(o_t[p].T.astype(BF16), wout[...])
             norm_rows(t2.at[p], w_near.at[p, 0], g[5:6])
-            w[p] = w_near[p, 0]
             gather_w[p].start()
             if p == 0:
                 gather_m[1].finish()
+        flushes[0].start()
+        og_load.wait()
+        column_of = lambda s, p: col[s, 2 + p : 3 + p, :]
+        fill_buffers(cap, column_of, lambda s, p: og[s, p], range(count), gbuf)
+        gather_w[0].finish()
         gather_w[1].forward()
-        gather_w[0].finish()
         gather_w[1].finish()
-        bg.finish()
-
-    saved = attention_shapes(plan, rows, feature)
-    saved = [((2,) + s, d) if n != 3 else (s, d) for n, (s, d) in enumerate(saved)]
-    return fused(
-        plan,
-        body,
-        [hc, mid, memory, gains, inward, outward],
-        [
-            ((2, rows, feature), F32),
-            ((2, rows, feature), BF16),
-            ((2, count, rows, feature), BF16),
-            ((2, count, rows, feature), BF16),
-        ]
-        + saved,
-        "cross_forward",
-        cid=3,
-        peers=expert_peers(ids),
-        jobs=jobs,
-        in_specs=[None] * 4 + [ANYWHERE] * 2,
-        scratch=[
-            pltpu.VMEM((feature, 3 * feature), BF16),
-            pltpu.VMEM((feature, feature), BF16),
-            *forward_scratch(plan, rows, feature),
-            DMA((2,)),
-        ]
-        + [DMA((2, count))] * 4,
-        us=35,
-    )
-
-
-def decoder_experts(plan, w_near, og_near, col_near, own_col, crossed, out_grad, gains, weight_up, weight_down, jobs):
-    ids, count = plan.ids, plan.n_expert
-    experts, hidden, feature = weight_up.shape
-    rows = crossed.shape[1]
-    cap = 2 * rows // EXPERTS
-    length = count * 2 * cap
-
-    def body(bg, w, og, col, mine, t2, og_own, g, up, down, upstream, dg, result, buf, gbuf, act, slopes, *scratch):
-        j = pl.program_id(0)
-        back = Return(ids, *scratch)
-
-        @pl.when(j == 0)
-        def _():
-            bg.greet()
-            bg.start()
-            fill_buffers(cap, lambda s, p: col[s, 2 + p : 3 + p, :], lambda s, p: w[p, s], range(count), buf)
-            fill_buffers(cap, lambda s, p: col[s, 2 + p : 3 + p, :], lambda s, p: og[s, p], range(count), gbuf)
-
-        for at in range(0, hidden, WIDE):
-            span = slice(at, at + WIDE)
-            gelu_pair(nt(buf[j], up[0, span]), nt(gbuf[j], down[0, span]), act.at[:, span], slopes.at[:, span])
-        back.put(j, nn(slopes[...], up[0]).astype(BF16), cap)
-        back.start(j)
-        res = nn(act[...], down[0]).astype(BF16)
-        for s in range(count):
-            for p in range(2):
-                at = (2 * s + p) * cap
-                result[s, 0, p] = res[at : at + cap]
-
-        @pl.when(j == experts - 1)
-        def _():
-            bg.second()
-            back.finish(experts)
-            total = None
-            for p in range(2):
-                upstream[p] = gather_rows(ids, mine[p], back.rows(p))
-
-                def store(span, dx):
-                    upstream[p, span, :] = og_own[p, span, :] + dx
-
-                gain = norm_back_rows(t2.at[p], g[5:6], upstream.at[p], store)
-                total = gain if total is None else total + gain
-            dg[...] = total
-            bg.finish()
-
-    weight = pl.BlockSpec((1, hidden, feature), lambda j: (j, 0, 0))
-    return fused(
-        plan,
-        body,
-        [w_near, og_near, col_near, own_col, crossed, out_grad, gains, weight_up, weight_down],
-        [((2, rows, feature), F32), ((1, feature), F32), ((count, experts, 2, cap, feature), BF16)],
-        "decoder_experts",
-        cid=4,
-        peers=expert_peers(ids),
-        jobs=jobs,
-        grid=(experts,),
-        in_specs=[None] * 7 + [weight, weight],
-        out_specs=[None, None, pl.BlockSpec((count, 1, 2, cap, feature), lambda j: (0, j, 0, 0, 0))],
-        scratch=[pltpu.VMEM((experts, length, feature), BF16)] * 2
-        + [pltpu.VMEM((length, hidden), BF16)] * 2
-        + return_scratch(plan, experts, cap, feature),
-        us=30,
-    )
-
-
-def weight_grads(hq, hm, dq, dk, dv, o_t, d_branch):
-    return [tn(hq, dq), tn(hm, dk), tn(hm, dv), nn(o_t.astype(BF16), d_branch)]
-
-
-def cross_backward(
-    plan, upstream, final, hc, mid, gains, saved, inward, outward, jobs
-):
-    ids, count = plan.ids, plan.n_expert
-    rows, feature = mid.shape
-    length = count * rows
-
-    def body(bg, *refs):
-        up, e2, h, t1, g = refs[:5]
-        hm, k, k_t, v, q, o_t, lse, win_any, wout_any = refs[5:14]
-        fg, fg_low, fg_near, dt1, dw, dg2, dg4 = refs[14:21]
-        dk, dv, dq_t, do, *work, dw_acc, parts, got, win, wout, lsem = refs[21:-4]
-        sems = refs[-4:]
-        weights = [load(win_any.at[2], win, lsem.at[0]), load(wout_any.at[2], wout, lsem.at[1])]
-        for x in weights:
-            x.start()
-        scatter = [Scatter(ids, parts.at[p], got.at[p], sems[p].at[0], sems[p].at[1]) for p in range(2)]
-        gather = [Gather(ids, fg_near.at[p], sems[2 + p].at[0], sems[2 + p].at[1]) for p in range(2)]
+        bg.start(1)
+        flushes[1].start()
+        fill_buffers(cap, column_of, lambda s, p: w_near[p, s], range(count), buf)
+        for j in range(experts):
+            for x in fetch(j):
+                x.wait()
+            for at in range(0, hidden, WIDE):
+                span = slice(at, at + WIDE)
+                gelu_pair(
+                    nt(buf[j], wup[j % 2, span]), nt(gbuf[j], wdown[j % 2, span]), act.at[:, span], slopes.at[:, span]
+                )
+            back.put(j, nn(slopes[...], wup[j % 2]).astype(BF16), cap)
+            back.start(j)
+            res = nn(act[...], wdown[j % 2]).astype(BF16)
+            for s in range(count):
+                for p in range(2):
+                    at = (2 * s + p) * cap
+                    result[s, j, p] = res[at : at + cap]
+            if j + 2 < experts:
+                for x in fetch(j + 2):
+                    x.start()
+        flushes[2].start()
+        bg.start(2)
+        back.finish(experts)
+        total = None
+        for p in range(2):
+            upstream[p] = gather_rows(ids, mine[p], back.rows(p))
+
+            def store_up(span, dx):
+                upstream[p, span, :] = og_own[p, span, :] + dx
+
+            gain = norm_back_rows(t2.at[p], g[5:6], upstream.at[p], store_up)
+            total = gain if total is None else total + gain
+        dg5[...] = total
 
         def memory_back(p):
             fg[p] = scatter[p].finish()
@@ -1079,86 +1027,118 @@
                 fg_near[p, 0, span, :] = dx.astype(BF16)
 
             gain = norm_back_rows(e2.at[p], g[2:3], fg.at[p], store)
-            gather[p].start()
+            gather_f[p].start()
             if p == 0:
                 dg2[...] = gain
             else:
                 dg2[...] = dg2[...] + gain
 
-        bg.greet()
-        bg.start()
-        for x in weights:
-            x.wait()
-        dh = None
         for p in range(2):
-            d_branch = up[p].astype(BF16)
-            do[...] = nt(d_branch, wout[...]).astype(BF16)
-            between = () if p == 0 else ((1, scatter[0].middle), (2, lambda: memory_back(0)), (3, bg.second))
+            do[...] = nt(upstream[p].astype(BF16), wout[...]).astype(BF16)
+            between = () if p == 0 else ((1, scatter[0].middle), (2, lambda: memory_back(0)), (3, lambda: bg.start(3)))
             attend_backward(
-                q, k.at[p], v.at[p], k_t.at[p], do, o_t.at[p], lse.at[p], None, dk, dv, dq_t, work, between
+                q, k.at[p], v.at[p], k_t.at[p], do, o_t.at[p], lse.at[p], None, dk.at[p], dv.at[p], dq_t, (q_t, do_t, low), between
             )
-            for b in range(count):
+            for b in [i for i, r in enumerate(ids) if r % 2] + [i for i, r in enumerate(ids) if r % 2 == 0]:
                 span = slice(b * rows, (b + 1) * rows)
-                part = nt(dk[span, :], win[:, feature : 2 * feature]) + nt(dv[span, :], win[:, 2 * feature :])
+                part = nt(dk[p, span, :], win[:, feature : 2 * feature])
+                part = part + nt(dv[p, span, :], win[:, 2 * feature :])
                 parts[p, b] = part.astype(BF16)
             scatter[p].start()
-            dq = dq_t[...].astype(F32).T.astype(BF16)
-            back = nt(dq, win[:, :feature])
-            dh = back if dh is None else dh + back
-            if p == 1:
-                scatter[1].middle()
-                gather[0].forward()
-            grads = weight_grads(
-                h[...], hm[p].reshape(length, feature), dq, dk[...], dv[...], o_t[p], d_branch
+            dq[p] = dq_t[...].astype(F32).T.astype(BF16)
+        scatter[1].middle()
+        gather_f[0].forward()
+        grads = None
+        for p in range(2):
+            more = weight_grads(
+                h[...], hm[p].reshape(length, feature), dq[p], dk[p], dv[p], o_t[p], upstream[p].astype(BF16)
             )
-            for n, value in enumerate(grads):
-                at = slice(n * feature, (n + 1) * feature)
-                if p == 0:
-                    dw_acc[:, at] = value
-                else:
-                    dw[:, at] = (dw_acc[:, at] + value).astype(BF16)
+            grads = more if grads is None else [x + y for x, y in zip(grads, more)]
+        for n, value in enumerate(grads):
+            dw[:, n * feature : (n + 1) * feature] = value.astype(BF16)
         memory_back(1)
-        dt1[...] = dh
+        dt1[...] = nt(dq[0], win[:, :feature]) + nt(dq[1], win[:, :feature])
 
         def store_mid(span, dx):
-            dt1[span, :] = up[0, span, :] + up[1, span, :] + dx
+            dt1[span, :] = upstream[0, span, :] + upstream[1, span, :] + dx
 
         dg4[...] = norm_back_rows(t1, g[4:5], dt1, store_mid)
-        gather[1].forward()
-        gather[0].finish()
-        gather[1].finish()
+        gather_f[1].forward()
+        gather_f[0].finish()
+        gather_f[1].finish()
+        for x in flushes:
+            x.wait()
         bg.finish()
 
     block = (rows, feature)
+    two = (2,) + block
+    near = (2, count) + block
+    home = (count, experts, 2, cap, feature)
+    keys = (2, length, feature)
+    low_vmem = lambda *shape: pltpu.VMEM(shape, BF16)
     return fused(
         plan,
         body,
-        [upstream, final, hc, mid, gains, *saved, inward, outward],
+        [hc, mid, memory, final, gains, cols, own_col, out_grad, og_near, inward, outward, up, down],
         [
-            ((2,) + block, F32),
-            ((2,) + block, BF16),
-            ((2, count) + block, BF16),
+            (two, F32),
+            (near, BF16),
+            (home, BF16),
+            (two, F32),
+            (two, BF16),
+            (near, BF16),
             (block, F32),
             ((feature, 4 * feature), BF16),
             ((1, feature), F32),
             ((1, feature), F32),
+            ((1, feature), F32),
         ],
-        "cross_backward",
-        cid=5,
+        "middle",
+        cid=3,
         peers=expert_peers(ids),
         jobs=jobs,
-        in_specs=[None] * 12 + [ANYWHERE] * 2,
+        in_specs=[None] * 8 + [ANYWHERE] * 5,
+        out_specs=[ANYWHERE] * 3 + [None] * 8,
         scratch=[
-            *backward_scratch(plan, rows, feature),
-            pltpu.VMEM((feature, 4 * feature), F32),
-            pltpu.VMEM((2, count) + block, BF16),
-            pltpu.VMEM((2, count) + block, BF16),
-            pltpu.VMEM((feature, 3 * feature), BF16),
-            pltpu.VMEM((feature, feature), BF16),
-            DMA((2,)),
+            pltpu.VMEM(two, F32),
+            low_vmem(*near),
+            low_vmem(*home),
+            low_vmem(*og_near.shape),
+            low_vmem(*near),
+            low_vmem(*keys),
+            low_vmem(2, feature, length),
+            low_vmem(*keys),
+            low_vmem(*block),
+            pltpu.VMEM((2, feature, rows), F32),
+            pltpu.VMEM((2, heads, rows), F32),
+            low_vmem(feature, rows),
+            low_vmem(feature, length),
+            pltpu.VMEM((2, length, rows), F32),
+            low_vmem(2, length, rows),
+            low_vmem(feature, rows),
+            low_vmem(experts, slots, feature),
+            low_vmem(experts, slots, feature),
+            low_vmem(slots, hidden),
+            low_vmem(slots, hidden),
+            low_vmem(2, hidden, feature),
+            low_vmem(2, hidden, feature),
+            *return_scratch(plan, experts, cap, feature),
+            low_vmem(*keys),
+            low_vmem(*keys),
+            low_vmem(*two),
+            low_vmem(feature, rows),
+            low_vmem(*block),
+            low_vmem(*near),
+            low_vmem(*near),
+            pltpu.VMEM(two, F32),
+            low_vmem(feature, 3 * feature),
+            low_vmem(feature, feature),
+            DMA((3,)),
+            DMA((2, 2)),
+            DMA((3,)),
         ]
-        + [DMA((2, count))] * 4,
-        us=45,
+        + [DMA((2, count))] * 8,
+        us=130,
     )
 
 
@@ -1289,7 +1269,7 @@
             plan, ids, 1, up, saved_refs, win, wout, work, parts, scatter, dw, (ids, rows), (), lambda: None
         )
         scatter.middle()
-        bg.second()
+        bg.start(1)
         dg[...] = input_back(up, src, g[3:4], scatter, grad)
         bg.finish()
 
@@ -1438,7 +1418,7 @@
             d_branch = ups[n][...].astype(BF16)
             do[...] = nt(d_branch, wout[n]).astype(BF16)
             causal = (ids, rows) if n == 1 else None
-            between = () if n == 0 else ((0, bg.second), (1, scatter[0].middle), (3, lambda: finish(0)))
+            between = () if n == 0 else ((0, lambda: bg.start(1)), (1, scatter[0].middle), (3, lambda: finish(0)))
             attend_backward(q, k, v, k_t, do, o_t, lse, causal, dk, dv, dq_t, work, between)
             dq = dq_t[...].astype(F32).T.astype(BF16)
             for b in range(count):
@@ -1707,44 +1687,28 @@
         encoder_down,
         [Job(None, col_far, x=zr), Job(og, og_far, z=zc)],
     )
-    (t2, w, w_near, *cross_saved), (col_far, og_far, u_far) = cross_forward(
+    (t2, w_near, result, fg, fg_low, fg_near, dt1, cross_dw, dg2, dg4, dg5), (w_far, col_far, og_far, u_far) = middle(
         plan,
         hc,
         t1,
         memory,
+        e2,
+        col_near,
+        own_cols[1],
+        out_grad,
+        og_near,
         gains,
         *weights,
-        [Job(None, col_far, c=zr), Job(None, og_far, s=za + zb, near=og_near), Job(u, None, z=zr)],
-    )
-    (upstream, dg5, result), (og_far, w_far) = decoder_experts(
-        plan,
-        w_near,
-        og_near,
-        col_near,
-        own_cols[1],
-        t2,
-        out_grad,
-        gains,
         decoder_up,
         decoder_down,
-        [Job(None, og_far, c=za + zb, then_x=zc), Job(w, None, z=za + zb)],
-    )
-    (fg, fg_low, fg_near, dt1, cross_dw, dg2, dg4), (w_far, og_far, u_far) = cross_backward(
-        plan,
-        upstream,
-        e2,
-        hc,
-        t1,
-        gains,
-        cross_saved,
-        *weights,
         [
-            Job(w, w_far, z=zc, s=za + zb, then_x=zc, near=w_near, by_pass=True),
-            Job(None, og_far, c=zc),
-            Job(None, u_far, x=zr),
+            Job(og, None, later=[(1, "z", zc + za + zb), (1, "s", za + zb), (3, "x", zc)], by_pass=True, local=True),
+            Job(None, col_far, c=zr),
+            Job(None, og_far, s=za + zb, near=og_near, later=[(1, "c", za + zb), (2, "x", zc)]),
+            Job(u, None, z=zr),
         ],
     )
-    (de1, dg1), (w_far, u_far, fg_far) = encoder_experts(
+    (de1, dg1), (w_far, og_far, fg_far) = encoder_experts(
         plan,
         u_near,
         fg_near,
@@ -1755,7 +1719,7 @@
         gains,
         encoder_up,
         encoder_down,
-        [Job(None, w_far, c=zr), Job(None, u_far, c=zr), Job(fg_low, None, z=za + zb)],
+        [Job(None, w_far, c=zr), Job(None, og_far, c=zc), Job(fg_low, None, z=za + zb)],
     )
     dec_g, (fg_far,) = expert_weights(
         plan,
@@ -1768,14 +1732,18 @@
         decoder_down,
         [Job(fg_low, fg_far, z=zc, x=za + zb)],
     )
-    (target_grad, dec_dw, dg3), (fg_far, up_got) = decoder_backward(
+    (target_grad, dec_dw, dg3), (fg_far, u_far, up_got) = decoder_backward(
         plan,
         dt1,
         target,
         gains,
         dec_saved,
         *weights,
-        [Job(None, fg_far, x=zc, c=za + zb, then_c=zc), Swap(dec_g[0])],
+        [
+            Job(None, fg_far, x=zc, c=za + zb, later=[(1, "c", zc)]),
+            Job(None, u_far, s=zr, near=u_near, later=[(1, "c", zr)]),
+            Swap(dec_g[0]),
+        ],
     )
     (*enc_g, decoder_output), (down_got,) = expert_weights(
         plan,

time: 485 us -> 461 us (0.951)
  Pallas kernels: 471 us -> 442 us
    pallas_call x11 -> x9, Pallas kernels: 471 us -> 442 us  [fused(): pl.pallas_call(run, out_shape=[jax.ShapeDtypeStruct(s, d) for s, d in out...]
where the time goes in v5:
time: 461 us; the launch traced here: 453 us
  Pallas kernels  442 us (96%)
  local copies, waits for them, and re-layouts  7.37 us (2%)
    pallas_call x9, Pallas kernels, fused(): pl.pallas_call(run, out_shape=[jax.ShapeDtypeStruct(s, d) for s, d in out...  442 us

profile of v5, /device:TPU:0, one launch (start us, length us, event | category | flops | bytes accessed | tf_op | source)
XLA Modules:
  0.0 453.3 jit_solution(7223422443508430590)
XLA Ops:
  0.6 0.8 fusion
  1.4 0.6 reshape.43.refs_2_.refs_7_
  2.0 2.1 bitcast_convert_fusion.refs_3_.refs_8_
  4.1 45.2 %self_forward.1 = (f32[256,512]{1,0:T(8,128)}, bf16[256,512]{1,0:T(8,128)(2,1)}, bf16[1024,512]{1,0:T(8,128)(2,1)}, bf16[1024,512]{1,0:T(8,128)(2,1)}, bf16[512,...) custom-call(bf16[1,256,512]{2,1,0:T(8,128)(2,1)} %refs_1_.5, ...), custom_call_target="tpu_custom_call" | custom-call | flops 40249999360 | bytes 7356416 | tf_op jit(solution)/shard_map/self_forward/pallas_call | solution.py:516
  49.3 0.8 squeeze.10.refs_2_.refs_3_
  50.2 20.6 %expert_forward.1 = (f32[2,256,512]{2,1,0:T(8,128)}, bf16[2,256,512]{2,1,0:T(8,128)(2,1)}, s32[3,4,4,256]{3,2,1,0:T(4,128)}, bf16[3,4,2,256,512]{4,3,2,1,0:T(8,128)(2,1)}) custom-call(bf16[4,256,512]{2,1,0:T(8,128)(2,1)} %get-tuple-element.85.refs_0_.refs_13_.refs_4_, ...), custom_call_target="tpu_custom_call", output_to_operand_aliasing={{2}: (7, {}), {3}: (9, {})} | custom-call | flops 25300000768 | bytes 18380800 | tf_op jit(solution)/shard_map/expert_forward/pallas_call | solution.py:516
  70.7 0.8 squeeze.11.refs_6_.refs_2_
  71.6 131.6 %middle.1 = (f32[2,256,512]{2,1,0:T(8,128)}, bf16[2,4,256,512]{3,2,1,0:T(8,128)(2,1)}, bf16[4,4,2,32,512]{4,3,2,1,0:T(8,128)(2,1)}, f32[2,256,512]{2,1,0:T(8,128...) custom-call(bf16[256,512]{1,0:T(8,128)(2,1)} %get-tuple-element.83.r, ...), custom_call_target="tpu_custom_call", output_to_operand_aliasing={{12}: (13, {}), {13}: (15, {})} | custom-call | flops 149500002304 | bytes 28604416 | tf_op jit(solution)/shard_map/middle/pallas_call | solution.py:516
  203.2 29.9 %encoder_experts.1 = (f32[256,512]{1,0:T(8,128)}, f32[1,512]{1,0:T(1,128)}, bf16[3,4,2,256,512]{4,3,2,1,0:T(8,128)(2,1)}, bf16[3,4,2,256,512]{4,3,2,1,0:T(8,128)(2,1)}, bf16[3,4,2,256,512]{4,3,2,1,0:T(8,128)(2,1)}) custom-call(bf16[4,256,512]{2,1,0:T(8,128)(2,1)} %get-tuple-element.85.refs_0_.refs_13_.refs_4_, ...), custom_call_target="tpu_custom_call", output_to_operand_aliasing={{2}: (9, {}), {3}: (10, {})} | custom-call | flops 34500001792 | bytes 21526528 | tf_op jit(solution)/shard_map/encoder_experts/pallas_call | solution.py:516
  233.1 29.1 %decoder_weights.1 = (bf16[2,4,256,512]{3,2,1,0:T(8,128)(2,1)}, bf16[2,4,256,512]{3,2,1,0:T(8,128)(2,1)}, bf16[3,4,2,256,512]{4,3,2,1,0:T(8,128)(2,1)}) custom-call(s32[4,4,256]{2,1,0:T(4,128)} %get-tuple-element.82.refs_1_.refs_5_.refs_2_.refs_0_, s32[3,4,4,256]{3,2,1,0:T(4,128)} %get-tuple-element.95.refs_1_, ...), custom_call_target="tpu_custom_call", output_to_operand_aliasing={{2}: (9, {})} | custom-call | flops 28750000128 | bytes 33619968 | tf_op jit(solution)/shard_map/decoder_weights/pallas_call | solution.py:516
  262.3 0.0 copy-start.4
  262.3 0.0 copy-start.5
  262.3 0.0 copy-start.6
  262.3 0.0 copy-start.7
  262.3 0.0 copy-start.8
  262.3 0.0 copy-start.9
  262.3 31.6 %decoder_backward.1 = (f32[256,512]{1,0:T(8,128)}, bf16[512,2048]{1,0:T(8,128)(2,1)}, f32[1,512]{1,0:T(1,128)}, bf16[3,4,2,256,512]{4,3,2,1,0:T(8,128)(2,1)}, bf...) custom-call(f32[256,512]{1,0:T(8,128)} %get-tuple-element.97.refs_0_, ...), custom_call_target="tpu_custom_call", output_to_operand_aliasing={{3}: (12, {}), {4}: (14, {})} | custom-call | flops 32199999488 | bytes 12079104 | tf_op jit(solution)/shard_map/decoder_backward/pallas_call | solution.py:516
  293.9 0.0 copy-done.4
  293.9 0.0 copy-done.5
  293.9 0.1 convert_reduce_fusion
  294.0 0.1 reshape.46
  294.1 0.0 copy-done.6
  294.2 1.3 concatenate.3.refs_3_
  295.4 30.3 %encoder_weights.1 = (bf16[2,4,256,512]{3,2,1,0:T(8,128)(2,1)}, bf16[2,4,256,512]{3,2,1,0:T(8,128)(2,1)}, bf16[2,256,512]{2,1,0:T(8,128)(2,1)}, bf16[1,4,256,512]{3,2,1,0:T(8,128)(2,1)}) custom-call(s32[4,4,256]{2,1,0:T(4,128)} %get-tuple-element.82.refs_1_.refs_5_.refs_2_.refs_0_, s32[3,4,4,256]{3,2,1,0:T(4,128)} %get-tuple-element.95.refs_1_, ...), custom_call_target="tpu_custom_call" | custom-call | flops 28750000128 | bytes 31524864 | tf_op jit(solution)/shard_map/encoder_weights/pallas_call | solution.py:516
  325.8 110.4 %encoder_backward.1 = (f32[256,512]{1,0:T(8,128)}, bf16[3,512,2048]{2,1,0:T(8,128)(2,1)}, f32[8,512]{1,0:T(8,128)}, bf16[1,4,256,512]{3,2,1,0:T(8,128)(2,1)}, bf16[1,4,256,512]{3,2,1,0:T(8,128)(2,1)}) custom-call(f32[256,512]{1,0:T(8,128)} %get-tuple-element.122.refs_0_, bf16[1,256,512]{2,1,0:T(8,128)(2,1)} %refs_1_.5, f32[6,512]{1,0:T(8,128)} %refs_2_.3, ...), custom_call_target="tpu_custom_call" | custom-call | flops 103499997184 | bytes 16289792 | tf_op jit(solution)/shard_map/encoder_backward/pallas_call | solution.py:516
  436.3 13.2 %finish.1 = (f32[3,512,1536]{2,1,0:T(8,128)}, f32[3,512,512]{2,1,0:T(8,128)}, f32[4,256,512]{2,1,0:T(8,128)}, f32[4,256,512]{2,1,0:T(8,128)}, f32[4,256,512]{2,1,0:T(8,128)}, /*index=5*/f32[4,256,512]{2,1,0:T(8,128)}) custom-call(bf16[3,512,2048]{2,1,0:T(8,128)(2,1)} %get-tuple-element.141.refs_0_, ...), custom_call_target="tpu_custom_call" | custom-call | flops 11500000256 | bytes 18874368 | tf_op jit(solution)/shard_map/finish/pallas_call | solution.py:516
  449.5 0.7 convert_element_type.17
  450.1 0.8 copy.73
  450.9 0.8 copy.74
  451.7 0.0 copy-done
  451.7 0.8 copy.75
  452.5 0.6 copy.76
  (16 shorter events, 0.1 us)
Async XLA Ops:
  262.3 31.6 %copy-start.4 = (s32[2,1,256]{2,1,0:T(1,128)S(1)}, s32[2,1,256]{2,1,0:T(1,128)}, u32[]{:S(2)}) copy-start(s32[2,1,256]{2,1,0:T(1,128)} %param.23) | copy-start | bytes 6148
  262.3 31.6 %copy-start.5 = (s32[2,1,256]{2,1,0:T(1,128)S(1)}, s32[2,1,256]{2,1,0:T(1,128)}, u32[]{:S(2)}) copy-start(s32[2,1,256]{2,1,0:T(1,128)} %param.25) | copy-start | bytes 6148
  262.3 31.9 %copy-start.6 = (f32[1,512]{1,0:T(1,128)S(1)}, f32[1,512]{1,0:T(1,128)}, u32[]{:S(2)}) copy-start(f32[1,512]{1,0:T(1,128)} %get-tuple-element.124) | copy-start | bytes 6148
  262.3 31.9 %copy-start.7 = (f32[1,512]{1,0:T(1,128)S(1)}, f32[1,512]{1,0:T(1,128)}, u32[]{:S(2)}) copy-start(f32[1,512]{1,0:T(1,128)} %get-tuple-element.126) | copy-start | bytes 6148
  262.3 31.9 %copy-start.8 = (f32[1,512]{1,0:T(1,128)S(1)}, f32[1,512]{1,0:T(1,128)}, u32[]{:S(2)}) copy-start(f32[1,512]{1,0:T(1,128)} %get-tuple-element.127) | copy-start | bytes 6148
  262.3 31.9 %copy-start.9 = (f32[1,512]{1,0:T(1,128)S(1)}, f32[1,512]{1,0:T(1,128)}, u32[]{:S(2)}) copy-start(f32[1,512]{1,0:T(1,128)} %get-tuple-element.123) | copy-start | bytes 6148
  436.2 13.2 %copy-start.3 = (f32[8,512]{1,0:T(8,128)S(1)}, f32[8,512]{1,0:T(8,128)}, u32[]{:S(2)}) copy-start(f32[8,512]{1,0:T(8,128)} %get-tuple-element.148) | copy-start | bytes 49156
  436.2 13.9 %copy-start.1 = (bf16[2,256,512]{2,1,0:T(8,128)(2,1)S(1)}, bf16[2,256,512]{2,1,0:T(8,128)(2,1)}, u32[]{:S(2)}) copy-start(bf16[2,256,512]{2,1,0:T(8,128)(2,1)} %get-tuple-element.121) | copy-start | bytes 1572868
  436.3 14.7 %copy-start.2 = (f32[256,512]{1,0:T(8,128)S(1)}, f32[256,512]{1,0:T(8,128)}, u32[]{:S(2)}) copy-start(f32[256,512]{1,0:T(8,128)} %get-tuple-element.139) | copy-start | bytes 1572868
  436.3 15.5 %copy-start = (f32[256,512]{1,0:T(8,128)S(1)}, f32[256,512]{1,0:T(8,128)}, u32[]{:S(2)}) copy-start(f32[256,512]{1,0:T(8,128)} %get-tuple-element.140) | copy-start | bytes 1572868

commit v6 on v5

--- a/solution.py
+++ b/solution.py
@@ -320,6 +320,9 @@
         for c in mine:
             c[-1].start()
 
+    def paced(self):
+        return sum(c[3] == "p" for c in self.copies())
+
     def release(self, n):
         paced = [c[-1] for c in self.copies() if c[3] == "p"]
         for copy in paced[self.released : self.released + n]:
@@ -363,7 +366,7 @@
         x = [(0, 2 * b) for b in powers(plan.n_expert // 2)]
         y = [(b, 0) for b in powers(plan.ny)]
         z = [(plan.ny * b, 0) for b in powers(plan.nz)]
-        return [x + y + z, y + z + x, z + x + y]
+        return [x + z + y, z + x + y, y + z + x]
 
     @classmethod
     def tmp_rows(cls, plan, rows):
@@ -980,10 +983,11 @@
         og_load.wait()
         column_of = lambda s, p: col[s, 2 + p : 3 + p, :]
         fill_buffers(cap, column_of, lambda s, p: og[s, p], range(count), gbuf)
+        bg.start(1)
         gather_w[0].finish()
         gather_w[1].forward()
         gather_w[1].finish()
-        bg.start(1)
+        bg.start(2)
         flushes[1].start()
         fill_buffers(cap, column_of, lambda s, p: w_near[p, s], range(count), buf)
         for j in range(experts):
@@ -1005,7 +1009,7 @@
                 for x in fetch(j + 2):
                     x.start()
         flushes[2].start()
-        bg.start(2)
+        bg.start(3)
         back.finish(experts)
         total = None
         for p in range(2):
@@ -1017,6 +1021,7 @@
             gain = norm_back_rows(t2.at[p], g[5:6], upstream.at[p], store_up)
             total = gain if total is None else total + gain
         dg5[...] = total
+        bg.start(4)
 
         def memory_back(p):
             fg[p] = scatter[p].finish()
@@ -1035,7 +1040,7 @@
 
         for p in range(2):
             do[...] = nt(upstream[p].astype(BF16), wout[...]).astype(BF16)
-            between = () if p == 0 else ((1, scatter[0].middle), (2, lambda: memory_back(0)), (3, lambda: bg.start(3)))
+            between = () if p == 0 else ((1, scatter[0].middle), (2, lambda: memory_back(0)), (3, lambda: bg.start(5)))
             attend_backward(
                 q, k.at[p], v.at[p], k_t.at[p], do, o_t.at[p], lse.at[p], None, dk.at[p], dv.at[p], dq_t, (q_t, do_t, low), between
             )
@@ -1196,16 +1201,6 @@
     )
 
 
-def column_groups(n_dw, width):
-    if n_dw % 3 == 0:
-        return [(n, 0, width) for n in range(n_dw)]
-    cut = (width // 3) // 128 * 128
-    groups = []
-    for n in range(n_dw):
-        groups += [(n, 0, cut), (n, cut, width - 2 * cut), (n, width - cut, cut)]
-    return groups
-
-
 def attention_back(plan, ids, n, up, saved, win, wout, work, parts, scatter, dw, causal, between, after):
     hm, k, k_t, v, q, o_t, lse = saved
     dk, dv, dq_t, do, *rest = work
@@ -1288,27 +1283,46 @@
     )
 
 
-def encoder_backward(plan, enc_up, source, gains, saved, inward, outward, sums, small, jobs):
-    ids, count = plan.ids, plan.n_expert
+def last(plan, enc_up, source, gains, saved, inward, outward, sums, small, tokens, grads, cols, up, down, home, jobs):
+    ids, count, ny, nz = plan.ids, plan.n_expert, plan.ny, plan.nz
     _, rows, feature = source.shape
     width = 4 * feature
-    groups = column_groups(1, width)
+    groups = column_groups(width)
     steps = 1 + len(AllReduce.rotations(plan)[0])
     n_dw = len(sums) + 1
+    result, own_col, crossed = home
+    experts, hidden, _ = up.shape
+    cap = 2 * rows // EXPERTS
+    sources = count * nz
+    length = sources * 2 * cap
+    span = hidden // plan.n_dp
+    block = ny * span
 
     def body(bg, *refs):
-        up, src, g, sm = refs[:4]
-        saved_refs, win_any, wout_any = refs[4:11], refs[11], refs[12]
-        sums_any = refs[13 : 13 + n_dw - 1]
-        grad, sum_out, small_out = refs[12 + n_dw : 15 + n_dw]
-        *work, parts, got, win, wout, acc, tmp, small_tmp, lsem, asem, ssem, credits, sems = refs[15 + n_dw :]
+        ups, src, g, sm = refs[:4]
+        saved_refs, cn, cf, mine, t2 = refs[4:11], refs[11], refs[12], refs[13], refs[14]
+        win_any, wout_any, up_any, down_any, res_any = refs[15:20]
+        big, sums_any = refs[20:24], refs[24 : 23 + n_dw]
+        grad, sum_out, small_out, up_own, down_own, got_out, y_out = refs[23 + n_dw : 30 + n_dw]
+        rest = refs[30 + n_dw :]
+        *work, parts, got, win, wout = rest[:11]
+        near, far = rest[11:13]
+        wup, wdown, buf, gbuf, act, slopes, ret, acc, tmp, small_tmp = rest[13:23]
+        lsem, asem, ssem, credits, ysem, rs, rr, sems, osem = rest[23:]
         weights = [load(win_any.at[0], win, lsem.at[0]), load(wout_any.at[0], wout, lsem.at[1])]
+        first = pl.multiple_of(lax.div(lax.axis_index("dp"), ny) * block, block)
         firsts = [load(ref, acc.at[n], lsem.at[2 + n]) for n, ref in enumerate(sums_any)]
-        for x in weights + firsts:
+        at = 1 + n_dw
+        held = (near.at[0], far.at[:, :, 0], near, far)
+        bigs = [load(a, b, lsem.at[at + n]) for n, (a, b) in enumerate(zip(big, held))]
+        bigs.append(load(up_any.at[:, pl.ds(first, block)], wup, lsem.at[at + 4]))
+        bigs.append(load(down_any.at[:, pl.ds(first, block)], wdown, lsem.at[at + 5]))
+        own = load(res_any.at[0], ret.at[0], lsem.at[at + 6])
+        bring = [send(res_any.at[s], ret.at[s], rs.at[s], rr.at[s], (0, ids[s])) for s in range(1, count)]
+        for x in weights + firsts + bigs[:2] + bigs[4:] + [own]:
             x.start()
         small_out[...] = sm[...]
         bg.greet()
-        bg.start()
 
         def reduce(n):
             return AllReduce(
@@ -1317,149 +1331,155 @@
 
         for x in firsts:
             x.wait()
-        runs = [reduce(n) for n in range(n_dw - 1)]
-
-        def step(release=1):
-            for run in runs:
+        others = [reduce(n) for n in range(n_dw - 1)]
+        mine_run, waiting = [], []
+
+        def step(n=1):
+            for run in mine_run + others:
                 next(run, None)
-            bg.release(release)
-
-        step(0)
+            for _ in range(n):
+                if bg.released < bg.paced():
+                    bg.release(1)
+                elif waiting:
+                    waiting.pop(0).start()
+
+        step(2)
+        bg.start()
+
+        def after():
+            step()
+            for x in bring:
+                x.start()
+
         for x in weights:
             x.wait()
         scatter = Scatter(ids, parts, got, sems.at[0], sems.at[1])
-        between = ((2, step),)
         attention_back(
-            plan, ids, 0, up, saved_refs, win, wout, work, parts, scatter, acc.at[n_dw - 1], None, between, step
+            plan, ids, 0, ups, saved_refs, win, wout, work, parts, scatter, acc.at[n_dw - 1], None, ((2, lambda: step(0)),), after
         )
-        runs.append(reduce(n_dw - 1))
+        mine_run.append(reduce(n_dw - 1))
         step()
         scatter.middle()
-        step(1)
-        small_out[0:1, :] = input_back(up, src, g[0:1], scatter, grad)
-        runs.append(AllReduce(plan, acc, [], None, small_out, small_tmp, None, ssem).run())
+        col_of, token_of, grad_of = weight_sources(plan, 0, held[0:2], held[2:4], (cn, cf))
+        bigs[0].wait()
+        bigs[1].wait()
+        fill_buffers(cap, col_of, token_of, range(sources), buf)
+        for x in bigs[2:4]:
+            x.start()
+        small_out[0:1, :] = input_back(ups, src, g[0:1], scatter, grad)
+        mine_run.append(AllReduce(plan, acc, [], None, small_out, small_tmp, None, ssem).run())
+        step()
+        for x in bigs[2:]:
+            x.wait()
+        fill_buffers(cap, col_of, grad_of, range(sources), gbuf)
+        step()
+        y = lax.rem(lax.axis_index("dp"), ny)
+
+        def stage(r, j, n):
+            at = ((r - 1) * experts + j) * 2 + n
+            return (parts if at < count else got).at[at % count, pl.ds(0, span)]
+
+        def to_y(r, j, n):
+            return send(
+                stage(r, j, n), got_out.at[r - 1, j, n], ysem.at[0, r - 1, j, n], ysem.at[1, r - 1, j, n], (r, 0)
+            )
+
+        flushes = []
+        for r in reversed(range(ny)):
+            place = pl.ds(pl.multiple_of(xor(y, r) * span, span), span)
+            for j in range(experts):
+                products = weight_products(
+                    wup[j, place, :], wdown[j, place, :], buf.at[j], gbuf.at[j], act, slopes
+                )
+                for n, value in enumerate(products):
+                    if r == 0:
+                        here = far.at[0, j, n, pl.ds(0, span)]
+                        here[...] = value
+                        flush = load(here, (up_own, down_own)[n].at[j], osem.at[j, n])
+                        flush.start()
+                        flushes.append(flush)
+                    else:
+                        stage(r, j, n)[...] = value
+                        waiting.append(to_y(r, j, n))
+                if j % 2:
+                    step()
+        own.wait()
+        for x in bring:
+            x.wait()
+        for p in range(2):
+            mixed = gather_rows(ids, mine[p], [ret[s, :, p] for s in range(count)])
+            y_out[p] = (t2[p] + mixed).astype(BF16)
         for _ in range(2 * steps):
             step()
-        last = load(acc, sum_out, lsem.at[0])
-        last.start()
-        last.wait()
+        for run in others:
+            for _ in run:
+                pass
+        while waiting:
+            waiting.pop(0).start()
+        final = load(acc, sum_out, lsem.at[0])
+        final.start()
+        for r in range(1, ny):
+            for j in range(experts):
+                for n in range(2):
+                    to_y(r, j, n).wait()
+        for x in flushes + [final]:
+            x.wait()
         bg.finish()
 
     peers = expert_peers(ids)
+    peers = peers + [p for p in AllReduce.peers(plan) + [(r, 0) for r in range(1, ny)] if p not in peers]
+    big = [*tokens, *grads]
+    own_block = (experts, span, feature)
+    pair = (ny - 1, experts, 2, span, feature)
     return fused(
         plan,
         body,
-        [enc_up, source, gains, small, *saved, inward, outward, *sums],
-        [((rows, feature), F32), ((n_dw, feature, width), BF16), (small.shape, F32)],
-        "encoder_backward",
+        [enc_up, source, gains, small, *saved, *cols, own_col, crossed, inward, outward, up, down, result, *big, *sums],
+        [
+            ((rows, feature), F32),
+            ((n_dw, feature, width), BF16),
+            (small.shape, F32),
+            (own_block, BF16),
+            (own_block, BF16),
+            (pair, BF16),
+            ((2, rows, feature), BF16),
+        ],
+        "last",
         cid=9,
-        peers=peers + [p for p in AllReduce.peers(plan) if p not in peers],
+        peers=list(dict.fromkeys(peers)),
         jobs=jobs,
-        in_specs=[None] * 11 + [ANYWHERE] * (2 + len(sums)),
-        out_specs=[None, ANYWHERE, None],
+        in_specs=[None] * 15 + [ANYWHERE] * (9 + len(sums)),
+        out_specs=[None, ANYWHERE, None, ANYWHERE, ANYWHERE, ANYWHERE, None],
         scratch=attention_scratch(plan, rows, feature)
+        + [pltpu.VMEM(a.shape, BF16) for a in grads]
         + [
+            pltpu.VMEM((experts, block, feature), BF16),
+            pltpu.VMEM((experts, block, feature), BF16),
+            pltpu.VMEM((experts, length, feature), BF16),
+            pltpu.VMEM((experts, length, feature), BF16),
+            pltpu.VMEM((span, length), BF16),
+            pltpu.VMEM((span, length), BF16),
+            pltpu.VMEM(result.shape, BF16),
             pltpu.VMEM((n_dw, feature, width), BF16),
             pltpu.VMEM((n_dw, AllReduce.tmp_rows(plan, feature), width), BF16),
             pltpu.VMEM((steps,) + small.shape, F32),
-            DMA((1 + n_dw,)),
+            DMA((8 + n_dw,)),
             DMA((n_dw, 4, len(groups), steps)),
             DMA((2, steps)),
             pltpu.SemaphoreType.REGULAR((n_dw, len(groups), steps)),
+            DMA((2, ny - 1, experts, 2)),
+            DMA((count,)),
+            DMA((count,)),
             DMA((2, count)),
+            DMA((experts, 2)),
         ],
-        us=90,
-    )
-
-
-def column_groups(n_dw, width):
-    if n_dw % 3 == 0:
-        return [(n, 0, width) for n in range(n_dw)]
-    cut = (width // 3) // 128 * 128
-    groups = []
-    for n in range(n_dw):
-        groups += [(n, 0, cut), (n, cut, width - 2 * cut), (n, width - cut, cut)]
-    return groups
-
-
-def self_backward(plan, enc_up, dec_up, source, target, gains, enc_saved, dec_saved, inward, outward, jobs):
-    ids, count = plan.ids, plan.n_expert
-    _, rows, feature = source.shape
-    length = count * rows
-
-    def body(bg, *refs):
-        ups, srcs, g = refs[:2], refs[2:4], refs[4]
-        saved = (refs[5:12], refs[12:19])
-        win_any, wout_any = refs[19:21]
-        grads, dws, dgs = refs[21:23], refs[23:25], refs[25:27]
-        dk, dv, dq_t, do, *work, parts, got, win, wout, lsem = refs[27:-2]
-        sems = refs[-2:]
-        weights = [load(win_any.at[n], win.at[n], lsem.at[n]) for n in range(2)]
-        weights += [load(wout_any.at[n], wout.at[n], lsem.at[2 + n]) for n in range(2)]
-        for x in weights:
-            x.start()
-        scatter = [Scatter(ids, parts.at[n], got.at[n], sems[n].at[0], sems[n].at[1]) for n in range(2)]
-
-        def finish(n):
-            gain = 3 * n
-            grads[n][...] = scatter[n].finish()
-
-            def store(span, dx):
-                grads[n][span, :] = ups[n][span, :] + dx
-
-            dgs[n][...] = norm_back_rows(srcs[n].at[0], g[gain : gain + 1], grads[n], store)
-
-        bg.greet()
-        bg.start()
-        for x in weights:
-            x.wait()
-        for n in range(2):
-            hm, k, k_t, v, q, o_t, lse = saved[n]
-            d_branch = ups[n][...].astype(BF16)
-            do[...] = nt(d_branch, wout[n]).astype(BF16)
-            causal = (ids, rows) if n == 1 else None
-            between = () if n == 0 else ((0, lambda: bg.start(1)), (1, scatter[0].middle), (3, lambda: finish(0)))
-            attend_backward(q, k, v, k_t, do, o_t, lse, causal, dk, dv, dq_t, work, between)
-            dq = dq_t[...].astype(F32).T.astype(BF16)
-            for b in range(count):
-                span = slice(b * rows, (b + 1) * rows)
-                part = nt(dk[span, :], win[n, :, feature : 2 * feature])
-                part = part + nt(dv[span, :], win[n, :, 2 * feature :])
-                if b == 0:
-                    part = part + nt(dq, win[n, :, :feature])
-                parts[n, b] = part.astype(BF16)
-            scatter[n].start()
-            if n == 1:
-                scatter[1].middle()
-            for i, value in enumerate(
-                weight_grads(hm[0:rows, :], hm[...], dq, dk[...], dv[...], o_t[...], d_branch)
-            ):
-                dws[n][:, i * feature : (i + 1) * feature] = value.astype(BF16)
-        finish(1)
-        bg.finish()
-
-    block = (rows, feature)
-    return fused(
-        plan,
-        body,
-        [enc_up, dec_up, source, target, gains, *enc_saved, *dec_saved, inward, outward],
-        [(block, F32)] * 2 + [((feature, 4 * feature), BF16)] * 2 + [((1, feature), F32)] * 2,
-        "self_backward",
-        cid=7,
-        peers=expert_peers(ids),
-        jobs=jobs,
-        in_specs=[None] * 19 + [ANYWHERE] * 2,
-        scratch=[
-            *backward_scratch(plan, rows, feature),
-            pltpu.VMEM((2, count) + block, BF16),
-            pltpu.VMEM((2, count) + block, BF16),
-            pltpu.VMEM((2, feature, 3 * feature), BF16),
-            pltpu.VMEM((2, feature, feature), BF16),
-            DMA((4,)),
-        ]
-        + [DMA((2, count))] * 2,
-        us=40,
-    )
+        us=110,
+    )
+
+
+def column_groups(width):
+    small, large = width * 3 // 16 // 128 * 128, width // 2 // 128 * 128
+    return [(0, 0, large), (0, large, width - large - small), (0, width - small, small)]
 
 
 def weight_sources(plan, layer, tokens, grads, cols):
@@ -1489,7 +1509,7 @@
     return nn(slopes[...], buf[...]).astype(BF16), nn(act[...], gbuf[...]).astype(BF16)
 
 
-def expert_weights(plan, layer, cid, tokens, grads, cols, weight_up, weight_down, jobs, home=None):
+def expert_weights(plan, layer, cid, tokens, grads, cols, weight_up, weight_down, jobs):
     count, ny, nz, ids = plan.n_expert, plan.ny, plan.nz, plan.ids
     experts, hidden, feature = weight_up.shape
     rows = tokens[0].shape[-2]
@@ -1501,8 +1521,6 @@
 
     def body(bg, *refs):
         cn, cf = refs[:2]
-        if home is not None:
-            mine, res = refs[2:4]
         big, up_any, down_any = refs[n_small : n_small + 4], refs[n_small + 4], refs[n_small + 5]
         outs = refs[n_in:]
         up_out, down_out = outs[:2]
@@ -1514,15 +1532,6 @@
         for x in loads:
             x.start()
         bg.greet()
-        if home is not None:
-            ret, rs, rr = outs[n_out + 11 :]
-            own = load(refs[n_in - 1].at[0], ret.at[0], lsem.at[6])
-            own.start()
-            bring = [
-                send(refs[n_in - 1].at[s], ret.at[s], rs.at[s], rr.at[s], (0, ids[s])) for s in range(1, count)
-            ]
-            for x in bring:
-                x.start()
         bg.start()
         col_of, token_of, grad_of = weight_sources(plan, layer, held[0:2], held[2:4], (cn, cf))
         for n, (reader, dest) in enumerate(((token_of, buf), (grad_of, gbuf))):
@@ -1543,20 +1552,13 @@
                 return 0
 
             lax.fori_loop(0, experts, product, 0)
-        if home is not None:
-            own.wait()
-            for x in bring:
-                x.wait()
-            for p in range(2):
-                mixed = gather_rows(ids, mine[p], [ret[s, :, p] for s in range(count)])
-                outs[2][p] = (res[p] + mixed).astype(BF16)
         bg.finish()
 
-    small = [*cols] + ([] if home is None else [home[1], home[2]])
+    small = [*cols]
     n_small = len(small)
-    big = [tokens[0], tokens[1], grads[0], grads[1], weight_up, weight_down] + ([] if home is None else [home[0]])
+    big = [tokens[0], tokens[1], grads[0], grads[1], weight_up, weight_down]
     n_in = n_small + len(big)
-    outs = [((ny, experts, span, feature), BF16)] * 2 + ([] if home is None else [((2, rows, feature), BF16)])
+    outs = [((ny, experts, span, feature), BF16)] * 2
     n_out = len(outs)
     scratch = [pltpu.VMEM(a.shape, BF16) for a in big[:4]] + [
         pltpu.VMEM((experts, block, feature), BF16),
@@ -1565,10 +1567,8 @@
         pltpu.VMEM((experts, length, feature), BF16),
         pltpu.VMEM((span, length), BF16),
         pltpu.VMEM((span, length), BF16),
-        DMA((7,)),
+        DMA((6,)),
     ]
-    if home is not None:
-        scratch += [pltpu.VMEM(home[0].shape, BF16), DMA((count,)), DMA((count,))]
     return fused(
         plan,
         body,
@@ -1576,7 +1576,7 @@
         outs,
         ("encoder", "decoder")[layer] + "_weights",
         cid=cid,
-        peers=[] if home is None else expert_peers(ids),
+        peers=[],
         jobs=jobs,
         in_specs=[None] * n_small + [ANYWHERE] * len(big),
         scratch=scratch,
@@ -1584,19 +1584,21 @@
     )
 
 
-def finish(plan, sums, dec, dec_got, enc, enc_got):
+def finish(plan, sums, dec, dec_got, enc, enc_got, others_out):
     n_dw, feature, width = sums.shape
-    _, experts, span, _ = enc[0].shape
-    part = feature // experts
+    experts, span, _ = enc[0].shape
+    parts = 2
+    part, some = feature // (experts * parts), span // parts
     ny = plan.ny
 
-    def body(s, du, dd, dug, ddg, eu, ed, eug, edg, a_in, a_out, eu_out, ed_out, du_out, dd_out):
+    def body(s, du, dd, dug, ddg, eu, ed, eg, p0, p1, p2, a_in, a_out, eu_out, ed_out, du_out, dd_out, q0, q1, q2):
+        q0[...], q1[...], q2[...] = p0[...], p1[...], p2[...]
         for n in range(n_dw):
             a_in[n] = s[n_dw - 1 - n, :, : 3 * feature].astype(F32)
             a_out[n] = s[n_dw - 1 - n, :, 3 * feature :].astype(F32)
         for out, own, others in (
-            (eu_out, eu[0, 0], [eug[r, 0] for r in range(ny - 1)]),
-            (ed_out, ed[0, 0], [edg[r, 0] for r in range(ny - 1)]),
+            (eu_out, eu[0], [eg[r, 0, 0] for r in range(ny - 1)]),
+            (ed_out, ed[0], [eg[r, 0, 1] for r in range(ny - 1)]),
             (du_out, du[0, 0], [dug[r, 0] for r in range(ny - 1)]),
             (dd_out, dd[0, 0], [ddg[r, 0] for r in range(ny - 1)]),
         ):
@@ -1605,33 +1607,34 @@
                 total = total + other.astype(F32)
             out[0] = total
 
-    block = (1, span, feature)
-    first = pl.BlockSpec((1,) + block, lambda j: (0, j, 0, 0))
-    others = pl.BlockSpec((ny - 1,) + block, lambda j: (0, j, 0, 0))
-    own = pl.BlockSpec(block, lambda j: (j, 0, 0))
+    block = (1, some, feature)
+    first = pl.BlockSpec((1,) + block, lambda j, i: (0, j, i, 0))
+    others = pl.BlockSpec((ny - 1,) + block, lambda j, i: (0, j, i, 0))
+    own = pl.BlockSpec(block, lambda j, i: (j, i, 0))
+    rows = lambda w: pl.BlockSpec((n_dw, part, w), lambda j, i: (0, j * parts + i, 0))
+    tokens = others_out[0].shape[0] // (experts * parts)
+    flat = pl.BlockSpec((tokens, feature), lambda j, i: (j * parts + i, 0))
+    handed = [flat, flat, pl.BlockSpec((2, tokens, feature), lambda j, i: (0, j * parts + i, 0))]
     return fused(
         plan,
         body,
-        [sums, *dec, *dec_got, *enc, *enc_got],
-        [((n_dw, feature, 3 * feature), F32), ((n_dw, feature, feature), F32)] + [((experts, span, feature), F32)] * 4,
+        [sums, *dec, *dec_got, *enc, enc_got, *others_out],
+        [((n_dw, feature, 3 * feature), F32), ((n_dw, feature, feature), F32)] + [((experts, span, feature), F32)] * 4
+        + [(a.shape, a.dtype) for a in others_out],
         "finish",
-        grid=(experts,),
+        grid=(experts, parts),
         in_specs=[
-            pl.BlockSpec((n_dw, part, width), lambda j: (0, j, 0)),
+            rows(width),
             first,
             first,
             others,
             others,
-            first,
-            first,
-            others,
-            others,
+            own,
+            own,
+            pl.BlockSpec((ny - 1, 1, 2, some, feature), lambda j, i: (0, j, 0, i, 0)),
+            *handed,
         ],
-        out_specs=[
-            pl.BlockSpec((n_dw, part, 3 * feature), lambda j: (0, j, 0)),
-            pl.BlockSpec((n_dw, part, feature), lambda j: (0, j, 0)),
-        ]
-        + [own] * 4,
+        out_specs=[rows(3 * feature), rows(feature)] + [own] * 4 + handed,
         us=10,
     )[0]
 
@@ -1676,7 +1679,7 @@
     )
     e1, u, *enc_saved = enc
     t1, hc, *dec_saved = dec
-    (e2, memory), (col_far, og_far) = expert_forward(
+    (e2, memory), (col_far,) = expert_forward(
         plan,
         u_near,
         col_near,
@@ -1685,9 +1688,9 @@
         gains,
         encoder_up,
         encoder_down,
-        [Job(None, col_far, x=zr), Job(og, og_far, z=zc)],
-    )
-    (t2, w_near, result, fg, fg_low, fg_near, dt1, cross_dw, dg2, dg4, dg5), (w_far, col_far, og_far, u_far) = middle(
+        [Job(None, col_far, x=zr)],
+    )
+    (t2, w_near, result, fg, fg_low, fg_near, dt1, cross_dw, dg2, dg4, dg5), (w_far, col_far, u_far, og_far) = middle(
         plan,
         hc,
         t1,
@@ -1702,10 +1705,16 @@
         decoder_up,
         decoder_down,
         [
-            Job(og, None, later=[(1, "z", zc + za + zb), (1, "s", za + zb), (3, "x", zc)], by_pass=True, local=True),
+            Job(
+                og,
+                None,
+                later=[(2, "z", zb + zc + za), (2, "s", za), (4, "x", zb), (5, "x", zc)],
+                by_pass=True,
+                local=True,
+            ),
             Job(None, col_far, c=zr),
-            Job(None, og_far, s=za + zb, near=og_near, later=[(1, "c", za + zb), (2, "x", zc)]),
             Job(u, None, z=zr),
+            Job(og, og_far, z=zc, s=za, near=og_near, later=[(1, "x", zb), (2, "c", za), (3, "x", zc)]),
         ],
     )
     (de1, dg1), (w_far, og_far, fg_far) = encoder_experts(
@@ -1719,7 +1728,7 @@
         gains,
         encoder_up,
         encoder_down,
-        [Job(None, w_far, c=zr), Job(None, og_far, c=zc), Job(fg_low, None, z=za + zb)],
+        [Job(None, w_far, c=zr), Job(None, og_far, c=zb + zc), Job(fg_low, None, z=za + zb)],
     )
     dec_g, (fg_far,) = expert_weights(
         plan,
@@ -1745,21 +1754,9 @@
             Swap(dec_g[0]),
         ],
     )
-    (*enc_g, decoder_output), (down_got,) = expert_weights(
-        plan,
-        0,
-        10,
-        (u_near, u_far),
-        (fg_near, fg_far),
-        (col_near, col_far),
-        encoder_up,
-        encoder_down,
-        [Swap(dec_g[1])],
-        (result, own_cols[1], t2),
-    )
     count_row = jnp.pad(counts.reshape(1, -1), ((0, 1), (0, feature - counts.size)))
     small = jnp.concatenate([jnp.zeros_like(dg1), dg1, dg2, dg3, dg4, dg5, count_row], axis=0)
-    (source_grad, sums, small), enc_got = encoder_backward(
+    (source_grad, sums, small, up_own, down_own, enc_got, decoder_output), (down_got,) = last(
         plan,
         de1,
         source,
@@ -1768,10 +1765,22 @@
         *weights,
         [cross_dw, dec_dw],
         small,
-        [Swap(enc_g[0], paced=True), Swap(enc_g[1], paced=True)],
-    )
-    a_in, a_out, enc_up_g, enc_down_g, dec_up_g, dec_down_g = finish(
-        plan, sums, dec_g, (up_got, down_got), enc_g, enc_got
+        (u_near, u_far),
+        (fg_near, fg_far),
+        (col_near, col_far),
+        encoder_up,
+        encoder_down,
+        (result, own_cols[1], t2),
+        [Swap(dec_g[1], paced=True)],
+    )
+    a_in, a_out, enc_up_g, enc_down_g, dec_up_g, dec_down_g, source_grad, target_grad, decoder_output = finish(
+        plan,
+        sums,
+        dec_g,
+        (up_got, down_got),
+        (up_own, down_own),
+        enc_got,
+        (source_grad, target_grad, decoder_output),
     )
     return (
         decoder_output.reshape(2, 1, rows, feature),

time: 461 us -> 457 us (level); the launches traced: 453 us -> 457 us
  Pallas kernels: 442 us -> 448 us
    pallas_call x9 -> x8, Pallas kernels: 442 us -> 448 us  [fused(): pl.pallas_call(run, out_shape=[jax.ShapeDtypeStruct(s, d) for s, d in out...]
where the time goes in v6:
time: 457 us
  Pallas kernels  448 us (98%)
  local copies, waits for them, and re-layouts  5 us (1%)
    pallas_call x8, Pallas kernels, fused(): pl.pallas_call(run, out_shape=[jax.ShapeDtypeStruct(s, d) for s, d in out...  448 us

profile of v6, /device:TPU:0, one launch (start us, length us, event | category | flops | bytes accessed | tf_op | source)
XLA Modules:
  0.0 457.1 jit_solution(1895442906304154967)
XLA Ops:
  0.6 0.8 fusion
  1.4 0.6 reshape.43.refs_2_.refs_7_
  2.0 2.1 bitcast_convert_fusion.refs_3_.refs_8_.refs_15_
  4.1 45.2 %self_forward.1 = (f32[256,512]{1,0:T(8,128)}, bf16[256,512]{1,0:T(8,128)(2,1)}, bf16[1024,512]{1,0:T(8,128)(2,1)}, bf16[1024,512]{1,0:T(8,128)(2,1)}, bf16[512,...) custom-call(bf16[1,256,512]{2,1,0:T(8,128)(2,1)} %refs_1_.5, ...), custom_call_target="tpu_custom_call" | custom-call | flops 40249999360 | bytes 7356416 | tf_op jit(solution)/shard_map/self_forward/pallas_call | solution.py:519
  49.3 0.8 squeeze.10.refs_2_.refs_3_
  50.1 20.8 %expert_forward.1 = (f32[2,256,512]{2,1,0:T(8,128)}, bf16[2,256,512]{2,1,0:T(8,128)(2,1)}, s32[3,4,4,256]{3,2,1,0:T(4,128)}) custom-call(bf16[4,256,512]{2,1,0:T(8,128)(2,1)} %get-tuple-element.83.refs_0_.refs_13_.refs_20_, s32[4,4,256]{2,1,0:T(4,128)} %get-tuple-element.86.refs_1_.refs_5_.refs_2_.refs_0_.refs_11_, ...), custom_call_target="tpu_custom_call", output_to_operand_aliasing={{2}: (7, {})} | custom-call | flops 25300000768 | bytes 18380800 | tf_op jit(solution)/shard_map/expert_forward/pallas_call | solution.py:519
  71.0 0.8 squeeze.11.refs_6_.refs_13_
  71.8 147.7 %middle.1 = (f32[2,256,512]{2,1,0:T(8,128)}, bf16[2,4,256,512]{3,2,1,0:T(8,128)(2,1)}, bf16[4,4,2,32,512]{4,3,2,1,0:T(8,128)(2,1)}, f32[2,256,512]{2,1,0:T(8,128...) custom-call(bf16[256,512]{1,0:T(8,128)(2,1)} %get-tuple-element.84.r, ...), custom_call_target="tpu_custom_call", output_to_operand_aliasing={{12}: (13, {}), {14}: (17, {})} | custom-call | flops 149500002304 | bytes 28604416 | tf_op jit(solution)/shard_map/middle/pallas_call | solution.py:519
  219.6 31.7 %encoder_experts.1 = (f32[256,512]{1,0:T(8,128)}, f32[1,512]{1,0:T(1,128)}, bf16[3,4,2,256,512]{4,3,2,1,0:T(8,128)(2,1)}, bf16[3,4,2,256,512]{4,3,2,1,0:T(8,128)(2,1)}, bf16[3,4,2,256,512]{4,3,2,1,0:T(8,128)(2,1)}) custom-call(bf16[4,256,512]{2,1,0:T(8,128)(2,1)} %get-tuple-element.83.refs_0_.refs_13_.refs_20_, ...), custom_call_target="tpu_custom_call", output_to_operand_aliasing={{2}: (9, {}), {3}: (10, {})} | custom-call | flops 34500001792 | bytes 21526528 | tf_op jit(solution)/shard_map/encoder_experts/pallas_call | solution.py:519
  251.3 27.8 %decoder_weights.1 = (bf16[2,4,256,512]{3,2,1,0:T(8,128)(2,1)}, bf16[2,4,256,512]{3,2,1,0:T(8,128)(2,1)}, bf16[3,4,2,256,512]{4,3,2,1,0:T(8,128)(2,1)}) custom-call(s32[4,4,256]{2,1,0:T(4,128)} %get-tuple-element.86.refs_1_.refs_5_.refs_2_.refs_0_.refs_11_, s32[3,4,4,256]{3,2,1,0:T(4,128)} %get-tuple-element.111.refs_1_.refs_12_, ...), custom_call_target="tpu_custom_call", output_to_operand_aliasing={{2}: (9, {})} | custom-call | flops 28750000128 | bytes 33619968 | tf_op jit(solution)/shard_map/decoder_weights/pallas_call | solution.py:519
  279.0 0.0 copy-start.1
  279.0 0.0 copy-start.2
  279.1 0.0 copy-start.3
  279.1 0.0 copy-start.4
  279.1 0.0 copy-start.5
  279.1 0.0 copy-start.6
  279.1 31.8 %decoder_backward.1 = (f32[256,512]{1,0:T(8,128)}, bf16[512,2048]{1,0:T(8,128)(2,1)}, f32[1,512]{1,0:T(1,128)}, bf16[3,4,2,256,512]{4,3,2,1,0:T(8,128)(2,1)}, bf...) custom-call(f32[256,512]{1,0:T(8,128)} %get-tuple-element.103.refs_0, ...), custom_call_target="tpu_custom_call", output_to_operand_aliasing={{3}: (12, {}), {4}: (14, {})} | custom-call | flops 32199999488 | bytes 12079104 | tf_op jit(solution)/shard_map/decoder_backward/pallas_call | solution.py:519
  310.9 0.0 copy-done.1
  311.0 0.0 copy-done.2
  311.0 0.1 convert_reduce_fusion
  311.1 0.1 reshape.45
  311.2 0.0 copy-done.3
  311.2 0.0 copy-done.4
  311.2 0.0 copy-done.5
  311.2 0.0 copy-done.6
  311.2 1.3 concatenate.3.refs_3_
  312.6 128.8 %last.1 = (f32[256,512]{1,0:T(8,128)}, bf16[3,512,2048]{2,1,0:T(8,128)(2,1)}, f32[8,512]{1,0:T(8,128)}, bf16[4,256,512]{2,1,0:T(8,128)(2,1)}, bf16[4,256,512]{2,...) custom-call(f32[256,512]{1,0:T(8,128)} %get-tuple-element.100.refs_0, ...), custom_call_target="tpu_custom_call" | custom-call | flops 126500003840 | bytes 47814656 | tf_op jit(solution)/shard_map/last/pallas_call | solution.py:519
  441.3 0.0 copy-start
  441.4 14.3 %finish.1 = (f32[3,512,1536]{2,1,0:T(8,128)}, f32[3,512,512]{2,1,0:T(8,128)}, f32[4,256,512]{2,1,0:T(8,128)}, f32[4,256,512]{2,1,0:T(8,128)}, f32[4,256,512]{2,1...) custom-call(bf16[3,512,2048]{2,1,0:T(8,128)(2,1)} %get-tuple-element, ...), custom_call_target="tpu_custom_call" | custom-call | flops 11500000256 | bytes 18350080 | tf_op jit(solution)/shard_map/finish/pallas_call | solution.py:519
  455.6 0.0 copy-done
  455.7 0.7 convert_element_type.17
  456.3 0.6 copy.68
  (6 shorter events, 0.1 us)
Async XLA Ops:
  279.0 31.9 %copy-start.1 = (s32[2,1,256]{2,1,0:T(1,128)S(1)}, s32[2,1,256]{2,1,0:T(1,128)}, u32[]{:S(2)}) copy-start(s32[2,1,256]{2,1,0:T(1,128)} %param.23) | copy-start | bytes 6148
  279.0 31.9 %copy-start.2 = (s32[2,1,256]{2,1,0:T(1,128)S(1)}, s32[2,1,256]{2,1,0:T(1,128)}, u32[]{:S(2)}) copy-start(s32[2,1,256]{2,1,0:T(1,128)} %param.25) | copy-start | bytes 6148
  279.1 32.1 %copy-start.3 = (f32[1,512]{1,0:T(1,128)S(1)}, f32[1,512]{1,0:T(1,128)}, u32[]{:S(2)}) copy-start(f32[1,512]{1,0:T(1,128)} %get-tuple-element.102) | copy-start | bytes 6148
  279.1 32.1 %copy-start.4 = (f32[1,512]{1,0:T(1,128)S(1)}, f32[1,512]{1,0:T(1,128)}, u32[]{:S(2)}) copy-start(f32[1,512]{1,0:T(1,128)} %get-tuple-element.120) | copy-start | bytes 6148
  279.1 32.1 %copy-start.5 = (f32[1,512]{1,0:T(1,128)S(1)}, f32[1,512]{1,0:T(1,128)}, u32[]{:S(2)}) copy-start(f32[1,512]{1,0:T(1,128)} %get-tuple-element.121) | copy-start | bytes 6148
  279.1 32.1 %copy-start.6 = (f32[1,512]{1,0:T(1,128)S(1)}, f32[1,512]{1,0:T(1,128)}, u32[]{:S(2)}) copy-start(f32[1,512]{1,0:T(1,128)} %get-tuple-element.101) | copy-start | bytes 6148
  441.3 14.3 %copy-start = (f32[8,512]{1,0:T(8,128)S(1)}, f32[8,512]{1,0:T(8,128)}, u32[]{:S(2)}) copy-start(f32[8,512]{1,0:T(8,128)} %get-tuple-element.150) | copy-start | bytes 49156
